TPU v7x, 256 devices: a whole 4x4x8 slice. The times are simulated.
256 devices in a mesh: gx: 8 (over y, x_hi), yz: 32 (over x_lo, z, core).
Axes of the slice: x: 4 (x_hi: 2, x_lo: 2; x = x_hi * 2 + x_lo), y: 4, z: 8, core: 2. Of those that a mesh axis runs over, the one named last changes fastest.
Arguments:
- features: bfloat16 [16, 32, 128, 1152], P('gx', 'yz'), may hold values from -6 to 6
- positions: float32 [16, 32, 3, 128], P('gx', 'yz'), may hold values from 0 to 1
- edge_dst: int32 [3, 16, 32, 128], P(None, 'gx', 'yz'), may hold values from 0 to 1535, as said below
- edge_shift: int32 [3, 16, 32, 128], P(None, 'gx', 'yz'), may hold values from -1 to 1
- radial_weights: float32 [8, 896], replicated, may hold values from -2 to 2
- readout_weights: float32 [8, 256], replicated, may hold values from -0.1875 to 0.1875
- w_scalar: bfloat16 [128, 128], replicated, may hold values from -0.5 to 0.5
- w_gate: bfloat16 [128, 128], replicated, may hold values from -0.5 to 0.5
- w_vector: bfloat16 [128, 128], replicated, may hold values from -0.5 to 0.5
- w_tensor: bfloat16 [128, 128], replicated, may hold values from -0.5 to 0.5
Outputs:
- mixed_features: bfloat16 [16, 32, 128, 1152], P('gx', 'yz')
- forces: float32 [16, 32, 3, 128], P('gx', 'yz')
Inputs may be any that keep to these rules, and one draw needn't show every extreme that they name: `edge_dst`: each index names a slot of a pillar in the local layout of (4) x (3) pillars of 128 slots (ghost pillars around the device's own, pillar after pillar, then slot); its pillar is the edge's own pillar or one of the eight around it.
All inputs are finite; a program needn't handle non-finite values.
Results may differ from a plain program's by a relative error of at most 0.005.
Values may be sent and summed in bfloat16 or wider, within the bound.
A program may use at most 64 MiB of HBM per device.

v0:
```python
import math

import jax
import jax.numpy as jnp
from jax import lax
from jax.experimental import pallas as pl
from jax.experimental.pallas import tpu as pltpu
from jax.sharding import PartitionSpec as P

MESH = pl.DeviceIdType.MESH
F32 = jnp.float32
BF16 = jnp.bfloat16
SOFTENING = 0.25
SPACING = 0.6
ROOT_THREE = math.sqrt(3.0)
C = 128
S = 128
NB = 8
NE = 3
NP = 2
BLOCKS = 9
READ_BLOCKS = 4
KP = NE * NP
ROWS = NE * S
NEAR = 9 * S
STEP = 16
GROUPS = ((0, 4), (4, 7), (7, 9))
GROUPS2 = ((0, 2), (2, 4))
DIRECTIONS = tuple((dx, dy) for dx in (-1, 0, 1) for dy in (-1, 0, 1) if (dx, dy) != (0, 0))


def split(x):
    high = x.astype(BF16).astype(F32)
    return high, x - high


def dot(a, b, contract=(1, 0)):
    dims = (((contract[0],), (contract[1],)), ((), ()))
    return lax.dot_general(a, b, dims, preferred_element_type=F32)


PLACE = {0: 0, -1: 1, 1: 2}


def near_slot(p, j):
    return (j // 2, j % 2) if j < 6 else (j - 6, 3 - p)


def near_pillar(p, j):
    y, slot = near_slot(p, j)
    return (1, 2, 3, 0)[slot], (1, 0, 2)[y]


def block(bufs, c, *at):
    for buf in bufs:
        if c < buf.shape[2]:
            return buf.at[(*at, c)]
        c -= buf.shape[2]


class Halo:
    COUNT = 10

    def __init__(self, bufs, send, recv, device, low_wrap, high_wrap):
        self.copies = {}
        self.low_wrap, self.high_wrap = low_wrap, high_wrap
        own, ghosts = pl.ds(0, 2), pl.ds(2, 2)
        for g, buf in enumerate(bufs):
            spans = {
                "x0": (buf.at[0, 0], buf.at[0, 2], (-1, 0)),
                "x1": (buf.at[0, 1], buf.at[0, 3], (1, 0)),
            }
            for sign, step, to in (("m", -1, 2), ("p", 1, 1)):
                spans |= {
                    "y" + sign: (buf.at[0, own], buf.at[to, own], (0, step)),
                    "c" + sign: (buf.at[0, ghosts], buf.at[to, ghosts], (0, step)),
                    "w0" + sign: (buf.at[0, 0], buf.at[to, 2], (-1, step)),
                    "w1" + sign: (buf.at[0, 1], buf.at[to, 3], (1, step)),
                }
            for n, (name, (src, dst, step)) in enumerate(spans.items()):
                self.copies[name, g] = pltpu.make_async_remote_copy(
                    src_ref=src,
                    dst_ref=dst,
                    send_sem=send.at[g, n],
                    recv_sem=recv.at[g, n],
                    device_id=device(*step),
                    device_id_type=MESH,
                )

    def start(self, g, *names):
        for name in names:
            self.copies[name, g].start()

    def arrived(self, g, *names):
        for name in names:
            self.copies[name, g].wait_recv()

    def sends(self, sign, plain, wrap):
        wraps = self.low_wrap if sign == "m" else self.high_wrap
        if wrap is not None:
            pl.when(wraps)(wrap)
        if plain is not None:
            pl.when(jnp.logical_not(wraps))(plain)

    def own(self, g):
        self.start(g, "x0", "x1", "ym", "yp")
        for sign in "mp":
            self.sends(sign, None, lambda: self.start(g, "w0" + sign, "w1" + sign))

    def near(self, g):
        self.arrived(g, "ym", "yp")

    def corners(self, g):
        self.arrived(g, "x0", "x1")
        for sign in "mp":
            self.sends(sign, lambda: self.start(g, "c" + sign), None)

    def rest(self, g):
        for sign, wraps in (("m", self.high_wrap), ("p", self.low_wrap)):
            pl.when(wraps)(lambda: self.arrived(g, "w0" + sign, "w1" + sign))
            pl.when(jnp.logical_not(wraps))(lambda: self.arrived(g, "c" + sign))

    def sent(self, groups):
        def done(*names):
            for g in groups:
                for name in names:
                    self.copies[name, g].wait_send()

        done("x0", "x1", "ym", "yp")
        for sign in "mp":
            self.sends(sign, lambda: done("c" + sign), lambda: done("w0" + sign, "w1" + sign))


def kernel(
    gx_size,
    yz_size,
    feat,
    *refs,
):
    small_in, refs = refs[:9], refs[9:]
    mixed, forces, *refs = refs
    small, refs = refs[:9], refs[9:]
    run(gx_size, yz_size, feat, small_in, small, mixed, forces, *refs)


def run(
    gx_size,
    yz_size,
    feat,
    small_in,
    small,
    mixed,
    forces,
    ext0,
    ext1,
    ext2,
    mix0,
    mix1,
    posx,
    oh,
    coef,
    qcoef,
    wide,
    zf,
    pj,
    geo,
    edges,
    acc,
    gsc,
    mix_out,
    xq,
    grad,
    extf,
    frecv,
    small_sem,
    load_sem,
    out_sem,
    pos_send,
    pos_recv,
    f1_send,
    f1_recv,
    f2_send,
    f2_recv,
    fo_send,
    fo_recv,
):
    ext, ext2 = (ext0, ext1, ext2), (mix0, mix1)
    gx = lax.axis_index("gx")
    yz = lax.axis_index("yz")

    half = yz_size // 2
    low_wrap = lax.rem(yz, half) == 0
    high_wrap = lax.rem(yz, half) == half - 1

    def device(dx, dy):
        return (lax.rem(gx + dx + gx_size, gx_size), lax.rem(yz + dy + yz_size, yz_size))

    small_loads = [
        pltpu.make_async_copy(small_in[i], small[i], small_sem.at[i]) for i in range(len(small))
    ]
    for load in small_loads:
        load.start()
    pos, dst, shift, wr, wq, w_scalar, w_gate, w_vector, w_tensor = small
    loads = []
    for c in range(BLOCKS):
        load = pltpu.make_async_copy(
            feat.at[:, 0, :, pl.ds(c * C, C)], block(ext, c, 0, pl.ds(0, 2)), load_sem.at[c]
        )
        load.start()
        loads.append(load)

    barrier = pltpu.get_barrier_semaphore()
    for step in DIRECTIONS:
        pl.semaphore_signal(barrier, inc=1, device_id=device(*step), device_id_type=MESH)

    for load in small_loads:
        load.wait()
    for p in range(NP):
        posx[0, p] = jnp.zeros((8, S), F32)
        for m in range(3):
            posx[0, p, pl.ds(m, 1), :] = pos[p, m]
    pl.semaphore_wait(barrier, len(DIRECTIONS))

    pos_copies = []
    for n, (dx, dy) in enumerate(DIRECTIONS):
        if dx == 0:
            here, there = pl.ds(0, 2), pl.ds(0, 2)
        elif dx == 1:
            here, there = pl.ds(1, 1), pl.ds(3, 1)
        else:
            here, there = pl.ds(0, 1), pl.ds(2, 1)
        copy = pltpu.make_async_remote_copy(
            src_ref=posx.at[0, here],
            dst_ref=posx.at[PLACE[-dy], there],
            send_sem=pos_send.at[n],
            recv_sem=pos_recv.at[n],
            device_id=device(dx, dy),
            device_id_type=MESH,
        )
        copy.start()
        pos_copies.append(copy)

    halo = Halo(ext, f1_send, f1_recv, device, low_wrap, high_wrap)
    for g, (lo, hi) in enumerate(GROUPS):
        for c in range(lo, hi):
            loads[c].wait()
        halo.own(g)

    lane = lax.broadcasted_iota(jnp.int32, (S, S), 1).astype(F32)
    edges[...] = jnp.zeros_like(edges)
    for k in range(NE):
        for p in range(NP):
            row = dst[k, p].astype(F32)
            edges[0, pl.ds(k * NP + p, 1), :] = row
            edges[1, pl.ds(k * NP + p, 1), :] = shift[k, p].astype(F32)
            column = jnp.transpose(jnp.broadcast_to(row, (S, S))) - lane
            for j in range(9):
                x, y = near_pillar(p, j)
                hit = column == float((3 * x + y) * S)
                oh[p, pl.ds(k * S, S), pl.ds(j * S, S)] = jnp.where(hit, 1.0, 0.0).astype(BF16)

    wide[...] = jnp.zeros_like(wide)
    w_r, rest_r = split(wr[...])
    w_q, rest_q = split(wq[...])
    zeros_r = jnp.zeros_like(w_r)
    zeros_q = jnp.zeros_like(w_q)
    n_r, n_q = 7 * C, 2 * C
    wide[pl.ds(0, 32), pl.ds(0, n_r)] = jnp.concatenate([w_r, rest_r, w_r, zeros_r], 0).astype(BF16)
    wide[pl.ds(0, 32), pl.ds(n_r, n_q)] = jnp.concatenate([w_q, rest_q, w_q, zeros_q], 0).astype(BF16)
    wide[pl.ds(32, 32), pl.ds(n_r + n_q, n_q)] = jnp.concatenate([w_q, rest_q, w_q, zeros_q], 0).astype(BF16)
    copy_row = lax.broadcasted_iota(jnp.int32, (8, 8 * C), 0)
    copy_col = lax.broadcasted_iota(jnp.int32, (8, 8 * C), 1)
    copies = jnp.where((copy_col >= copy_row * C) & (copy_col < (copy_row + 1) * C), 1.0, 0.0)
    wide[pl.ds(64, 16), pl.ds(n_r + 2 * n_q, 8 * C)] = jnp.concatenate([copies, copies], 0).astype(BF16)

    for copy in pos_copies:
        copy.wait_recv()
    for p in range(NP):
        places = jnp.concatenate([posx[near_slot(p, j)] for j in range(9)], axis=1)
        first, rest = split(places)
        second, third = split(rest)
        parts = jnp.concatenate([first, second, third, jnp.zeros_like(first)], 0).astype(BF16)
        found = dot(parts, oh[p], (1, 1))
        far = (found[0:8] + found[8:16]) + found[16:24]
        for k in range(NE):
            pj[k * NP + p] = far[:, k * S : (k + 1) * S] - posx[0, p]

    place = edges[0]
    own_p = lax.rem(lax.broadcasted_iota(jnp.int32, (8, S), 0), NP).astype(F32)
    one = jnp.ones_like(place)
    nil = jnp.zeros_like(place)

    def at_least(x, bound):
        return jnp.where(x >= float(bound), one, nil)

    ext_x = at_least(place, 3 * S) + at_least(place, 6 * S) + at_least(place, 9 * S)
    left = place - ext_x * float(3 * S)
    ext_y = at_least(left, S) + at_least(left, 2 * S)
    disp_x = pj[:, 0, :] + (ext_x - 1.0 - own_p)
    disp_y = pj[:, 1, :] + (ext_y - 1.0)
    disp_z = pj[:, 2, :] + edges[1]
    rho = jnp.sqrt(disp_x * disp_x + disp_y * disp_y + disp_z * disp_z + SOFTENING)
    inverse = 1.0 / rho
    u_x, u_y, u_z = disp_x * inverse, disp_y * inverse, disp_z * inverse
    geo[0] = u_x
    geo[1] = u_y
    geo[2] = u_z
    geo[3] = inverse
    length_sq = u_x * u_x + u_y * u_y + u_z * u_z
    angular = (
        u_x,
        u_y,
        u_z,
        ROOT_THREE * u_x * u_y,
        ROOT_THREE * u_y * u_z,
        0.5 * (3.0 * u_z * u_z - length_sq),
        ROOT_THREE * u_x * u_z,
        0.5 * ROOT_THREE * (u_x * u_x - u_y * u_y),
    )
    zf[...] = jnp.zeros_like(zf)
    for b in range(NB):
        off = (rho - (0.5 + SPACING * b)) / SPACING
        basis = jnp.exp(-(off * off))
        slope = basis * off * (-2.0 / SPACING)
        high, low = split(basis)
        zf[b] = high
        zf[8 + b] = high
        zf[16 + b] = low
        high, low = split(slope)
        zf[32 + b] = high
        zf[40 + b] = high
        zf[48 + b] = low
        high, low = split(angular[b])
        zf[64 + b] = high
        zf[72 + b] = low

    halo.corners(0)
    for p in range(NP):
        for k in range(NE):
            rows = jnp.transpose(zf[:, k * NP + p, :]).astype(BF16)
            at = pl.ds(p * ROWS + k * S, S)
            for f in range(0, 19, 2):
                n = min(2, 19 - f)
                out = dot(rows, wide[:, pl.ds(f * C, n * C)])
                for i in range(n):
                    if f + i < 7:
                        coef[f + i, at, :] = out[:, i * C : (i + 1) * C]
                    elif f + i < 11:
                        qcoef[f + i - 7, at, :] = out[:, i * C : (i + 1) * C]
                    else:
                        coef[f + i - 4, at, :] = out[:, i * C : (i + 1) * C]

    def gather(bufs, lo, hi, beyond):
        for p in range(NP):
            for c in range(lo, hi, 2):
                n = min(2, hi - c)
                parts = [c + i for i in range(n)]
                if beyond:
                    rows = [block(bufs, i, pl.ds(0, 3), 3 - p)[...].reshape(3 * S, C) for i in parts]
                    out = dot(oh[p, :, pl.ds(6 * S, 3 * S)], jnp.concatenate(rows, axis=1))
                else:
                    rows = [block(bufs, i, pl.ds(0, 3), pl.ds(0, 2))[...].reshape(6 * S, C) for i in parts]
                    out = dot(oh[p, :, pl.ds(0, 6 * S)], jnp.concatenate(rows, axis=1))
                at = pl.ds(p * ROWS, ROWS)
                for i in range(n):
                    term = out[:, i * C : (i + 1) * C]
                    gsc[c + i, at, :] = gsc[c + i, at, :] + term if beyond else term

    def each_row(fn):
        for p in range(NP):

            def run(i, carry, p=p):
                r = pl.multiple_of(i * STEP, STEP)
                fn(p, r, [pl.ds(p * ROWS + k * S + r, STEP) for k in range(NE)], pl.ds(p * S + r, STEP))
                return carry

            lax.fori_loop(0, S // STEP, run, 0)

    def message_sv(p, r, at, to):
        total = [jnp.zeros((STEP, C), F32) for _ in range(BLOCKS)]
        for k in range(NE):
            e = at[k]
            s = gsc[0, e, :]
            v = [gsc[1 + m, e, :] for m in range(3)]
            u = [coef[7 + m, e, :] for m in range(3)]
            along = u[0] * v[0] + u[1] * v[1] + u[2] * v[2]
            total[0] = total[0] + coef[0, e, :] * s + coef[1, e, :] * along
            r3s = coef[3, e, :] * s
            r4 = coef[4, e, :]
            for m in range(3):
                total[1 + m] = total[1 + m] + r3s * u[m] + r4 * v[m]
            r5s = coef[5, e, :] * s
            for n in range(5):
                total[4 + n] = total[4 + n] + r5s * coef[10 + n, e, :]
        for b in range(BLOCKS):
            acc[b, to, :] = total[b]

    def message_t(lo, hi):
        def fn(p, r, at, to):
            total = [acc[b, to, :] for b in (0, *range(lo, hi))]
            for k in range(NE):
                e = at[k]
                along = None
                r6 = coef[6, e, :]
                for n in range(lo, hi):
                    t = gsc[n, e, :]
                    term = coef[6 + n, e, :] * t
                    along = term if along is None else along + term
                    total[1 + n - lo] = total[1 + n - lo] + r6 * t
                total[0] = total[0] + coef[2, e, :] * along
            for i, b in enumerate((0, *range(lo, hi))):
                acc[b, to, :] = total[i]

        return fn

    third = 1.0 / NE

    def mix(lo, hi, weight):
        for b in range(lo, hi):
            acc[b] = dot((acc[b] * third).astype(BF16), weight[...])

    halo.near(0)
    gather(ext, 0, 4, False)
    halo.near(1)
    gather(ext, 4, 7, False)
    halo.corners(1)
    halo.near(2)
    gather(ext, 7, 9, False)
    halo.rest(0)
    gather(ext, 0, 4, True)
    each_row(message_sv)
    mix(1, 4, w_vector)
    halo.corners(2)
    halo.rest(1)
    gather(ext, 4, 7, True)
    each_row(message_t(4, 7))
    mix(4, 7, w_tensor)
    halo.rest(2)
    gather(ext, 7, 9, True)
    each_row(message_t(7, 9))
    mix(7, 9, w_tensor)

    scalar = (acc[0] * third).astype(BF16)
    pre = dot(scalar, w_scalar[...])
    acc[0] = pre * jax.nn.sigmoid(pre)
    gsc[0, pl.ds(0, NP * S), :] = jax.nn.sigmoid(dot(scalar, w_gate[...]))

    def update_sv(p, r, at, to):
        gate = gsc[0, to, :]
        rows = pl.ds(r, STEP)
        for b in range(READ_BLOCKS):
            old = block(ext, b, 0, p)[rows, :].astype(F32)
            step = gate * acc[b, to, :] if b > 0 else acc[0, to, :]
            new = (old + step).astype(BF16)
            block(ext2, b, 0, p)[rows, :] = new
            mix_out[p, 0, rows, pl.ds(b * C, C)] = new

    each_row(update_sv)
    halo2 = Halo(ext2, f2_send, f2_recv, device, low_wrap, high_wrap)
    for g in range(len(GROUPS2)):
        halo2.own(g)

    def update_t(p, r, at, to):
        gate = gsc[0, to, :]
        rows = pl.ds(r, STEP)
        for b in range(READ_BLOCKS, BLOCKS):
            old = block(ext, b, 0, p)[rows, :].astype(F32)
            mix_out[p, 0, rows, pl.ds(b * C, C)] = (old + gate * acc[b, to, :]).astype(BF16)

    each_row(update_t)
    write = pltpu.make_async_copy(mix_out, mixed, out_sem)
    write.start()

    halo2.near(0)
    gather(ext2, 0, 2, False)
    halo2.corners(0)
    halo2.near(1)
    gather(ext2, 2, 4, False)
    halo2.corners(1)
    halo.sent(range(len(GROUPS)))
    halo2.rest(0)
    gather(ext2, 0, 2, True)
    halo2.rest(1)
    gather(ext2, 2, 4, True)

    def pair(p, r, at, to):
        rows = pl.ds(r, STEP)
        own = [block(ext2, b, 0, p)[rows, :].astype(F32) for b in range(READ_BLOCKS)]
        for k in range(NE):
            e = at[k]
            far = [gsc[b, e, :] for b in range(READ_BLOCKS)]
            u = [coef[7 + m, e, :] for m in range(3)]
            own_along = u[0] * own[1] + u[1] * own[2] + u[2] * own[3]
            far_along = u[0] * far[1] + u[1] * far[2] + u[2] * far[3]
            q1 = qcoef[1, e, :]
            own_q, far_q = q1 * own_along, q1 * far_along
            terms = [qcoef[2, e, :] * (own[0] * far[0]) + qcoef[3, e, :] * (own_along * far_along)]
            for m in range(3):
                terms.append(own[1 + m] * far_q + own_q * far[1 + m])
            at_col = (k * NP + p) * 2 * C
            for q in range(4):
                high, low = split(terms[q])
                xq[pl.ds(q * S + r, STEP), pl.ds(at_col, C)] = high.astype(BF16)
                xq[pl.ds(q * S + r, STEP), pl.ds(at_col + C, C)] = low.astype(BF16)

    each_row(pair)
    mask_row = lax.broadcasted_iota(jnp.int32, (16, KP * 2 * C), 0) * (2 * C)
    mask_col = lax.broadcasted_iota(jnp.int32, (16, KP * 2 * C), 1)
    mask = jnp.where((mask_col >= mask_row) & (mask_col < mask_row + 2 * C), 1.0, 0.0).astype(BF16)
    sums = dot(mask, xq[...], (1, 1))[0:8]
    t_rho, g_x, g_y, g_z = (sums[:, q * S : (q + 1) * S] for q in range(4))
    u_x, u_y, u_z = geo[0], geo[1], geo[2]
    inverse = geo[3]
    radial_part = t_rho - (u_x * g_x + u_y * g_y + u_z * g_z) * inverse
    grad[...] = jnp.zeros_like(grad)
    grad[0] = radial_part * u_x + g_x * inverse
    grad[1] = radial_part * u_y + g_y * inverse
    grad[2] = radial_part * u_z + g_z * inverse

    parts = []
    for p in range(NP):
        terms = jnp.concatenate([grad[:, k * NP + p, :] for k in range(NE)], axis=1)
        first, rest = split(terms)
        second, third_part = split(rest)
        parts.append(
            jnp.concatenate([first, second, third_part, jnp.zeros_like(first)], 0).astype(BF16)
        )

    def scatter(lo, hi):
        seen = {}
        for p in range(NP):
            out = dot(parts[p], oh[p, :, pl.ds(lo * S, (hi - lo) * S)])
            out = (out[0:8] + out[8:16]) + out[16:24]
            for j in range(lo, hi):
                term = out[:, (j - lo) * S : (j - lo + 1) * S]
                at = near_slot(p, j)
                seen[at] = seen[at] - term if at in seen else -term
        for at, value in seen.items():
            extf[at] = value

    scatter(2, 9)
    force_copies = []
    for n, (dx, dy) in enumerate(DIRECTIONS):
        if dx == 0:
            here, there = pl.ds(0, 2), pl.ds(0, 2)
        elif dx == 1:
            here, there = pl.ds(2, 1), pl.ds(0, 1)
        else:
            here, there = pl.ds(3, 1), pl.ds(1, 1)
        copy = pltpu.make_async_remote_copy(
            src_ref=extf.at[PLACE[dy], here],
            dst_ref=frecv.at[n, there],
            send_sem=fo_send.at[n],
            recv_sem=fo_recv.at[n],
            device_id=device(dx, dy),
            device_id_type=MESH,
        )
        copy.start()
        force_copies.append(copy)

    scatter(0, 2)
    total = []
    for p in range(NP):
        mine = extf[0, p]
        for k in range(NE):
            mine = mine + grad[:, k * NP + p, :]
        total.append(mine)
    for n, (dx, dy) in enumerate(DIRECTIONS):
        force_copies[n].wait_recv()
        for p in range(NP):
            if dx == 0 or (dx == 1) == (p == 0):
                total[p] = total[p] + frecv[n, p]
    for p in range(NP):
        for m in range(3):
            forces[p, m] = total[p][m : m + 1]

    for copy in (*pos_copies, *force_copies):
        copy.wait_send()
    halo2.sent(range(len(GROUPS2)))
    write.wait()


def solution(mesh):
    gx_size, yz_size = mesh.shape["gx"], mesh.shape["yz"]

    def body(features, positions, *rest):
        args = (features, jnp.transpose(positions, (0, 2, 1, 3)), *rest)
        vmem = pl.BlockSpec(memory_space=pltpu.VMEM)
        anywhere = pl.BlockSpec(memory_space=pl.ANY)
        dma = pltpu.SemaphoreType.DMA
        n_dir = len(DIRECTIONS)

        def run_all(*refs):
            kernel(gx_size, yz_size, *refs)

        small = [pltpu.VMEM(x.shape, x.dtype) for x in args[1:]]
        new_features, force = pl.pallas_call(
            run_all,
            out_shape=(
                jax.ShapeDtypeStruct((NP, 1, S, BLOCKS * C), BF16),
                jax.ShapeDtypeStruct((NP, 3, 1, S), F32),
            ),
            in_specs=[pl.BlockSpec(memory_space=pltpu.HBM)] * 10,
            out_specs=(anywhere, vmem),
            scratch_shapes=small
            + [
                *[pltpu.VMEM((3, 4, hi - lo, S, C), BF16) for lo, hi in GROUPS + GROUPS2],
                pltpu.VMEM((3, 4, 8, S), F32),
                pltpu.VMEM((NP, ROWS, NEAR), BF16),
                pltpu.VMEM((15, NP * ROWS, C), F32),
                pltpu.VMEM((4, NP * ROWS, C), F32),
                pltpu.VMEM((128, 19 * C), BF16),
                pltpu.VMEM((128, 8, S), F32),
                pltpu.VMEM((8, 8, S), F32),
                pltpu.VMEM((4, 8, S), F32),
                pltpu.VMEM((2, 8, S), F32),
                pltpu.VMEM((BLOCKS, NP * S, C), F32),
                pltpu.VMEM((BLOCKS, NP * ROWS, C), F32),
                pltpu.VMEM((NP, 1, S, BLOCKS * C), BF16),
                pltpu.VMEM((4 * S, KP * 2 * C), BF16),
                pltpu.VMEM((8, 8, S), F32),
                pltpu.VMEM((3, 4, 8, S), F32),
                pltpu.VMEM((n_dir, NP, 8, S), F32),
                dma((len(small),)),
                dma((BLOCKS,)),
                dma,
                dma((n_dir,)),
                dma((n_dir,)),
                dma((len(GROUPS), Halo.COUNT)),
                dma((len(GROUPS), Halo.COUNT)),
                dma((len(GROUPS2), Halo.COUNT)),
                dma((len(GROUPS2), Halo.COUNT)),
                dma((n_dir,)),
                dma((n_dir,)),
            ],
            compiler_params=pltpu.CompilerParams(
                collective_id=0, has_side_effects=True, vmem_limit_bytes=60 * 1024 * 1024
            ),
            cost_estimate=pl.CostEstimate(
                flops=4 * 10**9, bytes_accessed=2 * 10**6, transcendentals=10**5
            ),
        )(*args)
        return new_features, jnp.transpose(force, (0, 2, 1, 3))

    in_specs = (
        P("gx", "yz", None, None),
        P("gx", "yz", None, None),
        P(None, "gx", "yz", None),
        P(None, "gx", "yz", None),
        P(),
        P(),
        P(),
        P(),
        P(),
        P(),
    )
    out_specs = (P("gx", "yz", None, None), P("gx", "yz", None, None))
    return jax.shard_map(body, mesh=mesh, in_specs=in_specs, out_specs=out_specs, check_vma=False)
```

profile of v0, /device:TPU:2, one launch (start us, length us, event | category | flops | bytes accessed | tf_op | source)
XLA Modules:
  0.0 60.0 jit_solution(8396229596975119850)
XLA Ops:
  0.6 56.8 %shard_map.113 = (bf16[2,1,128,1152]{3,2,1,0:T(8,128)(2,1)}, f32[2,3,1,128]{3,2,1,0:T(1,128)}) custom-call(bf16[2,1,128,1152]{3,2,1,0:T(8,128)(2,1)} %refs_0_.1, f32[2,3,1,128]{3,2,1,0:T(1,128)} %bitcast.3, s32[3,2,1,128]{3,2,1,0:T(1,128)} %refs_2_.1, s32[3,2,1,128]{3,2,1,0:T(1,128)} %refs_3_.1, f32[8,896]{1,0:T(8,128)} %refs_4_.1, f32[8,256]{1,0:T(8,128)} %refs_5_.1, ...), custom_call_target="tpu_custom_call" | custom-call | flops 4000000000 | bytes 2000000 | tf_op jit(solution)/shard_map/pallas_call | solution.py:597
  57.4 0.0 copy-start
  57.5 1.9 %copy.14 = bf16[2,1,128,1152]{3,2,1,0:T(8,128)(2,1)} copy(bf16[2,1,128,1152]{3,2,1,0:T(8,128)(2,1)} %get-tuple-element.8) | data formatting | bytes 1179648
  59.4 0.0 copy-done
  59.4 0.6 copy.15
Async XLA Ops:
  57.4 1.9 %copy-start = (f32[2,3,1,128]{3,2,1,0:T(1,128)S(1)}, f32[2,3,1,128]{3,2,1,0:T(1,128)}, u32[]{:S(2)}) copy-start(f32[2,3,1,128]{3,2,1,0:T(1,128)} %get-tuple-element.5) | copy-start | bytes 9220
where the time goes:
time: 60.8 us; the launch traced here: 60 us
  Pallas kernels  56.8 us (93%)
  local copies, waits for them, and re-layouts  2.51 us (4%)
  between operations  0.65 us (1%)
    pallas_call x1, Pallas kernels, body(): pl.pallas_call(run_all, out_shape=(jax.ShapeDtypeStruct((NP, 1, S, BLOCKS...  56.8 us
    unnamed x4, local copies, waits for them, and re-layouts  2.51 us

commit v1 on v0

--- a/solution.py
+++ b/solution.py
@@ -161,14 +161,19 @@
     coef,
     qcoef,
     wide,
+    w_turned,
     zf,
+    ang,
     pj,
     geo,
     edges,
     acc,
+    gate,
     gsc,
+    raw,
     mix_out,
-    xq,
+    side,
+    sums,
     grad,
     extf,
     frecv,
@@ -201,13 +206,8 @@
     for load in small_loads:
         load.start()
     pos, dst, shift, wr, wq, w_scalar, w_gate, w_vector, w_tensor = small
-    loads = []
-    for c in range(BLOCKS):
-        load = pltpu.make_async_copy(
-            feat.at[:, 0, :, pl.ds(c * C, C)], block(ext, c, 0, pl.ds(0, 2)), load_sem.at[c]
-        )
-        load.start()
-        loads.append(load)
+    feat_load = pltpu.make_async_copy(feat, raw, load_sem)
+    feat_load.start()
 
     barrier = pltpu.get_barrier_semaphore()
     for step in DIRECTIONS:
@@ -219,6 +219,15 @@
         posx[0, p] = jnp.zeros((8, S), F32)
         for m in range(3):
             posx[0, p, pl.ds(m, 1), :] = pos[p, m]
+
+    def turn(g):
+        for c in range(*GROUPS[g]):
+            for p in range(NP):
+                tile = raw[p, 0, :, pl.ds(c * C, C)].astype(F32)
+                block(ext, c, 0, p)[...] = jnp.transpose(tile).astype(BF16)
+
+    feat_load.wait()
+    turn(0)
     pl.semaphore_wait(barrier, len(DIRECTIONS))
 
     pos_copies = []
@@ -241,37 +250,31 @@
         pos_copies.append(copy)
 
     halo = Halo(ext, f1_send, f1_recv, device, low_wrap, high_wrap)
-    for g, (lo, hi) in enumerate(GROUPS):
-        for c in range(lo, hi):
-            loads[c].wait()
+    halo.own(0)
+    for g in range(1, len(GROUPS)):
+        turn(g)
         halo.own(g)
 
-    lane = lax.broadcasted_iota(jnp.int32, (S, S), 1).astype(F32)
+    atom = lax.broadcasted_iota(jnp.int32, (S, ROWS), 0).astype(F32)
     edges[...] = jnp.zeros_like(edges)
-    for k in range(NE):
-        for p in range(NP):
-            row = dst[k, p].astype(F32)
-            edges[0, pl.ds(k * NP + p, 1), :] = row
+    for p in range(NP):
+        rows = [dst[k, p].astype(F32) for k in range(NE)]
+        for k in range(NE):
+            edges[0, pl.ds(k * NP + p, 1), :] = rows[k]
             edges[1, pl.ds(k * NP + p, 1), :] = shift[k, p].astype(F32)
-            column = jnp.transpose(jnp.broadcast_to(row, (S, S))) - lane
-            for j in range(9):
-                x, y = near_pillar(p, j)
-                hit = column == float((3 * x + y) * S)
-                oh[p, pl.ds(k * S, S), pl.ds(j * S, S)] = jnp.where(hit, 1.0, 0.0).astype(BF16)
-
-    wide[...] = jnp.zeros_like(wide)
-    w_r, rest_r = split(wr[...])
-    w_q, rest_q = split(wq[...])
-    zeros_r = jnp.zeros_like(w_r)
-    zeros_q = jnp.zeros_like(w_q)
-    n_r, n_q = 7 * C, 2 * C
-    wide[pl.ds(0, 32), pl.ds(0, n_r)] = jnp.concatenate([w_r, rest_r, w_r, zeros_r], 0).astype(BF16)
-    wide[pl.ds(0, 32), pl.ds(n_r, n_q)] = jnp.concatenate([w_q, rest_q, w_q, zeros_q], 0).astype(BF16)
-    wide[pl.ds(32, 32), pl.ds(n_r + n_q, n_q)] = jnp.concatenate([w_q, rest_q, w_q, zeros_q], 0).astype(BF16)
-    copy_row = lax.broadcasted_iota(jnp.int32, (8, 8 * C), 0)
-    copy_col = lax.broadcasted_iota(jnp.int32, (8, 8 * C), 1)
-    copies = jnp.where((copy_col >= copy_row * C) & (copy_col < (copy_row + 1) * C), 1.0, 0.0)
-    wide[pl.ds(64, 16), pl.ds(n_r + 2 * n_q, 8 * C)] = jnp.concatenate([copies, copies], 0).astype(BF16)
+        place = jnp.concatenate(rows, axis=1) - atom
+        for j in range(9):
+            x, y = near_pillar(p, j)
+            hit = place == float((3 * x + y) * S)
+            oh[p, pl.ds(j * S, S), :] = jnp.where(hit, 1.0, 0.0).astype(BF16)
+
+    for f in range(9):
+        w = wr[:, pl.ds(f * C, C)] if f < 7 else wq[:, pl.ds((f - 7) * C, C)]
+        high, low = split(w)
+        rows = jnp.concatenate([high, low, high, jnp.zeros_like(w)], axis=0)
+        wide[pl.ds(f * C, C), :] = jnp.transpose(rows).astype(BF16)
+    for i, w in enumerate((w_scalar, w_gate, w_vector, w_tensor)):
+        w_turned[pl.ds(i * C, C), :] = jnp.transpose(w[...].astype(F32)).astype(BF16)
 
     for copy in pos_copies:
         copy.wait_recv()
@@ -280,12 +283,13 @@
         first, rest = split(places)
         second, third = split(rest)
         parts = jnp.concatenate([first, second, third, jnp.zeros_like(first)], 0).astype(BF16)
-        found = dot(parts, oh[p], (1, 1))
+        found = dot(parts, oh[p])
         far = (found[0:8] + found[8:16]) + found[16:24]
         for k in range(NE):
             pj[k * NP + p] = far[:, k * S : (k + 1) * S] - posx[0, p]
 
     place = edges[0]
+    pj[pl.ds(KP, 8 - KP)] = jnp.zeros((8 - KP, 8, S), F32)
     own_p = lax.rem(lax.broadcasted_iota(jnp.int32, (8, S), 0), NP).astype(F32)
     one = jnp.ones_like(place)
     nil = jnp.zeros_like(place)
@@ -302,10 +306,7 @@
     rho = jnp.sqrt(disp_x * disp_x + disp_y * disp_y + disp_z * disp_z + SOFTENING)
     inverse = 1.0 / rho
     u_x, u_y, u_z = disp_x * inverse, disp_y * inverse, disp_z * inverse
-    geo[0] = u_x
-    geo[1] = u_y
-    geo[2] = u_z
-    geo[3] = inverse
+    geo[...] = inverse
     length_sq = u_x * u_x + u_y * u_y + u_z * u_z
     angular = (
         u_x,
@@ -317,200 +318,211 @@
         ROOT_THREE * u_x * u_z,
         0.5 * ROOT_THREE * (u_x * u_x - u_y * u_y),
     )
+    for f in range(8):
+        ang[f] = angular[f]
     zf[...] = jnp.zeros_like(zf)
     for b in range(NB):
         off = (rho - (0.5 + SPACING * b)) / SPACING
         basis = jnp.exp(-(off * off))
         slope = basis * off * (-2.0 / SPACING)
-        high, low = split(basis)
-        zf[b] = high
-        zf[8 + b] = high
-        zf[16 + b] = low
-        high, low = split(slope)
-        zf[32 + b] = high
-        zf[40 + b] = high
-        zf[48 + b] = low
-        high, low = split(angular[b])
-        zf[64 + b] = high
-        zf[72 + b] = low
-
-    halo.corners(0)
-    for p in range(NP):
-        for k in range(NE):
-            rows = jnp.transpose(zf[:, k * NP + p, :]).astype(BF16)
-            at = pl.ds(p * ROWS + k * S, S)
-            for f in range(0, 19, 2):
-                n = min(2, 19 - f)
-                out = dot(rows, wide[:, pl.ds(f * C, n * C)])
-                for i in range(n):
-                    if f + i < 7:
-                        coef[f + i, at, :] = out[:, i * C : (i + 1) * C]
-                    elif f + i < 11:
-                        qcoef[f + i - 7, at, :] = out[:, i * C : (i + 1) * C]
-                    else:
-                        coef[f + i - 4, at, :] = out[:, i * C : (i + 1) * C]
-
-    def gather(bufs, lo, hi, beyond):
+        for i, value in enumerate((basis, slope)):
+            high, low = split(value)
+            zf[32 * i + b] = high
+            zf[32 * i + 8 + b] = high
+            zf[32 * i + 16 + b] = low
+
+    def columns(p, k):
+        return pl.ds((p * NE + k) * S, S)
+
+    for p in range(NP):
+        values = jnp.concatenate([zf[:, k * NP + p, :] for k in range(NE)], axis=1).astype(BF16)
+        at = pl.ds(p * ROWS, ROWS)
+        out = dot(wide[pl.ds(0, 7 * C), :], values[0:32])
+        for f in range(7):
+            coef[f, :, at] = out[f * C : (f + 1) * C]
+        qcoef[0, :, at] = dot(wide[pl.ds(8 * C, C), :], values[0:32])
+        out = dot(wide[pl.ds(7 * C, 2 * C), :], values[32:64])
+        for f in range(2):
+            qcoef[1 + f, :, at] = out[f * C : (f + 1) * C]
+
+    def gather(bufs, g, lo, beyond):
+        buf = bufs[g]
+        n = buf.shape[2]
         for p in range(NP):
-            for c in range(lo, hi, 2):
-                n = min(2, hi - c)
-                parts = [c + i for i in range(n)]
-                if beyond:
-                    rows = [block(bufs, i, pl.ds(0, 3), 3 - p)[...].reshape(3 * S, C) for i in parts]
-                    out = dot(oh[p, :, pl.ds(6 * S, 3 * S)], jnp.concatenate(rows, axis=1))
-                else:
-                    rows = [block(bufs, i, pl.ds(0, 3), pl.ds(0, 2))[...].reshape(6 * S, C) for i in parts]
-                    out = dot(oh[p, :, pl.ds(0, 6 * S)], jnp.concatenate(rows, axis=1))
-                at = pl.ds(p * ROWS, ROWS)
-                for i in range(n):
-                    term = out[:, i * C : (i + 1) * C]
-                    gsc[c + i, at, :] = gsc[c + i, at, :] + term if beyond else term
+            around = range(6, 9) if beyond else range(6)
+            tiles = [buf[near_slot(p, j)].reshape(n * C, S) for j in around]
+            picks = oh[p, pl.ds(around[0] * S, len(around) * S), :]
+            out = dot(jnp.concatenate(tiles, axis=1), picks)
+            at = pl.ds(p * ROWS, ROWS)
+            for i in range(n):
+                term = out[i * C : (i + 1) * C]
+                gsc[lo + i, :, at] = gsc[lo + i, :, at] + term if beyond else term
 
     def each_row(fn):
         for p in range(NP):
 
             def run(i, carry, p=p):
-                r = pl.multiple_of(i * STEP, STEP)
-                fn(p, r, [pl.ds(p * ROWS + k * S + r, STEP) for k in range(NE)], pl.ds(p * S + r, STEP))
+                fn(p, pl.ds(pl.multiple_of(i * STEP, STEP), STEP))
                 return carry
 
-            lax.fori_loop(0, S // STEP, run, 0)
-
-    def message_sv(p, r, at, to):
-        total = [jnp.zeros((STEP, C), F32) for _ in range(BLOCKS)]
+            lax.fori_loop(0, C // STEP, run, 0)
+
+    def angle(f, p, k):
+        return ang[f, pl.ds(k * NP + p, 1), :]
+
+    def own_columns(p):
+        return pl.ds(p * S, S)
+
+    def message_sv(p, r):
+        total = [jnp.zeros((STEP, S), F32) for _ in range(BLOCKS)]
         for k in range(NE):
-            e = at[k]
-            s = gsc[0, e, :]
-            v = [gsc[1 + m, e, :] for m in range(3)]
-            u = [coef[7 + m, e, :] for m in range(3)]
+            e = columns(p, k)
+            s = gsc[0, r, e]
+            v = [gsc[1 + m, r, e] for m in range(3)]
+            u = [angle(m, p, k) for m in range(3)]
             along = u[0] * v[0] + u[1] * v[1] + u[2] * v[2]
-            total[0] = total[0] + coef[0, e, :] * s + coef[1, e, :] * along
-            r3s = coef[3, e, :] * s
-            r4 = coef[4, e, :]
+            total[0] = total[0] + coef[0, r, e] * s + coef[1, r, e] * along
+            r3s = coef[3, r, e] * s
+            r4 = coef[4, r, e]
             for m in range(3):
                 total[1 + m] = total[1 + m] + r3s * u[m] + r4 * v[m]
-            r5s = coef[5, e, :] * s
+            r5s = coef[5, r, e] * s
             for n in range(5):
-                total[4 + n] = total[4 + n] + r5s * coef[10 + n, e, :]
+                total[4 + n] = total[4 + n] + r5s * angle(3 + n, p, k)
         for b in range(BLOCKS):
-            acc[b, to, :] = total[b]
+            acc[b, r, own_columns(p)] = total[b]
 
     def message_t(lo, hi):
-        def fn(p, r, at, to):
-            total = [acc[b, to, :] for b in (0, *range(lo, hi))]
+        def fn(p, r):
+            at = own_columns(p)
+            total = [acc[b, r, at] for b in (0, *range(lo, hi))]
             for k in range(NE):
-                e = at[k]
+                e = columns(p, k)
                 along = None
-                r6 = coef[6, e, :]
+                r6 = coef[6, r, e]
                 for n in range(lo, hi):
-                    t = gsc[n, e, :]
-                    term = coef[6 + n, e, :] * t
+                    t = gsc[n, r, e]
+                    term = angle(n - 1, p, k) * t
                     along = term if along is None else along + term
                     total[1 + n - lo] = total[1 + n - lo] + r6 * t
-                total[0] = total[0] + coef[2, e, :] * along
+                total[0] = total[0] + coef[2, r, e] * along
             for i, b in enumerate((0, *range(lo, hi))):
-                acc[b, to, :] = total[i]
+                acc[b, r, at] = total[i]
 
         return fn
 
     third = 1.0 / NE
 
-    def mix(lo, hi, weight):
+    def mix(lo, hi, w):
+        terms = jnp.concatenate([(acc[b] * third).astype(BF16) for b in range(lo, hi)], axis=1)
+        out = dot(w_turned[pl.ds(w * C, C), :], terms)
         for b in range(lo, hi):
-            acc[b] = dot((acc[b] * third).astype(BF16), weight[...])
+            acc[b] = out[:, (b - lo) * NP * S : (b - lo + 1) * NP * S]
 
     halo.near(0)
-    gather(ext, 0, 4, False)
+    gather(ext, 0, 0, False)
+    halo.corners(0)
     halo.near(1)
-    gather(ext, 4, 7, False)
+    gather(ext, 1, 4, False)
+    halo.near(2)
+    gather(ext, 2, 7, False)
     halo.corners(1)
-    halo.near(2)
-    gather(ext, 7, 9, False)
     halo.rest(0)
-    gather(ext, 0, 4, True)
+    gather(ext, 0, 0, True)
     each_row(message_sv)
-    mix(1, 4, w_vector)
+    mix(1, 4, 2)
     halo.corners(2)
     halo.rest(1)
-    gather(ext, 4, 7, True)
+    gather(ext, 1, 4, True)
     each_row(message_t(4, 7))
-    mix(4, 7, w_tensor)
     halo.rest(2)
-    gather(ext, 7, 9, True)
+    gather(ext, 2, 7, True)
     each_row(message_t(7, 9))
-    mix(7, 9, w_tensor)
-
-    scalar = (acc[0] * third).astype(BF16)
-    pre = dot(scalar, w_scalar[...])
+
+    out = dot(w_turned[pl.ds(0, 2 * C), :], (acc[0] * third).astype(BF16))
+    pre = out[0:C]
     acc[0] = pre * jax.nn.sigmoid(pre)
-    gsc[0, pl.ds(0, NP * S), :] = jax.nn.sigmoid(dot(scalar, w_gate[...]))
-
-    def update_sv(p, r, at, to):
-        gate = gsc[0, to, :]
-        rows = pl.ds(r, STEP)
+    gate[...] = jax.nn.sigmoid(out[C : 2 * C])
+
+    def update_sv(p, r):
+        at = own_columns(p)
+        g = gate[r, at]
         for b in range(READ_BLOCKS):
-            old = block(ext, b, 0, p)[rows, :].astype(F32)
-            step = gate * acc[b, to, :] if b > 0 else acc[0, to, :]
-            new = (old + step).astype(BF16)
-            block(ext2, b, 0, p)[rows, :] = new
-            mix_out[p, 0, rows, pl.ds(b * C, C)] = new
+            old = block(ext, b, 0, p)[r, :].astype(F32)
+            step = g * acc[b, r, at] if b > 0 else acc[0, r, at]
+            block(ext2, b, 0, p)[r, :] = (old + step).astype(BF16)
 
     each_row(update_sv)
     halo2 = Halo(ext2, f2_send, f2_recv, device, low_wrap, high_wrap)
     for g in range(len(GROUPS2)):
         halo2.own(g)
 
-    def update_t(p, r, at, to):
-        gate = gsc[0, to, :]
-        rows = pl.ds(r, STEP)
-        for b in range(READ_BLOCKS, BLOCKS):
-            old = block(ext, b, 0, p)[rows, :].astype(F32)
-            mix_out[p, 0, rows, pl.ds(b * C, C)] = (old + gate * acc[b, to, :]).astype(BF16)
-
-    each_row(update_t)
+    mix(4, 9, 3)
+    for p in range(NP):
+        for b in range(BLOCKS):
+            if b < READ_BLOCKS:
+                new = block(ext2, b, 0, p)[...].astype(F32)
+            else:
+                at = own_columns(p)
+                new = block(ext, b, 0, p)[...].astype(F32) + gate[:, at] * acc[b, :, at]
+            mix_out[p, 0, :, pl.ds(b * C, C)] = jnp.transpose(new).astype(BF16)
     write = pltpu.make_async_copy(mix_out, mixed, out_sem)
     write.start()
 
+    def near_side(p, r):
+        own = [block(ext2, b, 0, p)[r, :].astype(F32) for b in range(READ_BLOCKS)]
+        for k in range(NE):
+            e = columns(p, k)
+            u = [angle(m, p, k) for m in range(3)]
+            along = u[0] * own[1] + u[1] * own[2] + u[2] * own[3]
+            q1 = qcoef[0, r, e]
+            side[0, r, e] = qcoef[1, r, e] * own[0]
+            side[1, r, e] = qcoef[2, r, e] * along
+            side[2, r, e] = q1 * along
+            for m in range(3):
+                side[3 + m, r, e] = q1 * own[1 + m]
+
     halo2.near(0)
-    gather(ext2, 0, 2, False)
+    gather(ext2, 0, 0, False)
     halo2.corners(0)
+    each_row(near_side)
     halo2.near(1)
-    gather(ext2, 2, 4, False)
+    gather(ext2, 1, 2, False)
     halo2.corners(1)
     halo.sent(range(len(GROUPS)))
     halo2.rest(0)
-    gather(ext2, 0, 2, True)
+    gather(ext2, 0, 0, True)
     halo2.rest(1)
-    gather(ext2, 2, 4, True)
-
-    def pair(p, r, at, to):
-        rows = pl.ds(r, STEP)
-        own = [block(ext2, b, 0, p)[rows, :].astype(F32) for b in range(READ_BLOCKS)]
+    gather(ext2, 1, 2, True)
+
+    sums[...] = jnp.zeros_like(sums)
+    for p in range(NP):
+
+        def pair(i, carry, p=p):
+            r = pl.ds(pl.multiple_of(i * STEP, STEP), STEP)
+            carry = list(carry)
+            for k in range(NE):
+                e = columns(p, k)
+                far = [gsc[b, r, e] for b in range(READ_BLOCKS)]
+                u = [angle(m, p, k) for m in range(3)]
+                along = u[0] * far[1] + u[1] * far[2] + u[2] * far[3]
+                carry[4 * k] = carry[4 * k] + side[0, r, e] * far[0] + side[1, r, e] * along
+                own_q = side[2, r, e]
+                for m in range(3):
+                    term = side[3 + m, r, e] * along + own_q * far[1 + m]
+                    carry[4 * k + 1 + m] = carry[4 * k + 1 + m] + term
+            return tuple(carry)
+
+        zero = jnp.zeros((STEP, S), F32)
+        totals = lax.fori_loop(0, C // STEP, pair, (zero,) * (4 * NE))
         for k in range(NE):
-            e = at[k]
-            far = [gsc[b, e, :] for b in range(READ_BLOCKS)]
-            u = [coef[7 + m, e, :] for m in range(3)]
-            own_along = u[0] * own[1] + u[1] * own[2] + u[2] * own[3]
-            far_along = u[0] * far[1] + u[1] * far[2] + u[2] * far[3]
-            q1 = qcoef[1, e, :]
-            own_q, far_q = q1 * own_along, q1 * far_along
-            terms = [qcoef[2, e, :] * (own[0] * far[0]) + qcoef[3, e, :] * (own_along * far_along)]
-            for m in range(3):
-                terms.append(own[1 + m] * far_q + own_q * far[1 + m])
-            at_col = (k * NP + p) * 2 * C
             for q in range(4):
-                high, low = split(terms[q])
-                xq[pl.ds(q * S + r, STEP), pl.ds(at_col, C)] = high.astype(BF16)
-                xq[pl.ds(q * S + r, STEP), pl.ds(at_col + C, C)] = low.astype(BF16)
-
-    each_row(pair)
-    mask_row = lax.broadcasted_iota(jnp.int32, (16, KP * 2 * C), 0) * (2 * C)
-    mask_col = lax.broadcasted_iota(jnp.int32, (16, KP * 2 * C), 1)
-    mask = jnp.where((mask_col >= mask_row) & (mask_col < mask_row + 2 * C), 1.0, 0.0).astype(BF16)
-    sums = dot(mask, xq[...], (1, 1))[0:8]
-    t_rho, g_x, g_y, g_z = (sums[:, q * S : (q + 1) * S] for q in range(4))
-    u_x, u_y, u_z = geo[0], geo[1], geo[2]
-    inverse = geo[3]
+                row = jnp.sum(totals[4 * k + q], axis=0, keepdims=True)
+                sums[q, pl.ds(k * NP + p, 1), :] = row
+
+    t_rho, g_x, g_y, g_z = (sums[q] for q in range(4))
+    u_x, u_y, u_z = ang[0], ang[1], ang[2]
+    inverse = geo[...]
     radial_part = t_rho - (u_x * g_x + u_y * g_y + u_z * g_z) * inverse
     grad[...] = jnp.zeros_like(grad)
     grad[0] = radial_part * u_x + g_x * inverse
@@ -529,7 +541,7 @@
     def scatter(lo, hi):
         seen = {}
         for p in range(NP):
-            out = dot(parts[p], oh[p, :, pl.ds(lo * S, (hi - lo) * S)])
+            out = dot(parts[p], oh[p, pl.ds(lo * S, (hi - lo) * S), :], (1, 1))
             out = (out[0:8] + out[8:16]) + out[16:24]
             for j in range(lo, hi):
                 term = out[:, (j - lo) * S : (j - lo + 1) * S]
@@ -606,23 +618,28 @@
             + [
                 *[pltpu.VMEM((3, 4, hi - lo, S, C), BF16) for lo, hi in GROUPS + GROUPS2],
                 pltpu.VMEM((3, 4, 8, S), F32),
-                pltpu.VMEM((NP, ROWS, NEAR), BF16),
-                pltpu.VMEM((15, NP * ROWS, C), F32),
-                pltpu.VMEM((4, NP * ROWS, C), F32),
-                pltpu.VMEM((128, 19 * C), BF16),
-                pltpu.VMEM((128, 8, S), F32),
+                pltpu.VMEM((NP, NEAR, ROWS), BF16),
+                pltpu.VMEM((7, C, NP * ROWS), F32),
+                pltpu.VMEM((3, C, NP * ROWS), F32),
+                pltpu.VMEM((9 * C, 32), BF16),
+                pltpu.VMEM((4 * C, C), BF16),
+                pltpu.VMEM((64, 8, S), F32),
                 pltpu.VMEM((8, 8, S), F32),
+                pltpu.VMEM((8, 8, S), F32),
+                pltpu.VMEM((8, S), F32),
+                pltpu.VMEM((2, 8, S), F32),
+                pltpu.VMEM((BLOCKS, C, NP * S), F32),
+                pltpu.VMEM((C, NP * S), F32),
+                pltpu.VMEM((BLOCKS, C, NP * ROWS), F32),
+                pltpu.VMEM((NP, 1, S, BLOCKS * C), BF16),
+                pltpu.VMEM((NP, 1, S, BLOCKS * C), BF16),
+                pltpu.VMEM((6, C, NP * ROWS), F32),
                 pltpu.VMEM((4, 8, S), F32),
-                pltpu.VMEM((2, 8, S), F32),
-                pltpu.VMEM((BLOCKS, NP * S, C), F32),
-                pltpu.VMEM((BLOCKS, NP * ROWS, C), F32),
-                pltpu.VMEM((NP, 1, S, BLOCKS * C), BF16),
-                pltpu.VMEM((4 * S, KP * 2 * C), BF16),
                 pltpu.VMEM((8, 8, S), F32),
                 pltpu.VMEM((3, 4, 8, S), F32),
                 pltpu.VMEM((n_dir, NP, 8, S), F32),
                 dma((len(small),)),
-                dma((BLOCKS,)),
+                dma,
                 dma,
                 dma((n_dir,)),
                 dma((n_dir,)),

time: 60.8 us -> 59.9 us (0.985)
  Pallas kernels: 56.8 us -> 55.8 us
    pallas_call x1, Pallas kernels: 56.8 us -> 55.8 us  [body(): pl.pallas_call(run_all, out_shape=(jax.ShapeDtypeStruct((NP, 1, S, BLOCKS...]
where the time goes in v1:
time: 59.9 us; the launch traced here: 59 us
  Pallas kernels  55.8 us (93%)
  local copies, waits for them, and re-layouts  2.51 us (4%)
  between operations  0.65 us (1%)
    pallas_call x1, Pallas kernels, body(): pl.pallas_call(run_all, out_shape=(jax.ShapeDtypeStruct((NP, 1, S, BLOCKS...  55.8 us
    unnamed x4, local copies, waits for them, and re-layouts  2.51 us

profile of v1, /device:TPU:2, one launch (start us, length us, event | category | flops | bytes accessed | tf_op | source)
XLA Modules:
  0.0 59.0 jit_solution(9668410007070418738)
XLA Ops:
  0.6 55.8 %shard_map.113 = (bf16[2,1,128,1152]{3,2,1,0:T(8,128)(2,1)}, f32[2,3,1,128]{3,2,1,0:T(1,128)}) custom-call(bf16[2,1,128,1152]{3,2,1,0:T(8,128)(2,1)} %refs_0_.1, f32[2,3,1,128]{3,2,1,0:T(1,128)} %bitcast.3, s32[3,2,1,128]{3,2,1,0:T(1,128)} %refs_2_.1, s32[3,2,1,128]{3,2,1,0:T(1,128)} %refs_3_.1, f32[8,896]{1,0:T(8,128)} %refs_4_.1, f32[8,256]{1,0:T(8,128)} %refs_5_.1, ...), custom_call_target="tpu_custom_call" | custom-call | flops 4000000000 | bytes 2000000 | tf_op jit(solution)/shard_map/pallas_call | solution.py:609
  56.5 0.0 copy-start
  56.5 1.9 %copy.14 = bf16[2,1,128,1152]{3,2,1,0:T(8,128)(2,1)} copy(bf16[2,1,128,1152]{3,2,1,0:T(8,128)(2,1)} %get-tuple-element.8) | data formatting | bytes 1179648
  58.4 0.0 copy-done
  58.4 0.6 copy.15
Async XLA Ops:
  56.5 1.9 %copy-start = (f32[2,3,1,128]{3,2,1,0:T(1,128)S(1)}, f32[2,3,1,128]{3,2,1,0:T(1,128)}, u32[]{:S(2)}) copy-start(f32[2,3,1,128]{3,2,1,0:T(1,128)} %get-tuple-element.5) | copy-start | bytes 9220

commit v2 on v1

--- a/solution.py
+++ b/solution.py
@@ -25,7 +25,7 @@
 NEAR = 9 * S
 STEP = 16
 GROUPS = ((0, 4), (4, 7), (7, 9))
-GROUPS2 = ((0, 2), (2, 4))
+GROUPS2 = ((0, 4),)
 DIRECTIONS = tuple((dx, dy) for dx in (-1, 0, 1) for dy in (-1, 0, 1) if (dx, dy) != (0, 0))
 
 
@@ -43,7 +43,8 @@
 
 
 def near_slot(p, j):
-    return (j // 2, j % 2) if j < 6 else (j - 6, 3 - p)
+    y = (1, 2, 0, 0, 1, 2, 0, 1, 2)[j]
+    return (y, (p, 1 - p, 3 - p)[j // 3])
 
 
 def near_pillar(p, j):
@@ -59,41 +60,43 @@
 
 
 class Halo:
-    COUNT = 10
+    COUNT = 12
 
     def __init__(self, bufs, send, recv, device, low_wrap, high_wrap):
         self.copies = {}
         self.low_wrap, self.high_wrap = low_wrap, high_wrap
-        own, ghosts = pl.ds(0, 2), pl.ds(2, 2)
         for g, buf in enumerate(bufs):
-            spans = {
-                "x0": (buf.at[0, 0], buf.at[0, 2], (-1, 0)),
-                "x1": (buf.at[0, 1], buf.at[0, 3], (1, 0)),
-            }
-            for sign, step, to in (("m", -1, 2), ("p", 1, 1)):
-                spans |= {
-                    "y" + sign: (buf.at[0, own], buf.at[to, own], (0, step)),
-                    "c" + sign: (buf.at[0, ghosts], buf.at[to, ghosts], (0, step)),
-                    "w0" + sign: (buf.at[0, 0], buf.at[to, 2], (-1, step)),
-                    "w1" + sign: (buf.at[0, 1], buf.at[to, 3], (1, step)),
-                }
-            for n, (name, (src, dst, step)) in enumerate(spans.items()):
-                self.copies[name, g] = pltpu.make_async_remote_copy(
-                    src_ref=src,
-                    dst_ref=dst,
-                    send_sem=send.at[g, n],
-                    recv_sem=recv.at[g, n],
-                    device_id=device(*step),
-                    device_id_type=MESH,
-                )
-
-    def start(self, g, *names):
+            n = 0
+            for own, ghost, dx in ((0, 2, -1), (1, 3, 1)):
+                spans = {"x": (buf.at[0, own], buf.at[0, ghost], (dx, 0))}
+                for sign, step, to in (("m", -1, 2), ("p", 1, 1)):
+                    spans |= {
+                        "y" + sign: (buf.at[0, own], buf.at[to, own], (0, step)),
+                        "c" + sign: (buf.at[0, ghost], buf.at[to, ghost], (0, step)),
+                        "w" + sign: (buf.at[0, own], buf.at[to, ghost], (dx, step)),
+                    }
+                for name, (src, dst, step) in spans.items():
+                    if name[0] != "w":
+                        slot = n
+                        n += 1
+                    else:
+                        slot = n - 1
+                    self.copies[name, own, g] = pltpu.make_async_remote_copy(
+                        src_ref=src,
+                        dst_ref=dst,
+                        send_sem=send.at[g, slot],
+                        recv_sem=recv.at[g, slot],
+                        device_id=device(*step),
+                        device_id_type=MESH,
+                    )
+
+    def start(self, own, g, *names):
         for name in names:
-            self.copies[name, g].start()
-
-    def arrived(self, g, *names):
+            self.copies[name, own, g].start()
+
+    def arrived(self, own, g, *names):
         for name in names:
-            self.copies[name, g].wait_recv()
+            self.copies[name, own, g].wait_recv()
 
     def sends(self, sign, plain, wrap):
         wraps = self.low_wrap if sign == "m" else self.high_wrap
@@ -102,33 +105,30 @@
         if plain is not None:
             pl.when(jnp.logical_not(wraps))(plain)
 
-    def own(self, g):
-        self.start(g, "x0", "x1", "ym", "yp")
+    def along_x(self, own, g):
+        self.start(own, g, "x")
         for sign in "mp":
-            self.sends(sign, None, lambda: self.start(g, "w0" + sign, "w1" + sign))
-
-    def near(self, g):
-        self.arrived(g, "ym", "yp")
-
-    def corners(self, g):
-        self.arrived(g, "x0", "x1")
+            self.sends(sign, None, lambda: self.start(own, g, "w" + sign))
+
+    def along_y(self, own, g):
+        self.start(own, g, "ym", "yp")
+
+    def near(self, own, g):
+        self.arrived(own, g, "ym", "yp")
+
+    def corners(self, own, g):
+        self.arrived(own, g, "x")
         for sign in "mp":
-            self.sends(sign, lambda: self.start(g, "c" + sign), None)
-
-    def rest(self, g):
-        for sign, wraps in (("m", self.high_wrap), ("p", self.low_wrap)):
-            pl.when(wraps)(lambda: self.arrived(g, "w0" + sign, "w1" + sign))
-            pl.when(jnp.logical_not(wraps))(lambda: self.arrived(g, "c" + sign))
+            self.sends(sign, lambda: self.start(own, g, "c" + sign), None)
+
+    def rest(self, own, g):
+        self.arrived(own, g, "cm", "cp")
 
     def sent(self, groups):
-        def done(*names):
-            for g in groups:
-                for name in names:
-                    self.copies[name, g].wait_send()
-
-        done("x0", "x1", "ym", "yp")
-        for sign in "mp":
-            self.sends(sign, lambda: done("c" + sign), lambda: done("w0" + sign, "w1" + sign))
+        for g in groups:
+            for own in range(NP):
+                for name in ("x", "ym", "yp", "cm", "cp"):
+                    self.copies[name, own, g].wait_send()
 
 
 def kernel(
@@ -155,7 +155,6 @@
     ext1,
     ext2,
     mix0,
-    mix1,
     posx,
     oh,
     coef,
@@ -189,7 +188,7 @@
     fo_send,
     fo_recv,
 ):
-    ext, ext2 = (ext0, ext1, ext2), (mix0, mix1)
+    ext, ext2 = (ext0, ext1, ext2), (mix0,)
     gx = lax.axis_index("gx")
     yz = lax.axis_index("yz")
 
@@ -250,10 +249,12 @@
         pos_copies.append(copy)
 
     halo = Halo(ext, f1_send, f1_recv, device, low_wrap, high_wrap)
-    halo.own(0)
-    for g in range(1, len(GROUPS)):
-        turn(g)
-        halo.own(g)
+    for g in range(len(GROUPS)):
+        if g > 0:
+            turn(g)
+        halo.along_x(1, g)
+        halo.along_y(0, g)
+        halo.along_y(1, g)
 
     atom = lax.broadcasted_iota(jnp.int32, (S, ROWS), 0).astype(F32)
     edges[...] = jnp.zeros_like(edges)
@@ -275,6 +276,8 @@
         wide[pl.ds(f * C, C), :] = jnp.transpose(rows).astype(BF16)
     for i, w in enumerate((w_scalar, w_gate, w_vector, w_tensor)):
         w_turned[pl.ds(i * C, C), :] = jnp.transpose(w[...].astype(F32)).astype(BF16)
+
+    halo.along_x(0, 0)
 
     for copy in pos_copies:
         copy.wait_recv()
@@ -345,27 +348,25 @@
         for f in range(2):
             qcoef[1 + f, :, at] = out[f * C : (f + 1) * C]
 
-    def gather(bufs, g, lo, beyond):
+    halo.along_x(0, 1)
+    halo.along_x(0, 2)
+
+    def gather(bufs, g, lo, p, first, last):
         buf = bufs[g]
         n = buf.shape[2]
-        for p in range(NP):
-            around = range(6, 9) if beyond else range(6)
-            tiles = [buf[near_slot(p, j)].reshape(n * C, S) for j in around]
-            picks = oh[p, pl.ds(around[0] * S, len(around) * S), :]
-            out = dot(jnp.concatenate(tiles, axis=1), picks)
-            at = pl.ds(p * ROWS, ROWS)
-            for i in range(n):
-                term = out[i * C : (i + 1) * C]
-                gsc[lo + i, :, at] = gsc[lo + i, :, at] + term if beyond else term
-
-    def each_row(fn):
-        for p in range(NP):
-
-            def run(i, carry, p=p):
-                fn(p, pl.ds(pl.multiple_of(i * STEP, STEP), STEP))
-                return carry
-
-            lax.fori_loop(0, C // STEP, run, 0)
+        tiles = [buf[near_slot(p, j)].reshape(n * C, S) for j in range(first, last)]
+        out = dot(jnp.concatenate(tiles, axis=1), oh[p, pl.ds(first * S, (last - first) * S), :])
+        at = pl.ds(p * ROWS, ROWS)
+        for i in range(n):
+            term = out[i * C : (i + 1) * C]
+            gsc[lo + i, :, at] = term if first == 0 else gsc[lo + i, :, at] + term
+
+    def each_row(p, fn):
+        def run(i, carry):
+            fn(p, pl.ds(pl.multiple_of(i * STEP, STEP), STEP))
+            return carry
+
+        lax.fori_loop(0, C // STEP, run, 0)
 
     def angle(f, p, k):
         return ang[f, pl.ds(k * NP + p, 1), :]
@@ -413,36 +414,12 @@
 
     third = 1.0 / NE
 
-    def mix(lo, hi, w):
-        terms = jnp.concatenate([(acc[b] * third).astype(BF16) for b in range(lo, hi)], axis=1)
+    def mix(p, lo, hi, w):
+        at = own_columns(p)
+        terms = jnp.concatenate([(acc[b, :, at] * third).astype(BF16) for b in range(lo, hi)], axis=1)
         out = dot(w_turned[pl.ds(w * C, C), :], terms)
         for b in range(lo, hi):
-            acc[b] = out[:, (b - lo) * NP * S : (b - lo + 1) * NP * S]
-
-    halo.near(0)
-    gather(ext, 0, 0, False)
-    halo.corners(0)
-    halo.near(1)
-    gather(ext, 1, 4, False)
-    halo.near(2)
-    gather(ext, 2, 7, False)
-    halo.corners(1)
-    halo.rest(0)
-    gather(ext, 0, 0, True)
-    each_row(message_sv)
-    mix(1, 4, 2)
-    halo.corners(2)
-    halo.rest(1)
-    gather(ext, 1, 4, True)
-    each_row(message_t(4, 7))
-    halo.rest(2)
-    gather(ext, 2, 7, True)
-    each_row(message_t(7, 9))
-
-    out = dot(w_turned[pl.ds(0, 2 * C), :], (acc[0] * third).astype(BF16))
-    pre = out[0:C]
-    acc[0] = pre * jax.nn.sigmoid(pre)
-    gate[...] = jax.nn.sigmoid(out[C : 2 * C])
+            acc[b, :, at] = out[:, (b - lo) * S : (b - lo + 1) * S]
 
     def update_sv(p, r):
         at = own_columns(p)
@@ -452,22 +429,61 @@
             step = g * acc[b, r, at] if b > 0 else acc[0, r, at]
             block(ext2, b, 0, p)[r, :] = (old + step).astype(BF16)
 
-    each_row(update_sv)
     halo2 = Halo(ext2, f2_send, f2_recv, device, low_wrap, high_wrap)
-    for g in range(len(GROUPS2)):
-        halo2.own(g)
-
-    mix(4, 9, 3)
-    for p in range(NP):
+
+    def finish(p):
+        at = own_columns(p)
+        out = dot(w_turned[pl.ds(0, 2 * C), :], (acc[0, :, at] * third).astype(BF16))
+        pre = out[0:C]
+        acc[0, :, at] = pre * jax.nn.sigmoid(pre)
+        gate[:, at] = jax.nn.sigmoid(out[C : 2 * C])
+        each_row(p, update_sv)
+        halo2.along_x(p, 0)
+        halo2.along_y(p, 0)
+
+    def finish_tensors(p):
+        mix(p, 4, 9, 3)
+        at = own_columns(p)
         for b in range(BLOCKS):
             if b < READ_BLOCKS:
                 new = block(ext2, b, 0, p)[...].astype(F32)
             else:
-                at = own_columns(p)
                 new = block(ext, b, 0, p)[...].astype(F32) + gate[:, at] * acc[b, :, at]
             mix_out[p, 0, :, pl.ds(b * C, C)] = jnp.transpose(new).astype(BF16)
-    write = pltpu.make_async_copy(mix_out, mixed, out_sem)
-    write.start()
+
+    starts = [lo for lo, _ in GROUPS]
+    for g in range(3):
+        halo.near(0, g)
+        halo.near(1, g)
+        gather(ext, g, starts[g], 0, 0, 6)
+        halo.corners(1, g)
+    for g in range(3):
+        gather(ext, g, starts[g], 1, 0, 6)
+    halo.rest(1, 0)
+    gather(ext, 0, starts[0], 0, 6, 9)
+    each_row(0, message_sv)
+    mix(0, 1, 4, 2)
+    halo.rest(1, 1)
+    gather(ext, 1, starts[1], 0, 6, 9)
+    each_row(0, message_t(4, 7))
+    halo.rest(1, 2)
+    gather(ext, 2, starts[2], 0, 6, 9)
+    each_row(0, message_t(7, 9))
+    finish(0)
+    halo.corners(0, 0)
+    halo.corners(0, 1)
+    halo.rest(0, 0)
+    gather(ext, 0, starts[0], 1, 6, 9)
+    each_row(1, message_sv)
+    mix(1, 1, 4, 2)
+    halo.corners(0, 2)
+    halo.rest(0, 1)
+    gather(ext, 1, starts[1], 1, 6, 9)
+    each_row(1, message_t(4, 7))
+    halo.rest(0, 2)
+    gather(ext, 2, starts[2], 1, 6, 9)
+    each_row(1, message_t(7, 9))
+    finish(1)
 
     def near_side(p, r):
         own = [block(ext2, b, 0, p)[r, :].astype(F32) for b in range(READ_BLOCKS)]
@@ -482,18 +498,23 @@
             for m in range(3):
                 side[3 + m, r, e] = q1 * own[1 + m]
 
-    halo2.near(0)
-    gather(ext2, 0, 0, False)
-    halo2.corners(0)
-    each_row(near_side)
-    halo2.near(1)
-    gather(ext2, 1, 2, False)
-    halo2.corners(1)
+    halo2.corners(0, 0)
+    halo2.near(0, 0)
+    gather(ext2, 0, 0, 0, 0, 3)
+    for p in range(NP):
+        each_row(p, near_side)
+        finish_tensors(p)
+    write = pltpu.make_async_copy(mix_out, mixed, out_sem)
+    write.start()
+    halo2.corners(1, 0)
+    halo2.near(1, 0)
+    gather(ext2, 0, 0, 0, 3, 6)
+    gather(ext2, 0, 0, 1, 0, 6)
     halo.sent(range(len(GROUPS)))
-    halo2.rest(0)
-    gather(ext2, 0, 0, True)
-    halo2.rest(1)
-    gather(ext2, 1, 2, True)
+    halo2.rest(0, 0)
+    gather(ext2, 0, 0, 1, 6, 9)
+    halo2.rest(1, 0)
+    gather(ext2, 0, 0, 0, 6, 9)
 
     sums[...] = jnp.zeros_like(sums)
     for p in range(NP):
@@ -538,19 +559,20 @@
             jnp.concatenate([first, second, third_part, jnp.zeros_like(first)], 0).astype(BF16)
         )
 
-    def scatter(lo, hi):
+    def scatter(*spans):
         seen = {}
         for p in range(NP):
-            out = dot(parts[p], oh[p, pl.ds(lo * S, (hi - lo) * S), :], (1, 1))
-            out = (out[0:8] + out[8:16]) + out[16:24]
-            for j in range(lo, hi):
-                term = out[:, (j - lo) * S : (j - lo + 1) * S]
-                at = near_slot(p, j)
-                seen[at] = seen[at] - term if at in seen else -term
+            for lo, hi in spans:
+                out = dot(parts[p], oh[p, pl.ds(lo * S, (hi - lo) * S), :], (1, 1))
+                out = (out[0:8] + out[8:16]) + out[16:24]
+                for j in range(lo, hi):
+                    term = out[:, (j - lo) * S : (j - lo + 1) * S]
+                    at = near_slot(p, j)
+                    seen[at] = seen[at] - term if at in seen else -term
         for at, value in seen.items():
             extf[at] = value
 
-    scatter(2, 9)
+    scatter((0, 2), (4, 9))
     force_copies = []
     for n, (dx, dy) in enumerate(DIRECTIONS):
         if dx == 0:
@@ -570,7 +592,7 @@
         copy.start()
         force_copies.append(copy)
 
-    scatter(0, 2)
+    scatter((2, 4))
     total = []
     for p in range(NP):
         mine = extf[0, p]

time: 59.9 us -> 59.7 us (level)
  the two profiles are of different devices: /device:TPU:2 before, /device:TPU:1 now
where the time goes in v2:
time: 59.7 us; the launch traced here: 59.6 us
  Pallas kernels  56.4 us (94%)
  local copies, waits for them, and re-layouts  2.51 us (4%)
  between operations  0.65 us (1%)
    pallas_call x1, Pallas kernels, body(): pl.pallas_call(run_all, out_shape=(jax.ShapeDtypeStruct((NP, 1, S, BLOCKS...  56.4 us
    unnamed x4, local copies, waits for them, and re-layouts  2.51 us

profile of v2, /device:TPU:1, one launch (start us, length us, event | category | flops | bytes accessed | tf_op | source)
XLA Modules:
  0.0 59.6 jit_solution(14403394469019677753)
XLA Ops:
  0.6 56.4 %shard_map.113 = (bf16[2,1,128,1152]{3,2,1,0:T(8,128)(2,1)}, f32[2,3,1,128]{3,2,1,0:T(1,128)}) custom-call(bf16[2,1,128,1152]{3,2,1,0:T(8,128)(2,1)} %refs_0_.1, f32[2,3,1,128]{3,2,1,0:T(1,128)} %bitcast.3, s32[3,2,1,128]{3,2,1,0:T(1,128)} %refs_2_.1, s32[3,2,1,128]{3,2,1,0:T(1,128)} %refs_3_.1, f32[8,896]{1,0:T(8,128)} %refs_4_.1, f32[8,256]{1,0:T(8,128)} %refs_5_.1, ...), custom_call_target="tpu_custom_call" | custom-call | flops 4000000000 | bytes 2000000 | tf_op jit(solution)/shard_map/pallas_call | solution.py:631
  57.1 0.0 copy-start
  57.1 1.9 %copy.14 = bf16[2,1,128,1152]{3,2,1,0:T(8,128)(2,1)} copy(bf16[2,1,128,1152]{3,2,1,0:T(8,128)(2,1)} %get-tuple-element.8) | data formatting | bytes 1179648
  59.0 0.0 copy-done
  59.0 0.6 copy.15
Async XLA Ops:
  57.1 1.9 %copy-start = (f32[2,3,1,128]{3,2,1,0:T(1,128)S(1)}, f32[2,3,1,128]{3,2,1,0:T(1,128)}, u32[]{:S(2)}) copy-start(f32[2,3,1,128]{3,2,1,0:T(1,128)} %get-tuple-element.5) | copy-start | bytes 9220

commit v3 on v1

--- a/solution.py
+++ b/solution.py
@@ -159,7 +159,6 @@
     posx,
     oh,
     coef,
-    qcoef,
     wide,
     w_turned,
     zf,
@@ -173,6 +172,7 @@
     raw,
     mix_out,
     side,
+    by_pillar,
     sums,
     grad,
     extf,
@@ -221,10 +221,15 @@
             posx[0, p, pl.ds(m, 1), :] = pos[p, m]
 
     def turn(g):
-        for c in range(*GROUPS[g]):
+        lo, hi = GROUPS[g]
+
+        def run(i, carry):
             for p in range(NP):
-                tile = raw[p, 0, :, pl.ds(c * C, C)].astype(F32)
-                block(ext, c, 0, p)[...] = jnp.transpose(tile).astype(BF16)
+                tile = raw[p, 0, :, pl.ds(pl.multiple_of((lo + i) * C, C), C)].astype(F32)
+                ext[g][0, p, i] = jnp.transpose(tile).astype(BF16)
+            return carry
+
+        lax.fori_loop(0, hi - lo, run, 0)
 
     feat_load.wait()
     turn(0)
@@ -257,22 +262,39 @@
 
     atom = lax.broadcasted_iota(jnp.int32, (S, ROWS), 0).astype(F32)
     edges[...] = jnp.zeros_like(edges)
+    places = []
     for p in range(NP):
         rows = [dst[k, p].astype(F32) for k in range(NE)]
         for k in range(NE):
             edges[0, pl.ds(k * NP + p, 1), :] = rows[k]
             edges[1, pl.ds(k * NP + p, 1), :] = shift[k, p].astype(F32)
-        place = jnp.concatenate(rows, axis=1) - atom
-        for j in range(9):
-            x, y = near_pillar(p, j)
-            hit = place == float((3 * x + y) * S)
-            oh[p, pl.ds(j * S, S), :] = jnp.where(hit, 1.0, 0.0).astype(BF16)
-
-    for f in range(9):
-        w = wr[:, pl.ds(f * C, C)] if f < 7 else wq[:, pl.ds((f - 7) * C, C)]
+        places.append(jnp.concatenate(rows, axis=1) - atom)
+
+    def pick(y, carry):
+        column = jnp.where(y == 0, 1, jnp.where(y == 1, 0, 2))
+        for p in range(NP):
+            for at, x in ((2 * y, 1), (2 * y + 1, 2), (6 + y, 3 * p)):
+                hit = places[p] == ((3 * x + column) * S).astype(F32)
+                rows = pl.ds(pl.multiple_of(at * S, S), S)
+                oh[p, rows, :] = jnp.where(hit, 1.0, 0.0).astype(BF16)
+        return carry
+
+    lax.fori_loop(0, 3, pick, 0)
+
+    def turned(w):
         high, low = split(w)
         rows = jnp.concatenate([high, low, high, jnp.zeros_like(w)], axis=0)
-        wide[pl.ds(f * C, C), :] = jnp.transpose(rows).astype(BF16)
+        return jnp.transpose(rows).astype(BF16)
+
+    def widen(f, carry):
+        wide[f] = turned(wr[:, pl.ds(pl.multiple_of(f * C, C), C)])
+        return carry
+
+    lax.fori_loop(0, 7, widen, 0)
+    wide[8] = turned(wq[:, pl.ds(0, C)])
+    last = turned(wq[:, pl.ds(C, C)])
+    wide[7] = last
+    wide[9] = last
     for i, w in enumerate((w_scalar, w_gate, w_vector, w_tensor)):
         w_turned[pl.ds(i * C, C), :] = jnp.transpose(w[...].astype(F32)).astype(BF16)
 
@@ -306,7 +328,10 @@
     rho = jnp.sqrt(disp_x * disp_x + disp_y * disp_y + disp_z * disp_z + SOFTENING)
     inverse = 1.0 / rho
     u_x, u_y, u_z = disp_x * inverse, disp_y * inverse, disp_z * inverse
-    geo[...] = inverse
+    geo[0] = u_x
+    geo[1] = u_y
+    geo[2] = u_z
+    geo[3] = inverse
     length_sq = u_x * u_x + u_y * u_y + u_z * u_z
     angular = (
         u_x,
@@ -319,7 +344,9 @@
         0.5 * ROOT_THREE * (u_x * u_x - u_y * u_y),
     )
     for f in range(8):
-        ang[f] = angular[f]
+        for k in range(NE):
+            for p in range(NP):
+                ang[p, f, pl.ds(k, 1), :] = angular[f][k * NP + p : k * NP + p + 1]
     zf[...] = jnp.zeros_like(zf)
     for b in range(NB):
         off = (rho - (0.5 + SPACING * b)) / SPACING
@@ -331,93 +358,101 @@
             zf[32 * i + 8 + b] = high
             zf[32 * i + 16 + b] = low
 
-    def columns(p, k):
-        return pl.ds((p * NE + k) * S, S)
+    def columns(k):
+        return pl.ds(k * S, S)
 
     for p in range(NP):
         values = jnp.concatenate([zf[:, k * NP + p, :] for k in range(NE)], axis=1).astype(BF16)
-        at = pl.ds(p * ROWS, ROWS)
-        out = dot(wide[pl.ds(0, 7 * C), :], values[0:32])
-        for f in range(7):
-            coef[f, :, at] = out[f * C : (f + 1) * C]
-        qcoef[0, :, at] = dot(wide[pl.ds(8 * C, C), :], values[0:32])
-        out = dot(wide[pl.ds(7 * C, 2 * C), :], values[32:64])
-        for f in range(2):
-            qcoef[1 + f, :, at] = out[f * C : (f + 1) * C]
+        basis_rows, slope_rows = values[0:32], values[32:64]
+
+        def expand(f, carry, p=p, rows=basis_rows):
+            coef[f, p] = dot(wide[f], rows)
+            return carry
+
+        lax.fori_loop(0, 8, expand, 0)
+        for f in (8, 9):
+            coef[f, p] = dot(wide[f], slope_rows)
 
     def gather(bufs, g, lo, beyond):
         buf = bufs[g]
         n = buf.shape[2]
-        for p in range(NP):
-            around = range(6, 9) if beyond else range(6)
-            tiles = [buf[near_slot(p, j)].reshape(n * C, S) for j in around]
-            picks = oh[p, pl.ds(around[0] * S, len(around) * S), :]
+
+        def run(p, carry):
+            if beyond:
+                tiles = [buf[y, 3 - p].reshape(n * C, S) for y in range(3)]
+                picks = oh[p, pl.ds(6 * S, 3 * S), :]
+            else:
+                tiles = [buf[y, slot].reshape(n * C, S) for y in range(3) for slot in range(2)]
+                picks = oh[p, pl.ds(0, 6 * S), :]
             out = dot(jnp.concatenate(tiles, axis=1), picks)
-            at = pl.ds(p * ROWS, ROWS)
             for i in range(n):
                 term = out[i * C : (i + 1) * C]
-                gsc[lo + i, :, at] = gsc[lo + i, :, at] + term if beyond else term
+                gsc[lo + i, p] = gsc[lo + i, p] + term if beyond else term
+            return carry
+
+        lax.fori_loop(0, NP, run, 0)
 
     def each_row(fn):
-        for p in range(NP):
-
-            def run(i, carry, p=p):
-                fn(p, pl.ds(pl.multiple_of(i * STEP, STEP), STEP))
-                return carry
-
-            lax.fori_loop(0, C // STEP, run, 0)
+        steps = C // STEP
+
+        def run(i, carry):
+            p = i // steps
+            fn(p, pl.ds(pl.multiple_of((i - p * steps) * STEP, STEP), STEP))
+            return carry
+
+        lax.fori_loop(0, NP * steps, run, 0)
 
     def angle(f, p, k):
-        return ang[f, pl.ds(k * NP + p, 1), :]
-
-    def own_columns(p):
-        return pl.ds(p * S, S)
+        return ang[p, f, pl.ds(k, 1), :]
 
     def message_sv(p, r):
         total = [jnp.zeros((STEP, S), F32) for _ in range(BLOCKS)]
         for k in range(NE):
-            e = columns(p, k)
-            s = gsc[0, r, e]
-            v = [gsc[1 + m, r, e] for m in range(3)]
+            e = columns(k)
+            s = gsc[0, p, r, e]
+            v = [gsc[1 + m, p, r, e] for m in range(3)]
             u = [angle(m, p, k) for m in range(3)]
             along = u[0] * v[0] + u[1] * v[1] + u[2] * v[2]
-            total[0] = total[0] + coef[0, r, e] * s + coef[1, r, e] * along
-            r3s = coef[3, r, e] * s
-            r4 = coef[4, r, e]
+            total[0] = total[0] + coef[0, p, r, e] * s + coef[1, p, r, e] * along
+            r3s = coef[3, p, r, e] * s
+            r4 = coef[4, p, r, e]
             for m in range(3):
                 total[1 + m] = total[1 + m] + r3s * u[m] + r4 * v[m]
-            r5s = coef[5, r, e] * s
+            r5s = coef[5, p, r, e] * s
             for n in range(5):
                 total[4 + n] = total[4 + n] + r5s * angle(3 + n, p, k)
         for b in range(BLOCKS):
-            acc[b, r, own_columns(p)] = total[b]
+            acc[b, p, r, :] = total[b]
 
     def message_t(lo, hi):
         def fn(p, r):
-            at = own_columns(p)
-            total = [acc[b, r, at] for b in (0, *range(lo, hi))]
+            total = [acc[b, p, r, :] for b in (0, *range(lo, hi))]
             for k in range(NE):
-                e = columns(p, k)
+                e = columns(k)
                 along = None
-                r6 = coef[6, r, e]
+                r6 = coef[6, p, r, e]
                 for n in range(lo, hi):
-                    t = gsc[n, r, e]
+                    t = gsc[n, p, r, e]
                     term = angle(n - 1, p, k) * t
                     along = term if along is None else along + term
                     total[1 + n - lo] = total[1 + n - lo] + r6 * t
-                total[0] = total[0] + coef[2, r, e] * along
+                total[0] = total[0] + coef[2, p, r, e] * along
             for i, b in enumerate((0, *range(lo, hi))):
-                acc[b, r, at] = total[i]
+                acc[b, p, r, :] = total[i]
 
         return fn
 
     third = 1.0 / NE
 
     def mix(lo, hi, w):
-        terms = jnp.concatenate([(acc[b] * third).astype(BF16) for b in range(lo, hi)], axis=1)
-        out = dot(w_turned[pl.ds(w * C, C), :], terms)
-        for b in range(lo, hi):
-            acc[b] = out[:, (b - lo) * NP * S : (b - lo + 1) * NP * S]
+        def run(p, carry):
+            terms = [(acc[b, p] * third).astype(BF16) for b in range(lo, hi)]
+            out = dot(w_turned[pl.ds(w * C, C), :], jnp.concatenate(terms, axis=1))
+            for b in range(lo, hi):
+                acc[b, p] = out[:, (b - lo) * S : (b - lo + 1) * S]
+            return carry
+
+        lax.fori_loop(0, NP, run, 0)
 
     halo.near(0)
     gather(ext, 0, 0, False)
@@ -439,18 +474,21 @@
     gather(ext, 2, 7, True)
     each_row(message_t(7, 9))
 
-    out = dot(w_turned[pl.ds(0, 2 * C), :], (acc[0] * third).astype(BF16))
-    pre = out[0:C]
-    acc[0] = pre * jax.nn.sigmoid(pre)
-    gate[...] = jax.nn.sigmoid(out[C : 2 * C])
+    def scalars(p, carry):
+        out = dot(w_turned[pl.ds(0, 2 * C), :], (acc[0, p] * third).astype(BF16))
+        pre = out[0:C]
+        acc[0, p] = pre * jax.nn.sigmoid(pre)
+        gate[p] = jax.nn.sigmoid(out[C : 2 * C])
+        return carry
+
+    lax.fori_loop(0, NP, scalars, 0)
 
     def update_sv(p, r):
-        at = own_columns(p)
-        g = gate[r, at]
+        g = gate[p, r, :]
         for b in range(READ_BLOCKS):
-            old = block(ext, b, 0, p)[r, :].astype(F32)
-            step = g * acc[b, r, at] if b > 0 else acc[0, r, at]
-            block(ext2, b, 0, p)[r, :] = (old + step).astype(BF16)
+            old = ext[0][0, p, b, r, :].astype(F32)
+            step = g * acc[b, p, r, :] if b > 0 else acc[0, p, r, :]
+            ext2[b // 2][0, p, b % 2, r, :] = (old + step).astype(BF16)
 
     each_row(update_sv)
     halo2 = Halo(ext2, f2_send, f2_recv, device, low_wrap, high_wrap)
@@ -458,29 +496,36 @@
         halo2.own(g)
 
     mix(4, 9, 3)
-    for p in range(NP):
-        for b in range(BLOCKS):
-            if b < READ_BLOCKS:
-                new = block(ext2, b, 0, p)[...].astype(F32)
-            else:
-                at = own_columns(p)
-                new = block(ext, b, 0, p)[...].astype(F32) + gate[:, at] * acc[b, :, at]
-            mix_out[p, 0, :, pl.ds(b * C, C)] = jnp.transpose(new).astype(BF16)
+
+    def results(lo, hi, value):
+        def run(i, carry):
+            for p in range(NP):
+                at = pl.ds(pl.multiple_of((lo + i) * C, C), C)
+                mix_out[p, 0, :, at] = jnp.transpose(value(p, i)).astype(BF16)
+            return carry
+
+        lax.fori_loop(0, hi - lo, run, 0)
+
+    for g, (lo, hi) in enumerate(GROUPS2):
+        results(lo, hi, lambda p, i: ext2[g][0, p, i].astype(F32))
+    for g, (lo, hi) in enumerate(GROUPS):
+        if g > 0:
+            results(lo, hi, lambda p, i: ext[g][0, p, i].astype(F32) + gate[p] * acc[lo + i, p])
     write = pltpu.make_async_copy(mix_out, mixed, out_sem)
     write.start()
 
     def near_side(p, r):
-        own = [block(ext2, b, 0, p)[r, :].astype(F32) for b in range(READ_BLOCKS)]
+        own = [ext2[b // 2][0, p, b % 2, r, :].astype(F32) for b in range(READ_BLOCKS)]
         for k in range(NE):
-            e = columns(p, k)
+            e = columns(k)
             u = [angle(m, p, k) for m in range(3)]
             along = u[0] * own[1] + u[1] * own[2] + u[2] * own[3]
-            q1 = qcoef[0, r, e]
-            side[0, r, e] = qcoef[1, r, e] * own[0]
-            side[1, r, e] = qcoef[2, r, e] * along
-            side[2, r, e] = q1 * along
+            q1 = coef[7, p, r, e]
+            side[0, p, r, e] = coef[8, p, r, e] * own[0]
+            side[1, p, r, e] = coef[9, p, r, e] * along
+            side[2, p, r, e] = q1 * along
             for m in range(3):
-                side[3 + m, r, e] = q1 * own[1 + m]
+                side[3 + m, p, r, e] = q1 * own[1 + m]
 
     halo2.near(0)
     gather(ext2, 0, 0, False)
@@ -495,21 +540,19 @@
     halo2.rest(1)
     gather(ext2, 1, 2, True)
 
-    sums[...] = jnp.zeros_like(sums)
-    for p in range(NP):
-
-        def pair(i, carry, p=p):
+    def pairs(p, outer):
+        def pair(i, carry):
             r = pl.ds(pl.multiple_of(i * STEP, STEP), STEP)
             carry = list(carry)
             for k in range(NE):
-                e = columns(p, k)
-                far = [gsc[b, r, e] for b in range(READ_BLOCKS)]
+                e = columns(k)
+                far = [gsc[b, p, r, e] for b in range(READ_BLOCKS)]
                 u = [angle(m, p, k) for m in range(3)]
                 along = u[0] * far[1] + u[1] * far[2] + u[2] * far[3]
-                carry[4 * k] = carry[4 * k] + side[0, r, e] * far[0] + side[1, r, e] * along
-                own_q = side[2, r, e]
+                carry[4 * k] = carry[4 * k] + side[0, p, r, e] * far[0] + side[1, p, r, e] * along
+                own_q = side[2, p, r, e]
                 for m in range(3):
-                    term = side[3 + m, r, e] * along + own_q * far[1 + m]
+                    term = side[3 + m, p, r, e] * along + own_q * far[1 + m]
                     carry[4 * k + 1 + m] = carry[4 * k + 1 + m] + term
             return tuple(carry)
 
@@ -518,11 +561,18 @@
         for k in range(NE):
             for q in range(4):
                 row = jnp.sum(totals[4 * k + q], axis=0, keepdims=True)
-                sums[q, pl.ds(k * NP + p, 1), :] = row
+                by_pillar[p, pl.ds(4 * k + q, 1), :] = row
+        return outer
+
+    lax.fori_loop(0, NP, pairs, 0)
+    sums[...] = jnp.zeros_like(sums)
+    for p in range(NP):
+        for k in range(NE):
+            for q in range(4):
+                sums[q, pl.ds(k * NP + p, 1), :] = by_pillar[p, pl.ds(4 * k + q, 1), :]
 
     t_rho, g_x, g_y, g_z = (sums[q] for q in range(4))
-    u_x, u_y, u_z = ang[0], ang[1], ang[2]
-    inverse = geo[...]
+    u_x, u_y, u_z, inverse = (geo[i] for i in range(4))
     radial_part = t_rho - (u_x * g_x + u_y * g_y + u_z * g_z) * inverse
     grad[...] = jnp.zeros_like(grad)
     grad[0] = radial_part * u_x + g_x * inverse
@@ -619,21 +669,21 @@
                 *[pltpu.VMEM((3, 4, hi - lo, S, C), BF16) for lo, hi in GROUPS + GROUPS2],
                 pltpu.VMEM((3, 4, 8, S), F32),
                 pltpu.VMEM((NP, NEAR, ROWS), BF16),
-                pltpu.VMEM((7, C, NP * ROWS), F32),
-                pltpu.VMEM((3, C, NP * ROWS), F32),
-                pltpu.VMEM((9 * C, 32), BF16),
+                pltpu.VMEM((10, NP, C, ROWS), F32),
+                pltpu.VMEM((10, C, 32), BF16),
                 pltpu.VMEM((4 * C, C), BF16),
                 pltpu.VMEM((64, 8, S), F32),
+                pltpu.VMEM((NP, 8, NE, S), F32),
                 pltpu.VMEM((8, 8, S), F32),
-                pltpu.VMEM((8, 8, S), F32),
-                pltpu.VMEM((8, S), F32),
+                pltpu.VMEM((4, 8, S), F32),
                 pltpu.VMEM((2, 8, S), F32),
-                pltpu.VMEM((BLOCKS, C, NP * S), F32),
-                pltpu.VMEM((C, NP * S), F32),
-                pltpu.VMEM((BLOCKS, C, NP * ROWS), F32),
+                pltpu.VMEM((BLOCKS, NP, C, S), F32),
+                pltpu.VMEM((NP, C, S), F32),
+                pltpu.VMEM((BLOCKS, NP, C, ROWS), F32),
                 pltpu.VMEM((NP, 1, S, BLOCKS * C), BF16),
                 pltpu.VMEM((NP, 1, S, BLOCKS * C), BF16),
-                pltpu.VMEM((6, C, NP * ROWS), F32),
+                pltpu.VMEM((6, NP, C, ROWS), F32),
+                pltpu.VMEM((NP, 4 * NE, S), F32),
                 pltpu.VMEM((4, 8, S), F32),
                 pltpu.VMEM((8, 8, S), F32),
                 pltpu.VMEM((3, 4, 8, S), F32),

time: 59.9 us -> 60.6 us (1.012)
  Pallas kernels: 55.8 us -> 56.8 us
    pallas_call x1, Pallas kernels: 55.8 us -> 56.8 us  [body(): pl.pallas_call(run_all, out_shape=(jax.ShapeDtypeStruct((NP, 1, S, BLOCKS...]
where the time goes in v3:
time: 60.6 us; the launch traced here: 59.9 us
  Pallas kernels  56.8 us (94%)
  local copies, waits for them, and re-layouts  2.51 us (4%)
  between operations  0.65 us (1%)
    pallas_call x1, Pallas kernels, body(): pl.pallas_call(run_all, out_shape=(jax.ShapeDtypeStruct((NP, 1, S, BLOCKS...  56.8 us
    unnamed x4, local copies, waits for them, and re-layouts  2.51 us

profile of v3, /device:TPU:2, one launch (start us, length us, event | category | flops | bytes accessed | tf_op | source)
XLA Modules:
  0.0 59.9 jit_solution(1426888120245970259)
XLA Ops:
  0.6 56.8 %shard_map.113 = (bf16[2,1,128,1152]{3,2,1,0:T(8,128)(2,1)}, f32[2,3,1,128]{3,2,1,0:T(1,128)}) custom-call(bf16[2,1,128,1152]{3,2,1,0:T(8,128)(2,1)} %refs_0_.1, f32[2,3,1,128]{3,2,1,0:T(1,128)} %bitcast.3, s32[3,2,1,128]{3,2,1,0:T(1,128)} %refs_2_.1, s32[3,2,1,128]{3,2,1,0:T(1,128)} %refs_3_.1, f32[8,896]{1,0:T(8,128)} %refs_4_.1, f32[8,256]{1,0:T(8,128)} %refs_5_.1, ...), custom_call_target="tpu_custom_call" | custom-call | flops 4000000000 | bytes 2000000 | tf_op jit(solution)/shard_map/pallas_call | solution.py:659
  57.4 0.0 copy-start
  57.4 1.9 %copy.14 = bf16[2,1,128,1152]{3,2,1,0:T(8,128)(2,1)} copy(bf16[2,1,128,1152]{3,2,1,0:T(8,128)(2,1)} %get-tuple-element.8) | data formatting | bytes 1179648
  59.3 0.0 copy-done
  59.3 0.6 copy.15
Async XLA Ops:
  57.4 1.9 %copy-start = (f32[2,3,1,128]{3,2,1,0:T(1,128)S(1)}, f32[2,3,1,128]{3,2,1,0:T(1,128)}, u32[]{:S(2)}) copy-start(f32[2,3,1,128]{3,2,1,0:T(1,128)} %get-tuple-element.5) | copy-start | bytes 9220

commit v4 on v3

--- a/solution.py
+++ b/solution.py
@@ -20,12 +20,28 @@
 NP = 2
 BLOCKS = 9
 READ_BLOCKS = 4
-KP = NE * NP
 ROWS = NE * S
 NEAR = 9 * S
 STEP = 16
-GROUPS = ((0, 4), (4, 7), (7, 9))
-GROUPS2 = ((0, 2), (2, 4))
+GROUPS = ((0, 4), (4, 7), (7, 8), (8, 9))
+GROUPS2 = ((0, 2), (2, 3), (3, 4))
+PILLARS = {
+    0: (1, 0),
+    1: (1, 1),
+    2: (2, 0),
+    3: (2, 1),
+    4: (0, 2),
+    5: (0, 3),
+    8: (0, 0),
+    9: (0, 1),
+    10: (1, 2),
+    11: (1, 3),
+    12: (2, 2),
+    13: (2, 3),
+}
+OWN = 8
+COUNT = 14
+EDGE_ROWS = 48
 DIRECTIONS = tuple((dx, dy) for dx in (-1, 0, 1) for dy in (-1, 0, 1) if (dx, dy) != (0, 0))
 
 
@@ -154,29 +170,32 @@
     ext0,
     ext1,
     ext2,
+    ext3,
     mix0,
     mix1,
+    mix2,
     posx,
     oh,
+    oh_own,
     coef,
+    readout,
     wide,
     w_turned,
     zf,
     ang,
     pj,
-    geo,
+    inverses,
+    target,
     edges,
     acc,
     gate,
     gsc,
+    ends,
     raw,
     mix_out,
     side,
-    by_pillar,
     sums,
     grad,
-    extf,
-    frecv,
     small_sem,
     load_sem,
     out_sem,
@@ -186,10 +205,8 @@
     f1_recv,
     f2_send,
     f2_recv,
-    fo_send,
-    fo_recv,
 ):
-    ext, ext2 = (ext0, ext1, ext2), (mix0, mix1)
+    ext, ext2 = (ext0, ext1, ext2, ext3), (mix0, mix1, mix2)
     gx = lax.axis_index("gx")
     yz = lax.axis_index("yz")
 
@@ -216,9 +233,12 @@
     for load in small_loads:
         load.wait()
     for p in range(NP):
-        posx[0, p] = jnp.zeros((8, S), F32)
+        posx[0, p] = jnp.zeros((16, S), F32)
         for m in range(3):
             posx[0, p, pl.ds(m, 1), :] = pos[p, m]
+        for k in range(NE):
+            posx[0, p, pl.ds(3 + k, 1), :] = dst[k, p].astype(F32)
+            posx[0, p, pl.ds(6 + k, 1), :] = shift[k, p].astype(F32)
 
     def turn(g):
         lo, hi = GROUPS[g]
@@ -261,13 +281,9 @@
         halo.own(g)
 
     atom = lax.broadcasted_iota(jnp.int32, (S, ROWS), 0).astype(F32)
-    edges[...] = jnp.zeros_like(edges)
     places = []
     for p in range(NP):
-        rows = [dst[k, p].astype(F32) for k in range(NE)]
-        for k in range(NE):
-            edges[0, pl.ds(k * NP + p, 1), :] = rows[k]
-            edges[1, pl.ds(k * NP + p, 1), :] = shift[k, p].astype(F32)
+        rows = [posx[0, p, pl.ds(3 + k, 1), :] for k in range(NE)]
         places.append(jnp.concatenate(rows, axis=1) - atom)
 
     def pick(y, carry):
@@ -300,19 +316,14 @@
 
     for copy in pos_copies:
         copy.wait_recv()
-    for p in range(NP):
-        places = jnp.concatenate([posx[near_slot(p, j)] for j in range(9)], axis=1)
-        first, rest = split(places)
-        second, third = split(rest)
-        parts = jnp.concatenate([first, second, third, jnp.zeros_like(first)], 0).astype(BF16)
-        found = dot(parts, oh[p])
-        far = (found[0:8] + found[8:16]) + found[16:24]
-        for k in range(NE):
-            pj[k * NP + p] = far[:, k * S : (k + 1) * S] - posx[0, p]
-
+    edges[...] = jnp.zeros_like(edges)
+    for q, (y, slot) in PILLARS.items():
+        at = pl.ds(NE * q, NE)
+        edges[0, at, :] = posx[y, slot, pl.ds(3, NE), :]
+        edges[1, at, :] = posx[y, slot, pl.ds(6, NE), :]
+        for i, value in ((2, slot % NP), (3, (1, 2, 3, 0)[slot]), (4, (1, 0, 2)[y])):
+            edges[i, at, :] = jnp.full((NE, S), value, F32)
     place = edges[0]
-    pj[pl.ds(KP, 8 - KP)] = jnp.zeros((8 - KP, 8, S), F32)
-    own_p = lax.rem(lax.broadcasted_iota(jnp.int32, (8, S), 0), NP).astype(F32)
     one = jnp.ones_like(place)
     nil = jnp.zeros_like(place)
 
@@ -322,16 +333,50 @@
     ext_x = at_least(place, 3 * S) + at_least(place, 6 * S) + at_least(place, 9 * S)
     left = place - ext_x * float(3 * S)
     ext_y = at_least(left, S) + at_least(left, 2 * S)
-    disp_x = pj[:, 0, :] + (ext_x - 1.0 - own_p)
-    disp_y = pj[:, 1, :] + (ext_y - 1.0)
+    step_x = ext_x - 1.0 - edges[2]
+    step_y = ext_y - 1.0
+    to_x = edges[3] + step_x - 1.0
+    mine = (edges[4] + step_y == 1.0) & (to_x >= 0.0) & (to_x <= 1.0)
+    target[...] = jnp.where(mine, to_x * S + (left - ext_y * S), -1.0)
+
+    atom = lax.broadcasted_iota(jnp.int32, (NP * S, ROWS), 0).astype(F32)
+
+    def own_pick(q, carry):
+        rows = [target[pl.ds(NE * q + k, 1), :] for k in range(NE)]
+        hit = jnp.concatenate(rows, axis=1) == atom
+        oh_own[:, pl.ds(pl.multiple_of(q * ROWS, ROWS), ROWS)] = jnp.where(hit, 1.0, 0.0).astype(BF16)
+        return carry
+
+    lax.fori_loop(0, 6, own_pick, 0)
+    lax.fori_loop(OWN, COUNT, own_pick, 0)
+
+    def in_parts(x):
+        first, rest = split(x)
+        second, third = split(rest)
+        return jnp.concatenate([first, second, third, jnp.zeros_like(first)], 0).astype(BF16)
+
+    def whole(x):
+        return (x[0:8] + x[8:16]) + x[16:24]
+
+    pj[...] = jnp.zeros_like(pj)
+    own_parts = in_parts(jnp.concatenate([posx[0, p, pl.ds(0, 8), :] for p in range(NP)], axis=1))
+    for q, (y, slot) in PILLARS.items():
+        if q in (OWN, OWN + 1):
+            near = [near_slot(slot, j) for j in range(9)]
+            parts = in_parts(jnp.concatenate([posx[b, a, pl.ds(0, 8), :] for b, a in near], axis=1))
+            far = whole(dot(parts, oh[slot]))
+        else:
+            far = whole(dot(own_parts, oh_own[:, pl.ds(q * ROWS, ROWS)]))
+        for k in range(NE):
+            pj[NE * q + k] = far[:, k * S : (k + 1) * S] - posx[y, slot, pl.ds(0, 8), :]
+
+    disp_x = pj[:, 0, :] + step_x
+    disp_y = pj[:, 1, :] + step_y
     disp_z = pj[:, 2, :] + edges[1]
     rho = jnp.sqrt(disp_x * disp_x + disp_y * disp_y + disp_z * disp_z + SOFTENING)
     inverse = 1.0 / rho
     u_x, u_y, u_z = disp_x * inverse, disp_y * inverse, disp_z * inverse
-    geo[0] = u_x
-    geo[1] = u_y
-    geo[2] = u_z
-    geo[3] = inverse
+    inverses[...] = inverse
     length_sq = u_x * u_x + u_y * u_y + u_z * u_z
     angular = (
         u_x,
@@ -344,9 +389,7 @@
         0.5 * ROOT_THREE * (u_x * u_x - u_y * u_y),
     )
     for f in range(8):
-        for k in range(NE):
-            for p in range(NP):
-                ang[p, f, pl.ds(k, 1), :] = angular[f][k * NP + p : k * NP + p + 1]
+        ang[f] = angular[f]
     zf[...] = jnp.zeros_like(zf)
     for b in range(NB):
         off = (rho - (0.5 + SPACING * b)) / SPACING
@@ -361,17 +404,19 @@
     def columns(k):
         return pl.ds(k * S, S)
 
-    for p in range(NP):
-        values = jnp.concatenate([zf[:, k * NP + p, :] for k in range(NE)], axis=1).astype(BF16)
+    for q in PILLARS:
+        values = jnp.concatenate([zf[:, NE * q + k, :] for k in range(NE)], axis=1).astype(BF16)
         basis_rows, slope_rows = values[0:32], values[32:64]
-
-        def expand(f, carry, p=p, rows=basis_rows):
-            coef[f, p] = dot(wide[f], rows)
-            return carry
-
-        lax.fori_loop(0, 8, expand, 0)
-        for f in (8, 9):
-            coef[f, p] = dot(wide[f], slope_rows)
+        if q in (OWN, OWN + 1):
+
+            def expand(f, carry, p=q - OWN, rows=basis_rows):
+                coef[f, p] = dot(wide[f], rows)
+                return carry
+
+            lax.fori_loop(0, 7, expand, 0)
+        readout[q, 0] = dot(wide[7], basis_rows)
+        readout[q, 1] = dot(wide[8], slope_rows)
+        readout[q, 2] = dot(wide[9], slope_rows)
 
     def gather(bufs, g, lo, beyond):
         buf = bufs[g]
@@ -402,8 +447,8 @@
 
         lax.fori_loop(0, NP * steps, run, 0)
 
-    def angle(f, p, k):
-        return ang[p, f, pl.ds(k, 1), :]
+    def angle(f, q, k):
+        return ang[f, pl.ds(NE * q + k, 1), :]
 
     def message_sv(p, r):
         total = [jnp.zeros((STEP, S), F32) for _ in range(BLOCKS)]
@@ -411,7 +456,7 @@
             e = columns(k)
             s = gsc[0, p, r, e]
             v = [gsc[1 + m, p, r, e] for m in range(3)]
-            u = [angle(m, p, k) for m in range(3)]
+            u = [angle(m, OWN + p, k) for m in range(3)]
             along = u[0] * v[0] + u[1] * v[1] + u[2] * v[2]
             total[0] = total[0] + coef[0, p, r, e] * s + coef[1, p, r, e] * along
             r3s = coef[3, p, r, e] * s
@@ -420,7 +465,7 @@
                 total[1 + m] = total[1 + m] + r3s * u[m] + r4 * v[m]
             r5s = coef[5, p, r, e] * s
             for n in range(5):
-                total[4 + n] = total[4 + n] + r5s * angle(3 + n, p, k)
+                total[4 + n] = total[4 + n] + r5s * angle(3 + n, OWN + p, k)
         for b in range(BLOCKS):
             acc[b, p, r, :] = total[b]
 
@@ -433,7 +478,7 @@
                 r6 = coef[6, p, r, e]
                 for n in range(lo, hi):
                     t = gsc[n, p, r, e]
-                    term = angle(n - 1, p, k) * t
+                    term = angle(n - 1, OWN + p, k) * t
                     along = term if along is None else along + term
                     total[1 + n - lo] = total[1 + n - lo] + r6 * t
                 total[0] = total[0] + coef[2, p, r, e] * along
@@ -457,10 +502,9 @@
     halo.near(0)
     gather(ext, 0, 0, False)
     halo.corners(0)
-    halo.near(1)
-    gather(ext, 1, 4, False)
-    halo.near(2)
-    gather(ext, 2, 7, False)
+    for g in range(1, len(GROUPS)):
+        halo.near(g)
+        gather(ext, g, GROUPS[g][0], False)
     halo.corners(1)
     halo.rest(0)
     gather(ext, 0, 0, True)
@@ -470,9 +514,13 @@
     halo.rest(1)
     gather(ext, 1, 4, True)
     each_row(message_t(4, 7))
+    halo.corners(3)
     halo.rest(2)
     gather(ext, 2, 7, True)
-    each_row(message_t(7, 9))
+    each_row(message_t(7, 8))
+    halo.rest(3)
+    gather(ext, 3, 8, True)
+    each_row(message_t(8, 9))
 
     def scalars(p, carry):
         out = dot(w_turned[pl.ds(0, 2 * C), :], (acc[0, p] * third).astype(BF16))
@@ -483,12 +531,16 @@
 
     lax.fori_loop(0, NP, scalars, 0)
 
+    def read_block(b, y, slot):
+        g = (0, 0, 1, 2)[b]
+        return ext2[g].at[y, slot, b - GROUPS2[g][0]]
+
     def update_sv(p, r):
         g = gate[p, r, :]
         for b in range(READ_BLOCKS):
             old = ext[0][0, p, b, r, :].astype(F32)
             step = g * acc[b, p, r, :] if b > 0 else acc[0, p, r, :]
-            ext2[b // 2][0, p, b % 2, r, :] = (old + step).astype(BF16)
+            read_block(b, 0, p)[r, :] = (old + step).astype(BF16)
 
     each_row(update_sv)
     halo2 = Halo(ext2, f2_send, f2_recv, device, low_wrap, high_wrap)
@@ -514,129 +566,129 @@
     write = pltpu.make_async_copy(mix_out, mixed, out_sem)
     write.start()
 
-    def near_side(p, r):
-        own = [ext2[b // 2][0, p, b % 2, r, :].astype(F32) for b in range(READ_BLOCKS)]
+    def near_side(q, r, end):
         for k in range(NE):
             e = columns(k)
-            u = [angle(m, p, k) for m in range(3)]
-            along = u[0] * own[1] + u[1] * own[2] + u[2] * own[3]
-            q1 = coef[7, p, r, e]
-            side[0, p, r, e] = coef[8, p, r, e] * own[0]
-            side[1, p, r, e] = coef[9, p, r, e] * along
-            side[2, p, r, e] = q1 * along
+            s, v = end(k)
+            u = [angle(m, q, k) for m in range(3)]
+            along = u[0] * v[0] + u[1] * v[1] + u[2] * v[2]
+            q1 = readout[q, 0, r, e]
+            side[q, 0, r, e] = readout[q, 1, r, e] * s
+            side[q, 1, r, e] = readout[q, 2, r, e] * along
+            side[q, 2, r, e] = q1 * along
             for m in range(3):
-                side[3 + m, p, r, e] = q1 * own[1 + m]
-
-    halo2.near(0)
-    gather(ext2, 0, 0, False)
+                side[q, 3 + m, r, e] = q1 * v[m]
+
+    def own_side(p, r):
+        own = [read_block(b, 0, p)[r, :].astype(F32) for b in range(READ_BLOCKS)]
+        near_side(OWN + p, r, lambda k: (own[0], own[1:]))
+
+    def ghost_sides(lo, hi):
+        def run(q, carry):
+            tiles = []
+            for p in range(NP):
+                parts = [ext2[g][0, p].reshape((b - a) * C, S) for g, (a, b) in enumerate(GROUPS2)]
+                tiles.append(jnp.concatenate(parts, axis=0))
+            picks = oh_own[:, pl.ds(pl.multiple_of(q * ROWS, ROWS), ROWS)]
+            ends[...] = dot(jnp.concatenate(tiles, axis=1), picks)
+
+            def rows(i, inner):
+                at = pl.multiple_of(i * STEP, STEP)
+
+                def end(k):
+                    far = [ends[pl.ds(b * C + at, STEP), columns(k)] for b in range(READ_BLOCKS)]
+                    return far[0], far[1:]
+
+                near_side(q, pl.ds(at, STEP), end)
+                return inner
+
+            lax.fori_loop(0, C // STEP, rows, 0)
+            return carry
+
+        lax.fori_loop(lo, hi, run, 0)
+
+    def pairs(lo, hi, far_rows):
+        def run(q, outer):
+            def pair(i, carry):
+                r = pl.ds(pl.multiple_of(i * STEP, STEP), STEP)
+                carry = list(carry)
+                get = far_rows(q, r)
+                for k in range(NE):
+                    e = columns(k)
+                    far = get(k)
+                    u = [angle(m, q, k) for m in range(3)]
+                    along = u[0] * far[1] + u[1] * far[2] + u[2] * far[3]
+                    carry[4 * k] = carry[4 * k] + side[q, 0, r, e] * far[0] + side[q, 1, r, e] * along
+                    own_q = side[q, 2, r, e]
+                    for m in range(3):
+                        term = side[q, 3 + m, r, e] * along + own_q * far[1 + m]
+                        carry[4 * k + 1 + m] = carry[4 * k + 1 + m] + term
+                return tuple(carry)
+
+            zero = jnp.zeros((STEP, S), F32)
+            totals = lax.fori_loop(0, C // STEP, pair, (zero,) * (4 * NE))
+            for k in range(NE):
+                for i in range(4):
+                    row = jnp.sum(totals[4 * k + i], axis=0, keepdims=True)
+                    sums[i, pl.ds(NE * q + k, 1), :] = row
+            return outer
+
+        lax.fori_loop(lo, hi, run, 0)
+
+    def own_far(q, r):
+        return lambda k: [gsc[b, q - OWN, r, columns(k)] for b in range(READ_BLOCKS)]
+
+    def ghost_far(place_of):
+        def rows(q, r):
+            y, slot = place_of(q)
+            far = [read_block(b, y, slot)[r, :].astype(F32) for b in range(READ_BLOCKS)]
+            return lambda k: far
+
+        return rows
+
+    def gradient(lo, hi):
+        rows = pl.ds(lo, hi - lo)
+        t_rho, g_x, g_y, g_z = (sums[i, rows, :] for i in range(4))
+        u_x, u_y, u_z, inverse = ang[0, rows, :], ang[1, rows, :], ang[2, rows, :], inverses[rows, :]
+        radial_part = t_rho - (u_x * g_x + u_y * g_y + u_z * g_z) * inverse
+        grad[0, rows, :] = radial_part * u_x + g_x * inverse
+        grad[1, rows, :] = radial_part * u_y + g_y * inverse
+        grad[2, rows, :] = radial_part * u_z + g_z * inverse
+        used = [NE * q + k for q in PILLARS for k in range(NE) if lo <= NE * q < hi]
+        parts = in_parts(jnp.concatenate([grad[:, row, :] for row in used], axis=1))
+        at = pl.ds(used[0] * S, len(used) * S)
+        return whole(dot(parts, oh_own[:, at], (1, 1)))
+
+    sums[...] = jnp.zeros_like(sums)
+    grad[...] = jnp.zeros_like(grad)
+    each_row(own_side)
+    for g, (lo, hi) in enumerate(GROUPS2):
+        halo2.near(g)
+        gather(ext2, g, lo, False)
     halo2.corners(0)
-    each_row(near_side)
-    halo2.near(1)
-    gather(ext2, 1, 2, False)
+    ghost_sides(0, 4)
+    pairs(0, 4, ghost_far(lambda q: (1 + q // 2, q % 2)))
     halo2.corners(1)
+    halo2.corners(2)
+    ghost_sides(4, 6)
+    pairs(4, 6, ghost_far(lambda q: (0, q - 2)))
+    ghost_sides(10, 14)
+    early = gradient(0, 24)
     halo.sent(range(len(GROUPS)))
-    halo2.rest(0)
-    gather(ext2, 0, 0, True)
-    halo2.rest(1)
-    gather(ext2, 1, 2, True)
-
-    def pairs(p, outer):
-        def pair(i, carry):
-            r = pl.ds(pl.multiple_of(i * STEP, STEP), STEP)
-            carry = list(carry)
-            for k in range(NE):
-                e = columns(k)
-                far = [gsc[b, p, r, e] for b in range(READ_BLOCKS)]
-                u = [angle(m, p, k) for m in range(3)]
-                along = u[0] * far[1] + u[1] * far[2] + u[2] * far[3]
-                carry[4 * k] = carry[4 * k] + side[0, p, r, e] * far[0] + side[1, p, r, e] * along
-                own_q = side[2, p, r, e]
-                for m in range(3):
-                    term = side[3 + m, p, r, e] * along + own_q * far[1 + m]
-                    carry[4 * k + 1 + m] = carry[4 * k + 1 + m] + term
-            return tuple(carry)
-
-        zero = jnp.zeros((STEP, S), F32)
-        totals = lax.fori_loop(0, C // STEP, pair, (zero,) * (4 * NE))
+    for g, (lo, hi) in enumerate(GROUPS2):
+        halo2.rest(g)
+        gather(ext2, g, lo, True)
+    pairs(OWN, OWN + 2, own_far)
+    pairs(10, 14, ghost_far(lambda q: (q // 2 - 4, 2 + q % 2)))
+    back = early + gradient(24, EDGE_ROWS)
+    for p in range(NP):
+        total = -back[:, p * S : (p + 1) * S]
         for k in range(NE):
-            for q in range(4):
-                row = jnp.sum(totals[4 * k + q], axis=0, keepdims=True)
-                by_pillar[p, pl.ds(4 * k + q, 1), :] = row
-        return outer
-
-    lax.fori_loop(0, NP, pairs, 0)
-    sums[...] = jnp.zeros_like(sums)
-    for p in range(NP):
-        for k in range(NE):
-            for q in range(4):
-                sums[q, pl.ds(k * NP + p, 1), :] = by_pillar[p, pl.ds(4 * k + q, 1), :]
-
-    t_rho, g_x, g_y, g_z = (sums[q] for q in range(4))
-    u_x, u_y, u_z, inverse = (geo[i] for i in range(4))
-    radial_part = t_rho - (u_x * g_x + u_y * g_y + u_z * g_z) * inverse
-    grad[...] = jnp.zeros_like(grad)
-    grad[0] = radial_part * u_x + g_x * inverse
-    grad[1] = radial_part * u_y + g_y * inverse
-    grad[2] = radial_part * u_z + g_z * inverse
-
-    parts = []
-    for p in range(NP):
-        terms = jnp.concatenate([grad[:, k * NP + p, :] for k in range(NE)], axis=1)
-        first, rest = split(terms)
-        second, third_part = split(rest)
-        parts.append(
-            jnp.concatenate([first, second, third_part, jnp.zeros_like(first)], 0).astype(BF16)
-        )
-
-    def scatter(lo, hi):
-        seen = {}
-        for p in range(NP):
-            out = dot(parts[p], oh[p, pl.ds(lo * S, (hi - lo) * S), :], (1, 1))
-            out = (out[0:8] + out[8:16]) + out[16:24]
-            for j in range(lo, hi):
-                term = out[:, (j - lo) * S : (j - lo + 1) * S]
-                at = near_slot(p, j)
-                seen[at] = seen[at] - term if at in seen else -term
-        for at, value in seen.items():
-            extf[at] = value
-
-    scatter(2, 9)
-    force_copies = []
-    for n, (dx, dy) in enumerate(DIRECTIONS):
-        if dx == 0:
-            here, there = pl.ds(0, 2), pl.ds(0, 2)
-        elif dx == 1:
-            here, there = pl.ds(2, 1), pl.ds(0, 1)
-        else:
-            here, there = pl.ds(3, 1), pl.ds(1, 1)
-        copy = pltpu.make_async_remote_copy(
-            src_ref=extf.at[PLACE[dy], here],
-            dst_ref=frecv.at[n, there],
-            send_sem=fo_send.at[n],
-            recv_sem=fo_recv.at[n],
-            device_id=device(dx, dy),
-            device_id_type=MESH,
-        )
-        copy.start()
-        force_copies.append(copy)
-
-    scatter(0, 2)
-    total = []
-    for p in range(NP):
-        mine = extf[0, p]
-        for k in range(NE):
-            mine = mine + grad[:, k * NP + p, :]
-        total.append(mine)
-    for n, (dx, dy) in enumerate(DIRECTIONS):
-        force_copies[n].wait_recv()
-        for p in range(NP):
-            if dx == 0 or (dx == 1) == (p == 0):
-                total[p] = total[p] + frecv[n, p]
-    for p in range(NP):
+            total = total + grad[:, NE * (OWN + p) + k, :]
         for m in range(3):
-            forces[p, m] = total[p][m : m + 1]
-
-    for copy in (*pos_copies, *force_copies):
+            forces[p, m] = total[m : m + 1]
+
+    for copy in pos_copies:
         copy.wait_send()
     halo2.sent(range(len(GROUPS2)))
     write.wait()
@@ -667,27 +719,28 @@
             scratch_shapes=small
             + [
                 *[pltpu.VMEM((3, 4, hi - lo, S, C), BF16) for lo, hi in GROUPS + GROUPS2],
-                pltpu.VMEM((3, 4, 8, S), F32),
+                pltpu.VMEM((3, 4, 16, S), F32),
                 pltpu.VMEM((NP, NEAR, ROWS), BF16),
-                pltpu.VMEM((10, NP, C, ROWS), F32),
+                pltpu.VMEM((NP * S, COUNT * ROWS), BF16),
+                pltpu.VMEM((7, NP, C, ROWS), F32),
+                pltpu.VMEM((COUNT, 3, C, ROWS), F32),
                 pltpu.VMEM((10, C, 32), BF16),
                 pltpu.VMEM((4 * C, C), BF16),
-                pltpu.VMEM((64, 8, S), F32),
-                pltpu.VMEM((NP, 8, NE, S), F32),
-                pltpu.VMEM((8, 8, S), F32),
-                pltpu.VMEM((4, 8, S), F32),
-                pltpu.VMEM((2, 8, S), F32),
+                pltpu.VMEM((64, EDGE_ROWS, S), F32),
+                pltpu.VMEM((8, EDGE_ROWS, S), F32),
+                pltpu.VMEM((EDGE_ROWS, 8, S), F32),
+                pltpu.VMEM((EDGE_ROWS, S), F32),
+                pltpu.VMEM((EDGE_ROWS, S), F32),
+                pltpu.VMEM((5, EDGE_ROWS, S), F32),
                 pltpu.VMEM((BLOCKS, NP, C, S), F32),
                 pltpu.VMEM((NP, C, S), F32),
                 pltpu.VMEM((BLOCKS, NP, C, ROWS), F32),
+                pltpu.VMEM((READ_BLOCKS * C, ROWS), F32),
                 pltpu.VMEM((NP, 1, S, BLOCKS * C), BF16),
                 pltpu.VMEM((NP, 1, S, BLOCKS * C), BF16),
-                pltpu.VMEM((6, NP, C, ROWS), F32),
-                pltpu.VMEM((NP, 4 * NE, S), F32),
-                pltpu.VMEM((4, 8, S), F32),
-                pltpu.VMEM((8, 8, S), F32),
-                pltpu.VMEM((3, 4, 8, S), F32),
-                pltpu.VMEM((n_dir, NP, 8, S), F32),
+                pltpu.VMEM((COUNT, 6, C, ROWS), F32),
+                pltpu.VMEM((4, EDGE_ROWS, S), F32),
+                pltpu.VMEM((8, EDGE_ROWS, S), F32),
                 dma((len(small),)),
                 dma,
                 dma,
@@ -697,14 +750,12 @@
                 dma((len(GROUPS), Halo.COUNT)),
                 dma((len(GROUPS2), Halo.COUNT)),
                 dma((len(GROUPS2), Halo.COUNT)),
-                dma((n_dir,)),
-                dma((n_dir,)),
             ],
             compiler_params=pltpu.CompilerParams(
                 collective_id=0, has_side_effects=True, vmem_limit_bytes=60 * 1024 * 1024
             ),
             cost_estimate=pl.CostEstimate(
-                flops=4 * 10**9, bytes_accessed=2 * 10**6, transcendentals=10**5
+                flops=6 * 10**9, bytes_accessed=2 * 10**6, transcendentals=10**5
             ),
         )(*args)
         return new_features, jnp.transpose(force, (0, 2, 1, 3))

time: 60.6 us -> 62 us (1.023)
  Pallas kernels: 56.8 us -> 58.2 us
    pallas_call x1, Pallas kernels: 56.8 us -> 58.2 us  [body(): pl.pallas_call(run_all, out_shape=(jax.ShapeDtypeStruct((NP, 1, S, BLOCKS...]
where the time goes in v4:
time: 62 us; the launch traced here: 61.4 us
  Pallas kernels  58.2 us (94%)
  local copies, waits for them, and re-layouts  2.51 us (4%)
  between operations  0.65 us (1%)
    pallas_call x1, Pallas kernels, body(): pl.pallas_call(run_all, out_shape=(jax.ShapeDtypeStruct((NP, 1, S, BLOCKS...  58.2 us
    unnamed x4, local copies, waits for them, and re-layouts  2.51 us

profile of v4, /device:TPU:2, one launch (start us, length us, event | category | flops | bytes accessed | tf_op | source)
XLA Modules:
  0.0 61.4 jit_solution(8974598806397468653)
XLA Ops:
  0.6 58.2 %shard_map.113 = (bf16[2,1,128,1152]{3,2,1,0:T(8,128)(2,1)}, f32[2,3,1,128]{3,2,1,0:T(1,128)}) custom-call(bf16[2,1,128,1152]{3,2,1,0:T(8,128)(2,1)} %refs_0_.1, f32[2,3,1,128]{3,2,1,0:T(1,128)} %bitcast.3, s32[3,2,1,128]{3,2,1,0:T(1,128)} %refs_2_.1, s32[3,2,1,128]{3,2,1,0:T(1,128)} %refs_3_.1, f32[8,896]{1,0:T(8,128)} %refs_4_.1, f32[8,256]{1,0:T(8,128)} %refs_5_.1, ...), custom_call_target="tpu_custom_call" | custom-call | flops 6000000000 | bytes 2000000 | tf_op jit(solution)/shard_map/pallas_call | solution.py:711
  58.9 0.0 copy-start
  58.9 1.9 %copy.14 = bf16[2,1,128,1152]{3,2,1,0:T(8,128)(2,1)} copy(bf16[2,1,128,1152]{3,2,1,0:T(8,128)(2,1)} %get-tuple-element.8) | data formatting | bytes 1179648
  60.8 0.0 copy-done
  60.8 0.6 copy.15
Async XLA Ops:
  58.9 1.9 %copy-start = (f32[2,3,1,128]{3,2,1,0:T(1,128)S(1)}, f32[2,3,1,128]{3,2,1,0:T(1,128)}, u32[]{:S(2)}) copy-start(f32[2,3,1,128]{3,2,1,0:T(1,128)} %get-tuple-element.5) | copy-start | bytes 9220

commit v5 on v2

--- a/solution.py
+++ b/solution.py
@@ -23,10 +23,10 @@
 KP = NE * NP
 ROWS = NE * S
 NEAR = 9 * S
-STEP = 16
+STEP = 32
 GROUPS = ((0, 4), (4, 7), (7, 9))
 GROUPS2 = ((0, 4),)
-DIRECTIONS = tuple((dx, dy) for dx in (-1, 0, 1) for dy in (-1, 0, 1) if (dx, dy) != (0, 0))
+DIRECTIONS = ((-1, -1), (-1, 1), (1, -1), (1, 1), (-1, 0), (1, 0), (0, -1), (0, 1))
 
 
 def split(x):
@@ -57,6 +57,20 @@
         if c < buf.shape[2]:
             return buf.at[(*at, c)]
         c -= buf.shape[2]
+
+
+def deliver(mixed, forces, mixed_out, forces_out, held, held_forces, sems):
+    parts = [(forces, held_forces, forces_out)]
+    parts += [(mixed.at[p], held.at[p], mixed_out.at[p]) for p in range(NP)]
+    reads = [pltpu.make_async_copy(a, b, sems.at[0, i]) for i, (a, b, _) in enumerate(parts)]
+    writes = [pltpu.make_async_copy(b, c, sems.at[1, i]) for i, (_, b, c) in enumerate(parts)]
+    for copy in reads:
+        copy.start()
+    for read, write in zip(reads, writes):
+        read.wait()
+        write.start()
+    for copy in writes:
+        copy.wait()
 
 
 class Halo:
@@ -229,6 +243,10 @@
     turn(0)
     pl.semaphore_wait(barrier, len(DIRECTIONS))
 
+    halo = Halo(ext, f1_send, f1_recv, device, low_wrap, high_wrap)
+    halo.along_x(1, 0)
+    halo.along_y(0, 0)
+    halo.along_y(1, 0)
     pos_copies = []
     for n, (dx, dy) in enumerate(DIRECTIONS):
         if dx == 0:
@@ -248,10 +266,8 @@
         copy.start()
         pos_copies.append(copy)
 
-    halo = Halo(ext, f1_send, f1_recv, device, low_wrap, high_wrap)
-    for g in range(len(GROUPS)):
-        if g > 0:
-            turn(g)
+    for g in range(1, len(GROUPS)):
+        turn(g)
         halo.along_x(1, g)
         halo.along_y(0, g)
         halo.along_y(1, g)
@@ -516,6 +532,9 @@
     halo2.rest(1, 0)
     gather(ext2, 0, 0, 0, 6, 9)
 
+    def fold(x):
+        return sum(x[8 * i : 8 * i + 8] for i in range(1, STEP // 8)) + x[0:8]
+
     sums[...] = jnp.zeros_like(sums)
     for p in range(NP):
 
@@ -527,14 +546,14 @@
                 far = [gsc[b, r, e] for b in range(READ_BLOCKS)]
                 u = [angle(m, p, k) for m in range(3)]
                 along = u[0] * far[1] + u[1] * far[2] + u[2] * far[3]
-                carry[4 * k] = carry[4 * k] + side[0, r, e] * far[0] + side[1, r, e] * along
+                carry[4 * k] = carry[4 * k] + fold(side[0, r, e] * far[0] + side[1, r, e] * along)
                 own_q = side[2, r, e]
                 for m in range(3):
                     term = side[3 + m, r, e] * along + own_q * far[1 + m]
-                    carry[4 * k + 1 + m] = carry[4 * k + 1 + m] + term
+                    carry[4 * k + 1 + m] = carry[4 * k + 1 + m] + fold(term)
             return tuple(carry)
 
-        zero = jnp.zeros((STEP, S), F32)
+        zero = jnp.zeros((8, S), F32)
         totals = lax.fori_loop(0, C // STEP, pair, (zero,) * (4 * NE))
         for k in range(NE):
             for q in range(4):
@@ -679,6 +698,22 @@
                 flops=4 * 10**9, bytes_accessed=2 * 10**6, transcendentals=10**5
             ),
         )(*args)
+        new_features, force = pl.pallas_call(
+            deliver,
+            out_shape=(
+                jax.ShapeDtypeStruct((NP, 1, S, BLOCKS * C), BF16),
+                jax.ShapeDtypeStruct((NP, 3, 1, S), F32),
+            ),
+            in_specs=[anywhere] * 2,
+            out_specs=(anywhere, anywhere),
+            scratch_shapes=[
+                pltpu.VMEM((NP, 1, S, BLOCKS * C), BF16),
+                pltpu.VMEM((NP, 3, 1, S), F32),
+                dma((2, 1 + NP)),
+            ],
+            compiler_params=pltpu.CompilerParams(vmem_limit_bytes=60 * 1024 * 1024),
+            cost_estimate=pl.CostEstimate(flops=0, bytes_accessed=12 * 10**5, transcendentals=0),
+        )(new_features, force)
         return new_features, jnp.transpose(force, (0, 2, 1, 3))
 
     in_specs = (

time: 59.7 us -> 60.1 us (level)
  Pallas kernels: 56.4 us -> 59.3 us
  local copies, waits for them, and re-layouts: 2.51 us -> 0 us
    unnamed x4 -> x0, local copies, waits for them, and re-layouts: 2.51 us -> none
    pallas_call x0 -> x1, Pallas kernels: none -> 1.83 us  [body(): pl.pallas_call(deliver, out_shape=(jax.ShapeDtypeStruct((NP, 1, S, BLOCKS...]
    pallas_call x1, Pallas kernels: 56.4 us -> 57.5 us  [body(): pl.pallas_call(run_all, out_shape=(jax.ShapeDtypeStruct((NP, 1, S, BLOCKS...]
where the time goes in v5:
time: 60.1 us; the launch traced here: 59.9 us
  Pallas kernels  59.3 us (99%)
  between operations  0.64 us (1%)
    pallas_call x1, Pallas kernels, body(): pl.pallas_call(run_all, out_shape=(jax.ShapeDtypeStruct((NP, 1, S, BLOCKS...  57.5 us
    pallas_call x1, Pallas kernels, body(): pl.pallas_call(deliver, out_shape=(jax.ShapeDtypeStruct((NP, 1, S, BLOCKS...  1.83 us

profile of v5, /device:TPU:1, one launch (start us, length us, event | category | flops | bytes accessed | tf_op | source)
XLA Modules:
  0.0 59.9 jit_solution(16646052628715068588)
XLA Ops:
  0.6 57.5 %shard_map.113 = (bf16[2,1,128,1152]{3,2,1,0:T(8,128)(2,1)}, f32[2,3,1,128]{3,2,1,0:T(1,128)}) custom-call(bf16[2,1,128,1152]{3,2,1,0:T(8,128)(2,1)} %refs_0_.1, f32[2,3,1,128]{3,2,1,0:T(1,128)} %bitcast.2, s32[3,2,1,128]{3,2,1,0:T(1,128)} %refs_2_.1, s32[3,2,1,128]{3,2,1,0:T(1,128)} %refs_3_.1, f32[8,896]{1,0:T(8,128)} %refs_4_.1, f32[8,256]{1,0:T(8,128)} %refs_5_.1, ...), custom_call_target="tpu_custom_call" | custom-call | flops 4000000000 | bytes 2000000 | tf_op jit(solution)/shard_map/pallas_call | solution.py:650
  58.1 1.8 %shard_map.114 = (bf16[2,1,128,1152]{3,2,1,0:T(8,128)(2,1)}, f32[2,3,1,128]{3,2,1,0:T(1,128)}) custom-call(bf16[2,1,128,1152]{3,2,1,0:T(8,128)(2,1)} %get-tuple-element.6.mixed, f32[2,3,1,128]{3,2,1,0:T(1,128)} %get-tuple-element.7.forces), custom_call_target="tpu_custom_call" | custom-call | bytes 1200000 | tf_op jit(solution)/shard_map/pallas_call | solution.py:701

commit v6 on v4

v6 whole, which is shorter than its diff:
```python
import math

import jax
import jax.numpy as jnp
from jax import lax
from jax.experimental import pallas as pl
from jax.experimental.pallas import tpu as pltpu
from jax.sharding import PartitionSpec as P

MESH = pl.DeviceIdType.MESH
F32 = jnp.float32
BF16 = jnp.bfloat16
SOFTENING = 0.25
SPACING = 0.6
ROOT_THREE = math.sqrt(3.0)
C = 128
S = 128
NB = 8
NE = 3
NP = 2
BLOCKS = 9
READ_BLOCKS = 4
ROWS = NE * S
STEP = 32
GROUPS = ((0, 4), (4, 7), (7, 9))
SUMS = ((1, 2, 3), (4, 5, 6), (7, 8, 0))
GROUPS2 = ((0, 2), (2, 4))
COUNT = 6
EDGE_ROWS = 24
NEIGHBOURS = ((-1, 0), (1, 0), (0, -1), (0, 1))


def split(x):
    high = x.astype(BF16).astype(F32)
    return high, x - high


def dot(a, b, contract=(1, 0)):
    dims = (((contract[0],), (contract[1],)), ((), ()))
    return lax.dot_general(a, b, dims, preferred_element_type=F32)


def deliver(mixed, forces, mixed_out, forces_out, held, held_forces, sems):
    parts = [(forces, held_forces, forces_out)]
    parts += [(mixed.at[p], held.at[p], mixed_out.at[p]) for p in range(NP)]
    reads = [pltpu.make_async_copy(a, b, sems.at[0, i]) for i, (a, b, _) in enumerate(parts)]
    writes = [pltpu.make_async_copy(b, c, sems.at[1, i]) for i, (_, b, c) in enumerate(parts)]
    for copy in reads:
        copy.start()
    for read, write in zip(reads, writes):
        read.wait()
        write.start()
    for copy in writes:
        copy.wait()


def kernel(
    gx_size,
    yz_size,
    feat,
    *refs,
):
    small_in, refs = refs[:9], refs[9:]
    mixed, forces, *refs = refs
    small, refs = refs[:9], refs[9:]
    run(gx_size, yz_size, feat, small_in, small, mixed, forces, *refs)


def run(
    gx_size,
    yz_size,
    feat,
    small_in,
    small,
    mixed,
    forces,
    ext0,
    ext1,
    ext2,
    mix0,
    mix1,
    part_out,
    part_in,
    posx,
    oh,
    coef,
    readout,
    wide,
    w_turned,
    zf,
    ang,
    pj,
    inverses,
    target,
    edges,
    acc,
    gate,
    gsc,
    raw,
    mix_out,
    side,
    sums,
    grad,
    force_y,
    force_y_in,
    force_x,
    force_x_in,
    small_sem,
    load_sem,
    out_sem,
    pos_send,
    pos_recv,
    x_send,
    x_recv,
    part_send,
    part_recv,
    mix_send,
    mix_recv,
    force_send,
    force_recv,
):
    ext, ext2 = (ext0, ext1, ext2), (mix0, mix1)
    gx = lax.axis_index("gx")
    yz = lax.axis_index("yz")

    def device(dx, dy):
        return (lax.rem(gx + dx + gx_size, gx_size), lax.rem(yz + dy + yz_size, yz_size))

    def remote(src, dst, send, recv, step):
        return pltpu.make_async_remote_copy(
            src_ref=src,
            dst_ref=dst,
            send_sem=send,
            recv_sem=recv,
            device_id=device(*step),
            device_id_type=MESH,
        )

    small_loads = [
        pltpu.make_async_copy(small_in[i], small[i], small_sem.at[i]) for i in range(len(small))
    ]
    feat_load = pltpu.make_async_copy(feat, raw, load_sem)
    feat_load.start()
    for load in small_loads:
        load.start()
    pos, dst, shift, wr, wq, w_scalar, w_gate, w_vector, w_tensor = small

    barrier = pltpu.get_barrier_semaphore()
    for step in NEIGHBOURS:
        pl.semaphore_signal(barrier, inc=1, device_id=device(*step), device_id_type=MESH)

    def turn(g):
        lo, hi = GROUPS[g]
        for i in range(hi - lo):
            for p in range(NP):
                tile = raw[p, 0, :, pl.ds((lo + i) * C, C)].astype(F32)
                ext[g][p, i] = jnp.transpose(tile).astype(BF16)

    feat_load.wait()
    turn(0)
    pl.semaphore_wait(barrier, len(NEIGHBOURS))

    x_copies = []
    for g in range(len(GROUPS)):
        for own, ghost, dx in ((0, 2, -1), (1, 3, 1)):
            x_copies.append(
                remote(ext[g].at[own], ext[g].at[ghost], x_send.at[g, own], x_recv.at[g, own], (dx, 0))
            )
    x_copies[0].start()
    x_copies[1].start()

    for load in small_loads:
        load.wait()
    for p in range(NP):
        posx[0, p] = jnp.zeros((16, S), F32)
        for m in range(3):
            posx[0, p, pl.ds(m, 1), :] = pos[p, m]
        for k in range(NE):
            posx[0, p, pl.ds(3 + k, 1), :] = dst[k, p].astype(F32)
            posx[0, p, pl.ds(6 + k, 1), :] = shift[k, p].astype(F32)
    own = pl.ds(0, NP)
    pos_copies = [
        remote(posx.at[0, 0], posx.at[0, 2], pos_send.at[0], pos_recv.at[0], (-1, 0)),
        remote(posx.at[0, 1], posx.at[0, 3], pos_send.at[1], pos_recv.at[1], (1, 0)),
        remote(posx.at[0, own], posx.at[2, own], pos_send.at[2], pos_recv.at[2], (0, -1)),
        remote(posx.at[0, own], posx.at[1, own], pos_send.at[3], pos_recv.at[3], (0, 1)),
    ]
    for copy in pos_copies:
        copy.start()
    for g in range(1, len(GROUPS)):
        turn(g)
        x_copies[2 * g].start()
        x_copies[2 * g + 1].start()

    def turned(w):
        high, low = split(w)
        rows = jnp.concatenate([high, low, high, jnp.zeros_like(w)], axis=0)
        return jnp.transpose(rows).astype(BF16)

    def widen(f, carry):
        at = pl.ds(pl.multiple_of(f * C, C), C)
        wide[at, :] = turned(wr[:, at])
        return carry

    lax.fori_loop(0, 7, widen, 0)
    wide[pl.ds(8 * C, C), :] = turned(wq[:, pl.ds(0, C)])
    last = turned(wq[:, pl.ds(C, C)])
    wide[pl.ds(7 * C, C), :] = last
    wide[pl.ds(9 * C, C), :] = last
    for i, w in enumerate((w_scalar, w_gate, w_vector, w_tensor)):
        w_turned[pl.ds(i * C, C), :] = jnp.transpose(w[...].astype(F32)).astype(BF16)

    for copy in pos_copies:
        copy.wait_recv()
    edges[...] = jnp.zeros_like(edges)
    for q in range(COUNT):
        y, p = q // NP, q % NP
        at = pl.ds(NE * q, NE)
        edges[0, at, :] = posx[y, p, pl.ds(3, NE), :]
        edges[1, at, :] = posx[y, p, pl.ds(6, NE), :]
        edges[2, at, :] = jnp.full((NE, S), p, F32)
        edges[3, at, :] = jnp.full((NE, S), (1, 0, 2)[y], F32)
    place = edges[0]
    one = jnp.ones_like(place)
    nil = jnp.zeros_like(place)

    def at_least(x, bound):
        return jnp.where(x >= float(bound), one, nil)

    ext_x = at_least(place, 3 * S) + at_least(place, 6 * S) + at_least(place, 9 * S)
    left = place - ext_x * float(3 * S)
    ext_y = at_least(left, S) + at_least(left, 2 * S)
    step_x = ext_x - 1.0 - edges[2]
    step_y = ext_y - 1.0
    target[...] = jnp.where(edges[3] + step_y == 1.0, ext_x * S + (left - ext_y * S), -1.0)

    atom = lax.broadcasted_iota(jnp.int32, (S, ROWS), 0).astype(F32)

    def pick(y, carry):
        for p in range(NP):
            rows = [target[pl.ds(NE * (NP * y + p) + k, 1), :] for k in range(NE)]
            ends = jnp.concatenate(rows, axis=1) - atom
            for i, x in enumerate((1, 2, 3 * p)):
                hit = jnp.where(ends == float(x * S), 1.0, 0.0).astype(BF16)
                oh[p, pl.ds(i * S, S), pl.ds(pl.multiple_of(y * ROWS, ROWS), ROWS)] = hit
        return carry

    lax.fori_loop(0, 3, pick, 0)

    def in_parts(x):
        first, rest = split(x)
        second, third = split(rest)
        return jnp.concatenate([first, second, third, jnp.zeros_like(first)], 0).astype(BF16)

    def whole(x):
        return (x[0:8] + x[8:16]) + x[16:24]

    pj[...] = jnp.zeros_like(pj)
    for p in range(NP):
        near = [posx[0, slot, pl.ds(0, 8), :] for slot in (0, 1, 3 - p)]
        far = whole(dot(in_parts(jnp.concatenate(near, axis=1)), oh[p]))
        for y in range(3):
            for k in range(NE):
                at = (NE * y + k) * S
                pj[NE * (NP * y + p) + k] = far[:, at : at + S] - posx[y, p, pl.ds(0, 8), :]

    disp_x = pj[:, 0, :] + step_x
    disp_y = pj[:, 1, :] + step_y
    disp_z = pj[:, 2, :] + edges[1]
    rho = jnp.sqrt(disp_x * disp_x + disp_y * disp_y + disp_z * disp_z + SOFTENING)
    inverse = 1.0 / rho
    u_x, u_y, u_z = disp_x * inverse, disp_y * inverse, disp_z * inverse
    inverses[...] = inverse
    length_sq = u_x * u_x + u_y * u_y + u_z * u_z
    angular = (
        u_x,
        u_y,
        u_z,
        ROOT_THREE * u_x * u_y,
        ROOT_THREE * u_y * u_z,
        0.5 * (3.0 * u_z * u_z - length_sq),
        ROOT_THREE * u_x * u_z,
        0.5 * ROOT_THREE * (u_x * u_x - u_y * u_y),
    )
    for f in range(8):
        ang[f] = angular[f]
    zf[...] = jnp.zeros_like(zf)
    for b in range(NB):
        off = (rho - (0.5 + SPACING * b)) / SPACING
        basis = jnp.exp(-(off * off))
        slope = basis * off * (-2.0 / SPACING)
        for i, value in enumerate((basis, slope)):
            high, low = split(value)
            zf[32 * i + b] = high
            zf[32 * i + 8 + b] = high
            zf[32 * i + 16 + b] = low

    def columns(k):
        return pl.ds(k * S, S)

    for q in range(COUNT):
        values = jnp.concatenate([zf[:, NE * q + k, :] for k in range(NE)], axis=1).astype(BF16)
        out = dot(wide[pl.ds(0, 8 * C), :], values[0:32])
        for f in range(7):
            coef[f, q] = out[f * C : (f + 1) * C]
        readout[q, 0] = out[7 * C : 8 * C]
        out = dot(wide[pl.ds(8 * C, 2 * C), :], values[32:64])
        readout[q, 1] = out[0:C]
        readout[q, 2] = out[C : 2 * C]

    def columns(k):
        return pl.ds(k * S, S)

    def gather(bufs, g, to, first, last):
        buf = bufs[g]
        n = buf.shape[1]

        def run(y, carry):
            for p in range(NP):
                tiles = [buf[slot].reshape(n * C, S) for slot in (0, 1, 3 - p)[first:last]]
                rows = pl.ds(first * S, (last - first) * S)
                picks = oh[p, rows, pl.ds(pl.multiple_of(y * ROWS, ROWS), ROWS)]
                out = dot(jnp.concatenate(tiles, axis=1), picks)
                for i in range(n):
                    gsc[to + i, NP * y + p] = out[i * C : (i + 1) * C]
            return carry

        lax.fori_loop(0, 3, run, 0)

    def each_row(fn, lo, hi):
        steps = C // STEP

        def run(i, carry):
            q = i // steps
            fn(q, pl.ds(pl.multiple_of((i - q * steps) * STEP, STEP), STEP))
            return carry

        lax.fori_loop(lo * steps, hi * steps, run, 0)

    def angle(f, q, k):
        return ang[f, pl.ds(NE * q + k, 1), :]

    def message_sv(p, r):
        total = [jnp.zeros((STEP, S), F32) for _ in range(BLOCKS)]
        for k in range(NE):
            e = columns(k)
            s = gsc[0, p, r, e]
            v = [gsc[1 + m, p, r, e] for m in range(3)]
            u = [angle(m, p, k) for m in range(3)]
            along = u[0] * v[0] + u[1] * v[1] + u[2] * v[2]
            total[0] = total[0] + coef[0, p, r, e] * s + coef[1, p, r, e] * along
            r3s = coef[3, p, r, e] * s
            r4 = coef[4, p, r, e]
            for m in range(3):
                total[1 + m] = total[1 + m] + r3s * u[m] + r4 * v[m]
            r5s = coef[5, p, r, e] * s
            for n in range(5):
                total[4 + n] = total[4 + n] + r5s * angle(3 + n, p, k)
        for b in range(BLOCKS):
            acc[b, p, r, :] = total[b]

    def message_t(lo, hi):
        def fn(p, r):
            total = [acc[b, p, r, :] for b in (0, *range(lo, hi))]
            for k in range(NE):
                e = columns(k)
                along = None
                r6 = coef[6, p, r, e]
                for n in range(lo, hi):
                    t = gsc[n, p, r, e]
                    term = angle(n - 1, p, k) * t
                    along = term if along is None else along + term
                    total[1 + n - lo] = total[1 + n - lo] + r6 * t
                total[0] = total[0] + coef[2, p, r, e] * along
            for i, b in enumerate((0, *range(lo, hi))):
                acc[b, p, r, :] = total[i]

        return fn

    third = 1.0 / NE

    def mix(lo, hi, w):
        def run(p, carry):
            terms = [(acc[b, p] * third).astype(BF16) for b in range(lo, hi)]
            out = dot(w_turned[pl.ds(w * C, C), :], jnp.concatenate(terms, axis=1))
            for b in range(lo, hi):
                acc[b, p] = out[:, (b - lo) * S : (b - lo + 1) * S]
            return carry

        lax.fori_loop(0, NP, run, 0)

    part_copies = []
    for h in range(len(SUMS)):
        for i, dy in ((0, -1), (1, 1)):
            part_copies.append(
                remote(
                    part_out.at[h, i],
                    part_in.at[h, 1 - i],
                    part_send.at[h, i],
                    part_recv.at[h, i],
                    (0, dy),
                )
            )

    def send_sums(h):
        for i in range(2):
            for p in range(NP):
                for j, b in enumerate(SUMS[h]):
                    part_out[h, i, p, j] = acc[b, NP * (1 + i) + p].astype(BF16)
            part_copies[2 * h + i].start()

    def add_sums(h):
        for i in range(2):
            part_copies[2 * h + i].wait_recv()
        for p in range(NP):
            for j, b in enumerate(SUMS[h]):
                acc[b, p] = acc[b, p] + part_in[h, 0, p, j].astype(F32) + part_in[h, 1, p, j].astype(F32)

    for g, (lo, hi) in enumerate(GROUPS):
        x_copies[2 * g].wait_recv()
        x_copies[2 * g + 1].wait_recv()
        gather(ext, g, lo, 0, 3)
        if g == 0:
            each_row(message_sv, 0, COUNT)
        else:
            each_row(message_t(lo, hi), 0, COUNT)
        send_sums(g)
    add_sums(0)
    mix(1, 4, 2)
    add_sums(1)
    add_sums(2)

    def scalars(p, carry):
        out = dot(w_turned[pl.ds(0, 2 * C), :], (acc[0, p] * third).astype(BF16))
        pre = out[0:C]
        acc[0, p] = pre * jax.nn.sigmoid(pre)
        gate[p] = jax.nn.sigmoid(out[C : 2 * C])
        return carry

    lax.fori_loop(0, NP, scalars, 0)

    def read_block(b, y, slot):
        g = b // 2
        return ext2[g].at[y, slot, b - GROUPS2[g][0]]

    def read_block(b, at):
        return ext2[b // 2].at[at, b % 2]

    def update_sv(p, r):
        g = gate[p, r, :]
        for b in range(READ_BLOCKS):
            old = ext[0][p, b, r, :].astype(F32)
            step = g * acc[b, p, r, :] if b > 0 else acc[0, p, r, :]
            read_block(b, p)[r, :] = (old + step).astype(BF16)

    each_row(update_sv, 0, NP)
    mix_x, mix_y = [], []
    for g, buf in enumerate(ext2):
        spans = (
            (mix_x, buf.at[0], buf.at[2], (-1, 0)),
            (mix_x, buf.at[1], buf.at[3], (1, 0)),
            (mix_y, buf.at[own], buf.at[pl.ds(6, NP)], (0, -1)),
            (mix_y, buf.at[own], buf.at[pl.ds(4, NP)], (0, 1)),
        )
        for n, (into, src, to, step) in enumerate(spans):
            into.append(remote(src, to, mix_send.at[g, n], mix_recv.at[g, n], step))
    for copy in (*mix_x, *mix_y):
        copy.start()

    def results(lo, hi, value):
        for i in range(hi - lo):
            for p in range(NP):
                mix_out[p, 0, :, pl.ds((lo + i) * C, C)] = jnp.transpose(value(p, i)).astype(BF16)

    mix(4, 9, 3)
    for g, (lo, hi) in enumerate(GROUPS2):
        results(lo, hi, lambda p, i: ext2[g][p, i].astype(F32))
    for g, (lo, hi) in enumerate(GROUPS):
        if g > 0:
            results(lo, hi, lambda p, i: ext[g][p, i].astype(F32) + gate[p] * acc[lo + i, p])
    write = pltpu.make_async_copy(mix_out, mixed, out_sem)
    write.start()

    def near_side(q, r):
        at = jnp.where(q < NP, q, q + 2)
        row = [read_block(b, at)[r, :].astype(F32) for b in range(READ_BLOCKS)]
        s, v = row[0], row[1:]
        for k in range(NE):
            e = columns(k)
            u = [angle(m, q, k) for m in range(3)]
            along = u[0] * v[0] + u[1] * v[1] + u[2] * v[2]
            q1 = readout[q, 0, r, e]
            side[q, 0, r, e] = readout[q, 1, r, e] * s
            side[q, 1, r, e] = readout[q, 2, r, e] * along
            side[q, 2, r, e] = q1 * along
            for m in range(3):
                side[q, 3 + m, r, e] = q1 * v[m]

    for g, (lo, hi) in enumerate(GROUPS2):
        gather(ext2, g, lo, 0, 2)
    each_row(near_side, 0, NP)
    for copy in mix_y:
        copy.wait_recv()
    each_row(near_side, NP, COUNT)
    for copy in (*pos_copies, *x_copies, *part_copies):
        copy.wait_send()
    for g, (lo, hi) in enumerate(GROUPS2):
        mix_x[2 * g].wait_recv()
        mix_x[2 * g + 1].wait_recv()
        gather(ext2, g, READ_BLOCKS + lo, 2, 3)

    def fold(x):
        return sum(x[8 * i : 8 * i + 8] for i in range(1, STEP // 8)) + x[0:8]

    sums[...] = jnp.zeros_like(sums)

    def pairs(q, outer):
        def pair(i, carry):
            r = pl.ds(pl.multiple_of(i * STEP, STEP), STEP)
            carry = list(carry)
            for k in range(NE):
                e = columns(k)
                far = [gsc[b, q, r, e] + gsc[READ_BLOCKS + b, q, r, e] for b in range(READ_BLOCKS)]
                u = [angle(m, q, k) for m in range(3)]
                along = u[0] * far[1] + u[1] * far[2] + u[2] * far[3]
                term = side[q, 0, r, e] * far[0] + side[q, 1, r, e] * along
                carry[4 * k] = carry[4 * k] + fold(term)
                own_q = side[q, 2, r, e]
                for m in range(3):
                    term = side[q, 3 + m, r, e] * along + own_q * far[1 + m]
                    carry[4 * k + 1 + m] = carry[4 * k + 1 + m] + fold(term)
            return tuple(carry)

        zero = jnp.zeros((8, S), F32)
        totals = lax.fori_loop(0, C // STEP, pair, (zero,) * (4 * NE))
        for k in range(NE):
            for i in range(4):
                row = jnp.sum(totals[4 * k + i], axis=0, keepdims=True)
                sums[i, pl.ds(NE * q + k, 1), :] = row
        return outer

    lax.fori_loop(0, COUNT, pairs, 0)

    t_rho, g_x, g_y, g_z = (sums[i] for i in range(4))
    u_x, u_y, u_z, inverse = ang[0], ang[1], ang[2], inverses[...]
    radial_part = t_rho - (u_x * g_x + u_y * g_y + u_z * g_z) * inverse
    grad[...] = jnp.zeros_like(grad)
    grad[0] = radial_part * u_x + g_x * inverse
    grad[1] = radial_part * u_y + g_y * inverse
    grad[2] = radial_part * u_z + g_z * inverse

    def at_atoms(q):
        return (grad[:, NE * q, :] + grad[:, NE * q + 1, :]) + grad[:, NE * q + 2, :]

    force_copies = []
    for i, dy in ((0, -1), (1, 1)):
        force_copies.append(
            remote(force_y.at[i], force_y_in.at[1 - i], force_send.at[i], force_recv.at[i], (0, dy))
        )
    for i, (p, dx) in enumerate(((0, 1), (1, -1))):
        force_copies.append(
            remote(force_x.at[p], force_x_in.at[p], force_send.at[2 + i], force_recv.at[2 + i], (dx, 0))
        )
    parts = []
    for p in range(NP):
        used = [NE * (NP * y + p) + k for y in range(3) for k in range(NE)]
        parts.append(in_parts(jnp.concatenate([grad[:, row, :] for row in used], axis=1)))
    total = [at_atoms(p) for p in range(NP)]
    for p in range(NP):
        out = whole(jnp.transpose(dot(oh[p], parts[p], (1, 1))))
        force_x[1 - p] = -out[:, 2 * S :]
        force_copies[3 - p].start()
        for i in range(NP):
            total[i] = total[i] - out[:, i * S : (i + 1) * S]
    for i in range(2):
        for p in range(NP):
            force_y[i, p] = at_atoms(NP * (1 + i) + p)
        force_copies[i].start()
    for copy in force_copies:
        copy.wait_recv()
    for p in range(NP):
        value = (total[p] + force_x_in[p]) + (force_y_in[0, p] + force_y_in[1, p])
        for m in range(3):
            forces[p, m] = value[m : m + 1]

    for copy in (*mix_x, *mix_y, *force_copies):
        copy.wait_send()
    write.wait()


def solution(mesh):
    gx_size, yz_size = mesh.shape["gx"], mesh.shape["yz"]

    def body(features, positions, *rest):
        args = (features, jnp.transpose(positions, (0, 2, 1, 3)), *rest)
        vmem = pl.BlockSpec(memory_space=pltpu.VMEM)
        anywhere = pl.BlockSpec(memory_space=pl.ANY)
        dma = pltpu.SemaphoreType.DMA

        def run_all(*refs):
            kernel(gx_size, yz_size, *refs)

        small = [pltpu.VMEM(x.shape, x.dtype) for x in args[1:]]
        new_features, force = pl.pallas_call(
            run_all,
            out_shape=(
                jax.ShapeDtypeStruct((NP, 1, S, BLOCKS * C), BF16),
                jax.ShapeDtypeStruct((NP, 3, 1, S), F32),
            ),
            in_specs=[anywhere] * 10,
            out_specs=(anywhere, vmem),
            scratch_shapes=small
            + [
                *[pltpu.VMEM((4, hi - lo, C, S), BF16) for lo, hi in GROUPS],
                *[pltpu.VMEM((8, hi - lo, C, S), BF16) for lo, hi in GROUPS2],
                pltpu.VMEM((len(SUMS), 2, NP, 3, C, S), BF16),
                pltpu.VMEM((len(SUMS), 2, NP, 3, C, S), BF16),
                pltpu.VMEM((3, 4, 16, S), F32),
                pltpu.VMEM((NP, 3 * S, 3 * ROWS), BF16),
                pltpu.VMEM((7, COUNT, C, ROWS), F32),
                pltpu.VMEM((COUNT, 3, C, ROWS), F32),
                pltpu.VMEM((10 * C, 32), BF16),
                pltpu.VMEM((4 * C, C), BF16),
                pltpu.VMEM((64, EDGE_ROWS, S), F32),
                pltpu.VMEM((8, EDGE_ROWS, S), F32),
                pltpu.VMEM((EDGE_ROWS, 8, S), F32),
                pltpu.VMEM((EDGE_ROWS, S), F32),
                pltpu.VMEM((EDGE_ROWS, S), F32),
                pltpu.VMEM((4, EDGE_ROWS, S), F32),
                pltpu.VMEM((BLOCKS, COUNT, C, S), F32),
                pltpu.VMEM((NP, C, S), F32),
                pltpu.VMEM((BLOCKS, COUNT, C, ROWS), F32),
                pltpu.VMEM((NP, 1, S, BLOCKS * C), BF16),
                pltpu.VMEM((NP, 1, S, BLOCKS * C), BF16),
                pltpu.VMEM((COUNT, 6, C, ROWS), F32),
                pltpu.VMEM((4, EDGE_ROWS, S), F32),
                pltpu.VMEM((8, EDGE_ROWS, S), F32),
                pltpu.VMEM((2, NP, 8, S), F32),
                pltpu.VMEM((2, NP, 8, S), F32),
                pltpu.VMEM((NP, 8, S), F32),
                pltpu.VMEM((NP, 8, S), F32),
                dma((len(small),)),
                dma,
                dma,
                dma((4,)),
                dma((4,)),
                dma((len(GROUPS), 2)),
                dma((len(GROUPS), 2)),
                dma((len(SUMS), 2)),
                dma((len(SUMS), 2)),
                dma((len(GROUPS2), 4)),
                dma((len(GROUPS2), 4)),
                dma((4,)),
                dma((4,)),
            ],
            compiler_params=pltpu.CompilerParams(
                collective_id=0, has_side_effects=True, vmem_limit_bytes=60 * 1024 * 1024
            ),
            cost_estimate=pl.CostEstimate(
                flops=6 * 10**9, bytes_accessed=2 * 10**6, transcendentals=10**5
            ),
        )(*args)
        new_features, force = pl.pallas_call(
            deliver,
            out_shape=(
                jax.ShapeDtypeStruct((NP, 1, S, BLOCKS * C), BF16),
                jax.ShapeDtypeStruct((NP, 3, 1, S), F32),
            ),
            in_specs=[anywhere] * 2,
            out_specs=(anywhere, anywhere),
            scratch_shapes=[
                pltpu.VMEM((NP, 1, S, BLOCKS * C), BF16),
                pltpu.VMEM((NP, 3, 1, S), F32),
                dma((2, 1 + NP)),
            ],
            compiler_params=pltpu.CompilerParams(vmem_limit_bytes=60 * 1024 * 1024),
            cost_estimate=pl.CostEstimate(flops=0, bytes_accessed=12 * 10**5, transcendentals=0),
        )(new_features, force)
        return new_features, jnp.transpose(force, (0, 2, 1, 3))

    in_specs = (
        P("gx", "yz", None, None),
        P("gx", "yz", None, None),
        P(None, "gx", "yz", None),
        P(None, "gx", "yz", None),
        P(),
        P(),
        P(),
        P(),
        P(),
        P(),
    )
    out_specs = (P("gx", "yz", None, None), P("gx", "yz", None, None))
    return jax.shard_map(body, mesh=mesh, in_specs=in_specs, out_specs=out_specs, check_vma=False)
```

time: 62 us -> 55.1 us (0.89)
  Pallas kernels: 58.2 us -> 54.3 us
  local copies, waits for them, and re-layouts: 2.51 us -> 0 us
    pallas_call x1, Pallas kernels: 58.2 us -> 52.5 us  [body(): pl.pallas_call(run_all, out_shape=(jax.ShapeDtypeStruct((NP, 1, S, BLOCKS...]
    unnamed x4 -> x0, local copies, waits for them, and re-layouts: 2.51 us -> none
    pallas_call x0 -> x1, Pallas kernels: none -> 1.83 us  [body(): pl.pallas_call(deliver, out_shape=(jax.ShapeDtypeStruct((NP, 1, S, BLOCKS...]
where the time goes in v6:
time: 55.1 us; the launch traced here: 54.9 us
  Pallas kernels  54.3 us (99%)
  between operations  0.64 us (1%)
    pallas_call x1, Pallas kernels, body(): pl.pallas_call(run_all, out_shape=(jax.ShapeDtypeStruct((NP, 1, S, BLOCKS...  52.5 us
    pallas_call x1, Pallas kernels, body(): pl.pallas_call(deliver, out_shape=(jax.ShapeDtypeStruct((NP, 1, S, BLOCKS...  1.83 us

profile of v6, /device:TPU:2, one launch (start us, length us, event | category | flops | bytes accessed | tf_op | source)
XLA Modules:
  0.0 54.9 jit_solution(10499002635308397496)
XLA Ops:
  0.6 52.5 %shard_map.113 = (bf16[2,1,128,1152]{3,2,1,0:T(8,128)(2,1)}, f32[2,3,1,128]{3,2,1,0:T(1,128)}) custom-call(bf16[2,1,128,1152]{3,2,1,0:T(8,128)(2,1)} %refs_0_.1, f32[2,3,1,128]{3,2,1,0:T(1,128)} %bitcast.2, s32[3,2,1,128]{3,2,1,0:T(1,128)} %refs_2_.1, s32[3,2,1,128]{3,2,1,0:T(1,128)} %refs_3_.1, f32[8,896]{1,0:T(8,128)} %refs_4_.1, f32[8,256]{1,0:T(8,128)} %refs_5_.1, ...), custom_call_target="tpu_custom_call" | custom-call | flops 6000000000 | bytes 2000000 | tf_op jit(solution)/shard_map/pallas_call | solution.py:604
  53.1 1.8 %shard_map.114 = (bf16[2,1,128,1152]{3,2,1,0:T(8,128)(2,1)}, f32[2,3,1,128]{3,2,1,0:T(1,128)}) custom-call(bf16[2,1,128,1152]{3,2,1,0:T(8,128)(2,1)} %get-tuple-element.6.mixed, f32[2,3,1,128]{3,2,1,0:T(1,128)} %get-tuple-element.7.forces), custom_call_target="tpu_custom_call" | custom-call | bytes 1200000 | tf_op jit(solution)/shard_map/pallas_call | solution.py:663

commit v7 on v6

--- a/solution.py
+++ b/solution.py
@@ -22,8 +22,8 @@
 READ_BLOCKS = 4
 ROWS = NE * S
 STEP = 32
-GROUPS = ((0, 4), (4, 7), (7, 9))
-SUMS = ((1, 2, 3), (4, 5, 6), (7, 8, 0))
+GROUPS = ((0, 4), (4, 6), (6, 8), (8, 9))
+SUMS = ((1, 2, 3), (4, 5), (6, 7), (8, 0))
 GROUPS2 = ((0, 2), (2, 4))
 COUNT = 6
 EDGE_ROWS = 24
@@ -77,49 +77,53 @@
     ext0,
     ext1,
     ext2,
+    ext3,
     mix0,
     mix1,
-    part_out,
-    part_in,
-    posx,
-    oh,
-    coef,
-    readout,
-    wide,
-    w_turned,
-    zf,
-    ang,
-    pj,
-    inverses,
-    target,
-    edges,
-    acc,
-    gate,
-    gsc,
-    raw,
-    mix_out,
-    side,
-    sums,
-    grad,
-    force_y,
-    force_y_in,
-    force_x,
-    force_x_in,
-    small_sem,
-    load_sem,
-    out_sem,
-    pos_send,
-    pos_recv,
-    x_send,
-    x_recv,
-    part_send,
-    part_recv,
-    mix_send,
-    mix_recv,
-    force_send,
-    force_recv,
+    *refs,
 ):
-    ext, ext2 = (ext0, ext1, ext2), (mix0, mix1)
+    n = len(SUMS)
+    part_out, part_in, refs = refs[:n], refs[n : 2 * n], refs[2 * n :]
+    (
+        posx,
+        oh,
+        coef,
+        readout,
+        wide,
+        w_turned,
+        zf,
+        ang,
+        pj,
+        inverses,
+        target,
+        edges,
+        acc,
+        gate,
+        gsc,
+        raw,
+        mix_out,
+        side,
+        sums,
+        grad,
+        force_y,
+        force_y_in,
+        force_x,
+        force_x_in,
+        small_sem,
+        load_sem,
+        out_sem,
+        pos_send,
+        pos_recv,
+        x_send,
+        x_recv,
+        part_send,
+        part_recv,
+        mix_send,
+        mix_recv,
+        force_send,
+        force_recv,
+    ) = refs
+    ext, ext2 = (ext0, ext1, ext2, ext3), (mix0, mix1)
     gx = lax.axis_index("gx")
     yz = lax.axis_index("yz")
 
@@ -203,12 +207,6 @@
         return carry
 
     lax.fori_loop(0, 7, widen, 0)
-    wide[pl.ds(8 * C, C), :] = turned(wq[:, pl.ds(0, C)])
-    last = turned(wq[:, pl.ds(C, C)])
-    wide[pl.ds(7 * C, C), :] = last
-    wide[pl.ds(9 * C, C), :] = last
-    for i, w in enumerate((w_scalar, w_gate, w_vector, w_tensor)):
-        w_turned[pl.ds(i * C, C), :] = jnp.transpose(w[...].astype(F32)).astype(BF16)
 
     for copy in pos_copies:
         copy.wait_recv()
@@ -298,15 +296,15 @@
     def columns(k):
         return pl.ds(k * S, S)
 
-    for q in range(COUNT):
-        values = jnp.concatenate([zf[:, NE * q + k, :] for k in range(NE)], axis=1).astype(BF16)
-        out = dot(wide[pl.ds(0, 8 * C), :], values[0:32])
+    def expanded(q, part, rows):
+        edge_rows = [zf[pl.ds(32 * part, 32), NE * q + k, :] for k in range(NP * NE)]
+        return dot(rows, jnp.concatenate(edge_rows, axis=1).astype(BF16))
+
+    for q in range(0, COUNT, NP):
+        out = expanded(q, 0, wide[pl.ds(0, 7 * C), :])
         for f in range(7):
-            coef[f, q] = out[f * C : (f + 1) * C]
-        readout[q, 0] = out[7 * C : 8 * C]
-        out = dot(wide[pl.ds(8 * C, 2 * C), :], values[32:64])
-        readout[q, 1] = out[0:C]
-        readout[q, 2] = out[C : 2 * C]
+            for p in range(NP):
+                coef[f, q + p] = out[f * C : (f + 1) * C, p * ROWS : (p + 1) * ROWS]
 
     def columns(k):
         return pl.ds(k * S, S)
@@ -315,17 +313,12 @@
         buf = bufs[g]
         n = buf.shape[1]
 
-        def run(y, carry):
-            for p in range(NP):
-                tiles = [buf[slot].reshape(n * C, S) for slot in (0, 1, 3 - p)[first:last]]
-                rows = pl.ds(first * S, (last - first) * S)
-                picks = oh[p, rows, pl.ds(pl.multiple_of(y * ROWS, ROWS), ROWS)]
-                out = dot(jnp.concatenate(tiles, axis=1), picks)
-                for i in range(n):
-                    gsc[to + i, NP * y + p] = out[i * C : (i + 1) * C]
-            return carry
-
-        lax.fori_loop(0, 3, run, 0)
+        for p in range(NP):
+            tiles = [buf[slot].reshape(n * C, S) for slot in (0, 1, 3 - p)[first:last]]
+            out = dot(jnp.concatenate(tiles, axis=1), oh[p, pl.ds(first * S, (last - first) * S), :])
+            for i in range(n):
+                for y in range(3):
+                    gsc[to + i, NP * y + p] = out[i * C : (i + 1) * C, y * ROWS : (y + 1) * ROWS]
 
     def each_row(fn, lo, hi):
         steps = C // STEP
@@ -394,8 +387,8 @@
         for i, dy in ((0, -1), (1, 1)):
             part_copies.append(
                 remote(
-                    part_out.at[h, i],
-                    part_in.at[h, 1 - i],
+                    part_out[h].at[i],
+                    part_in[h].at[1 - i],
                     part_send.at[h, i],
                     part_recv.at[h, i],
                     (0, dy),
@@ -406,7 +399,7 @@
         for i in range(2):
             for p in range(NP):
                 for j, b in enumerate(SUMS[h]):
-                    part_out[h, i, p, j] = acc[b, NP * (1 + i) + p].astype(BF16)
+                    part_out[h][i, p, j] = acc[b, NP * (1 + i) + p].astype(BF16)
             part_copies[2 * h + i].start()
 
     def add_sums(h):
@@ -414,7 +407,7 @@
             part_copies[2 * h + i].wait_recv()
         for p in range(NP):
             for j, b in enumerate(SUMS[h]):
-                acc[b, p] = acc[b, p] + part_in[h, 0, p, j].astype(F32) + part_in[h, 1, p, j].astype(F32)
+                acc[b, p] = acc[b, p] + part_in[h][0, p, j].astype(F32) + part_in[h][1, p, j].astype(F32)
 
     for g, (lo, hi) in enumerate(GROUPS):
         x_copies[2 * g].wait_recv()
@@ -425,10 +418,25 @@
         else:
             each_row(message_t(lo, hi), 0, COUNT)
         send_sums(g)
+
+    wide[pl.ds(8 * C, C), :] = turned(wq[:, pl.ds(0, C)])
+    last = turned(wq[:, pl.ds(C, C)])
+    wide[pl.ds(7 * C, C), :] = last
+    wide[pl.ds(9 * C, C), :] = last
+    for i, w in enumerate((w_scalar, w_gate, w_vector, w_tensor)):
+        w_turned[pl.ds(i * C, C), :] = jnp.transpose(w[...].astype(F32)).astype(BF16)
+    for q in range(0, COUNT, NP):
+        outs = [expanded(q, 0, wide[pl.ds(7 * C, C), :]), expanded(q, 1, wide[pl.ds(8 * C, 2 * C), :])]
+        for p in range(NP):
+            at = slice(p * ROWS, (p + 1) * ROWS)
+            readout[q + p, 0] = outs[0][:, at]
+            readout[q + p, 1] = outs[1][0:C, at]
+            readout[q + p, 2] = outs[1][C : 2 * C, at]
     add_sums(0)
     mix(1, 4, 2)
     add_sums(1)
     add_sums(2)
+    add_sums(3)
 
     def scalars(p, carry):
         out = dot(w_turned[pl.ds(0, 2 * C), :], (acc[0, p] * third).astype(BF16))
@@ -613,8 +621,8 @@
             + [
                 *[pltpu.VMEM((4, hi - lo, C, S), BF16) for lo, hi in GROUPS],
                 *[pltpu.VMEM((8, hi - lo, C, S), BF16) for lo, hi in GROUPS2],
-                pltpu.VMEM((len(SUMS), 2, NP, 3, C, S), BF16),
-                pltpu.VMEM((len(SUMS), 2, NP, 3, C, S), BF16),
+                *[pltpu.VMEM((2, NP, len(blocks), C, S), BF16) for blocks in SUMS],
+                *[pltpu.VMEM((2, NP, len(blocks), C, S), BF16) for blocks in SUMS],
                 pltpu.VMEM((3, 4, 16, S), F32),
                 pltpu.VMEM((NP, 3 * S, 3 * ROWS), BF16),
                 pltpu.VMEM((7, COUNT, C, ROWS), F32),

time: 55.1 us -> 53.7 us (0.975)
  Pallas kernels: 54.3 us -> 53 us
    pallas_call x1, Pallas kernels: 52.5 us -> 51.1 us  [body(): pl.pallas_call(run_all, out_shape=(jax.ShapeDtypeStruct((NP, 1, S, BLOCKS...]
where the time goes in v7:
time: 53.7 us; the launch traced here: 53.6 us
  Pallas kernels  53 us (99%)
  between operations  0.64 us (1%)
    pallas_call x1, Pallas kernels, body(): pl.pallas_call(run_all, out_shape=(jax.ShapeDtypeStruct((NP, 1, S, BLOCKS...  51.1 us
    pallas_call x1, Pallas kernels, body(): pl.pallas_call(deliver, out_shape=(jax.ShapeDtypeStruct((NP, 1, S, BLOCKS...  1.83 us

profile of v7, /device:TPU:2, one launch (start us, length us, event | category | flops | bytes accessed | tf_op | source)
XLA Modules:
  0.0 53.6 jit_solution(10637725063045647093)
XLA Ops:
  0.6 51.1 %shard_map.113 = (bf16[2,1,128,1152]{3,2,1,0:T(8,128)(2,1)}, f32[2,3,1,128]{3,2,1,0:T(1,128)}) custom-call(bf16[2,1,128,1152]{3,2,1,0:T(8,128)(2,1)} %refs_0_.1, f32[2,3,1,128]{3,2,1,0:T(1,128)} %bitcast.2, s32[3,2,1,128]{3,2,1,0:T(1,128)} %refs_2_.1, s32[3,2,1,128]{3,2,1,0:T(1,128)} %refs_3_.1, f32[8,896]{1,0:T(8,128)} %refs_4_.1, f32[8,256]{1,0:T(8,128)} %refs_5_.1, ...), custom_call_target="tpu_custom_call" | custom-call | flops 6000000000 | bytes 2000000 | tf_op jit(solution)/shard_map/pallas_call | solution.py:612
  51.8 1.8 %shard_map.114 = (bf16[2,1,128,1152]{3,2,1,0:T(8,128)(2,1)}, f32[2,3,1,128]{3,2,1,0:T(1,128)}) custom-call(bf16[2,1,128,1152]{3,2,1,0:T(8,128)(2,1)} %get-tuple-element.6.mixed, f32[2,3,1,128]{3,2,1,0:T(1,128)} %get-tuple-element.7.forces), custom_call_target="tpu_custom_call" | custom-call | bytes 1200000 | tf_op jit(solution)/shard_map/pallas_call | solution.py:671

commit v8 on v7

--- a/solution.py
+++ b/solution.py
@@ -42,7 +42,9 @@
 
 def deliver(mixed, forces, mixed_out, forces_out, held, held_forces, sems):
     parts = [(forces, held_forces, forces_out)]
-    parts += [(mixed.at[p], held.at[p], mixed_out.at[p]) for p in range(NP)]
+    for i in range(8):
+        at = (i // 4, 0, pl.ds(i % 4 * (S // 4), S // 4))
+        parts.append((mixed.at[at], held.at[at], mixed_out.at[at]))
     reads = [pltpu.make_async_copy(a, b, sems.at[0, i]) for i, (a, b, _) in enumerate(parts)]
     writes = [pltpu.make_async_copy(b, c, sems.at[1, i]) for i, (_, b, c) in enumerate(parts)]
     for copy in reads:
@@ -140,6 +142,10 @@
             device_id_type=MESH,
         )
 
+    barrier = pltpu.get_barrier_semaphore()
+    for step in NEIGHBOURS:
+        pl.semaphore_signal(barrier, inc=1, device_id=device(*step), device_id_type=MESH)
+
     small_loads = [
         pltpu.make_async_copy(small_in[i], small[i], small_sem.at[i]) for i in range(len(small))
     ]
@@ -149,16 +155,11 @@
         load.start()
     pos, dst, shift, wr, wq, w_scalar, w_gate, w_vector, w_tensor = small
 
-    barrier = pltpu.get_barrier_semaphore()
-    for step in NEIGHBOURS:
-        pl.semaphore_signal(barrier, inc=1, device_id=device(*step), device_id_type=MESH)
-
     def turn(g):
         lo, hi = GROUPS[g]
         for i in range(hi - lo):
             for p in range(NP):
-                tile = raw[p, 0, :, pl.ds((lo + i) * C, C)].astype(F32)
-                ext[g][p, i] = jnp.transpose(tile).astype(BF16)
+                ext[g][p, i] = jnp.transpose(raw[p, 0, :, pl.ds((lo + i) * C, C)])
 
     feat_load.wait()
     turn(0)
@@ -424,7 +425,7 @@
     wide[pl.ds(7 * C, C), :] = last
     wide[pl.ds(9 * C, C), :] = last
     for i, w in enumerate((w_scalar, w_gate, w_vector, w_tensor)):
-        w_turned[pl.ds(i * C, C), :] = jnp.transpose(w[...].astype(F32)).astype(BF16)
+        w_turned[pl.ds(i * C, C), :] = jnp.transpose(w[...])
     for q in range(0, COUNT, NP):
         outs = [expanded(q, 0, wide[pl.ds(7 * C, C), :]), expanded(q, 1, wide[pl.ds(8 * C, 2 * C), :])]
         for p in range(NP):
@@ -478,11 +479,11 @@
     def results(lo, hi, value):
         for i in range(hi - lo):
             for p in range(NP):
-                mix_out[p, 0, :, pl.ds((lo + i) * C, C)] = jnp.transpose(value(p, i)).astype(BF16)
+                mix_out[p, 0, :, pl.ds((lo + i) * C, C)] = jnp.transpose(value(p, i).astype(BF16))
 
     mix(4, 9, 3)
     for g, (lo, hi) in enumerate(GROUPS2):
-        results(lo, hi, lambda p, i: ext2[g][p, i].astype(F32))
+        results(lo, hi, lambda p, i: ext2[g][p, i])
     for g, (lo, hi) in enumerate(GROUPS):
         if g > 0:
             results(lo, hi, lambda p, i: ext[g][p, i].astype(F32) + gate[p] * acc[lo + i, p])
@@ -510,25 +511,19 @@
     for copy in mix_y:
         copy.wait_recv()
     each_row(near_side, NP, COUNT)
-    for copy in (*pos_copies, *x_copies, *part_copies):
-        copy.wait_send()
-    for g, (lo, hi) in enumerate(GROUPS2):
-        mix_x[2 * g].wait_recv()
-        mix_x[2 * g + 1].wait_recv()
-        gather(ext2, g, READ_BLOCKS + lo, 2, 3)
 
     def fold(x):
         return sum(x[8 * i : 8 * i + 8] for i in range(1, STEP // 8)) + x[0:8]
 
     sums[...] = jnp.zeros_like(sums)
 
-    def pairs(q, outer):
+    def pairs(q, lo, first):
         def pair(i, carry):
             r = pl.ds(pl.multiple_of(i * STEP, STEP), STEP)
             carry = list(carry)
             for k in range(NE):
                 e = columns(k)
-                far = [gsc[b, q, r, e] + gsc[READ_BLOCKS + b, q, r, e] for b in range(READ_BLOCKS)]
+                far = [gsc[lo + b, q, r, e] for b in range(READ_BLOCKS)]
                 u = [angle(m, q, k) for m in range(3)]
                 along = u[0] * far[1] + u[1] * far[2] + u[2] * far[3]
                 term = side[q, 0, r, e] * far[0] + side[q, 1, r, e] * along
@@ -544,10 +539,24 @@
         for k in range(NE):
             for i in range(4):
                 row = jnp.sum(totals[4 * k + i], axis=0, keepdims=True)
-                sums[i, pl.ds(NE * q + k, 1), :] = row
-        return outer
-
-    lax.fori_loop(0, COUNT, pairs, 0)
+                at = pl.ds(NE * q + k, 1)
+                sums[i, at, :] = row if first else sums[i, at, :] + row
+
+    def each_pairs(lo, first):
+        def run(q, carry):
+            pairs(q, lo, first)
+            return carry
+
+        lax.fori_loop(0, COUNT, run, 0)
+
+    each_pairs(0, True)
+    for copy in (*pos_copies, *x_copies, *part_copies):
+        copy.wait_send()
+    for g, (lo, hi) in enumerate(GROUPS2):
+        mix_x[2 * g].wait_recv()
+        mix_x[2 * g + 1].wait_recv()
+        gather(ext2, g, READ_BLOCKS + lo, 2, 3)
+    each_pairs(READ_BLOCKS, False)
 
     t_rho, g_x, g_y, g_z = (sums[i] for i in range(4))
     u_x, u_y, u_z, inverse = ang[0], ang[1], ang[2], inverses[...]
@@ -574,16 +583,20 @@
         used = [NE * (NP * y + p) + k for y in range(3) for k in range(NE)]
         parts.append(in_parts(jnp.concatenate([grad[:, row, :] for row in used], axis=1)))
     total = [at_atoms(p) for p in range(NP)]
+    def scatter(p, lo, hi):
+        return whole(jnp.transpose(dot(oh[p, pl.ds(lo * S, (hi - lo) * S), :], parts[p], (1, 1))))
+
     for p in range(NP):
-        out = whole(jnp.transpose(dot(oh[p], parts[p], (1, 1))))
-        force_x[1 - p] = -out[:, 2 * S :]
+        force_x[1 - p] = -scatter(p, 2, 3)
         force_copies[3 - p].start()
-        for i in range(NP):
-            total[i] = total[i] - out[:, i * S : (i + 1) * S]
     for i in range(2):
         for p in range(NP):
             force_y[i, p] = at_atoms(NP * (1 + i) + p)
         force_copies[i].start()
+    for p in range(NP):
+        out = scatter(p, 0, 2)
+        for i in range(NP):
+            total[i] = total[i] - out[:, i * S : (i + 1) * S]
     for copy in force_copies:
         copy.wait_recv()
     for p in range(NP):
@@ -679,7 +692,7 @@
             scratch_shapes=[
                 pltpu.VMEM((NP, 1, S, BLOCKS * C), BF16),
                 pltpu.VMEM((NP, 3, 1, S), F32),
-                dma((2, 1 + NP)),
+                dma((2, 9)),
             ],
             compiler_params=pltpu.CompilerParams(vmem_limit_bytes=60 * 1024 * 1024),
             cost_estimate=pl.CostEstimate(flops=0, bytes_accessed=12 * 10**5, transcendentals=0),

time: 53.7 us -> 53.2 us (level)
  Pallas kernels: 53 us -> 52.4 us
    pallas_call x1, Pallas kernels: 51.1 us -> 50.5 us  [body(): pl.pallas_call(run_all, out_shape=(jax.ShapeDtypeStruct((NP, 1, S, BLOCKS...]
where the time goes in v8:
time: 53.2 us; the launch traced here: 53 us
  Pallas kernels  52.4 us (98%)
  between operations  0.64 us (1%)
    pallas_call x1, Pallas kernels, body(): pl.pallas_call(run_all, out_shape=(jax.ShapeDtypeStruct((NP, 1, S, BLOCKS...  50.5 us
    pallas_call x1, Pallas kernels, body(): pl.pallas_call(deliver, out_shape=(jax.ShapeDtypeStruct((NP, 1, S, BLOCKS...  1.93 us

profile of v8, /device:TPU:2, one launch (start us, length us, event | category | flops | bytes accessed | tf_op | source)
XLA Modules:
  0.0 53.0 jit_solution(2326793087852798132)
XLA Ops:
  0.6 50.5 %shard_map.113 = (bf16[2,1,128,1152]{3,2,1,0:T(8,128)(2,1)}, f32[2,3,1,128]{3,2,1,0:T(1,128)}) custom-call(bf16[2,1,128,1152]{3,2,1,0:T(8,128)(2,1)} %refs_0_.1, f32[2,3,1,128]{3,2,1,0:T(1,128)} %bitcast.2, s32[3,2,1,128]{3,2,1,0:T(1,128)} %refs_2_.1, s32[3,2,1,128]{3,2,1,0:T(1,128)} %refs_3_.1, f32[8,896]{1,0:T(8,128)} %refs_4_.1, f32[8,256]{1,0:T(8,128)} %refs_5_.1, ...), custom_call_target="tpu_custom_call" | custom-call | flops 6000000000 | bytes 2000000 | tf_op jit(solution)/shard_map/pallas_call | solution.py:625
  51.1 1.9 %shard_map.114 = (bf16[2,1,128,1152]{3,2,1,0:T(8,128)(2,1)}, f32[2,3,1,128]{3,2,1,0:T(1,128)}) custom-call(bf16[2,1,128,1152]{3,2,1,0:T(8,128)(2,1)} %get-tuple-element.6.mixed, f32[2,3,1,128]{3,2,1,0:T(1,128)} %get-tuple-element.7.forces), custom_call_target="tpu_custom_call" | custom-call | bytes 1200000 | tf_op jit(solution)/shard_map/pallas_call | solution.py:684

commit v9 on v8

--- a/solution.py
+++ b/solution.py
@@ -42,9 +42,7 @@
 
 def deliver(mixed, forces, mixed_out, forces_out, held, held_forces, sems):
     parts = [(forces, held_forces, forces_out)]
-    for i in range(8):
-        at = (i // 4, 0, pl.ds(i % 4 * (S // 4), S // 4))
-        parts.append((mixed.at[at], held.at[at], mixed_out.at[at]))
+    parts += [(mixed.at[p], held.at[p], mixed_out.at[p]) for p in range(NP)]
     reads = [pltpu.make_async_copy(a, b, sems.at[0, i]) for i, (a, b, _) in enumerate(parts)]
     writes = [pltpu.make_async_copy(b, c, sems.at[1, i]) for i, (_, b, c) in enumerate(parts)]
     for copy in reads:
@@ -95,7 +93,6 @@
         w_turned,
         zf,
         ang,
-        pj,
         inverses,
         target,
         edges,
@@ -219,6 +216,8 @@
         edges[1, at, :] = posx[y, p, pl.ds(6, NE), :]
         edges[2, at, :] = jnp.full((NE, S), p, F32)
         edges[3, at, :] = jnp.full((NE, S), (1, 0, 2)[y], F32)
+        for m in range(3):
+            edges[4 + m, at, :] = jnp.broadcast_to(posx[y, p, pl.ds(m, 1), :], (NE, S))
     place = edges[0]
     one = jnp.ones_like(place)
     nil = jnp.zeros_like(place)
@@ -231,7 +230,8 @@
     ext_y = at_least(left, S) + at_least(left, 2 * S)
     step_x = ext_x - 1.0 - edges[2]
     step_y = ext_y - 1.0
-    target[...] = jnp.where(edges[3] + step_y == 1.0, ext_x * S + (left - ext_y * S), -1.0)
+    far_slot = left - ext_y * S
+    target[...] = jnp.where(edges[3] + step_y == 1.0, ext_x * S + far_slot, -1.0)
 
     atom = lax.broadcasted_iota(jnp.int32, (S, ROWS), 0).astype(F32)
 
@@ -254,18 +254,20 @@
     def whole(x):
         return (x[0:8] + x[8:16]) + x[16:24]
 
-    pj[...] = jnp.zeros_like(pj)
-    for p in range(NP):
-        near = [posx[0, slot, pl.ds(0, 8), :] for slot in (0, 1, 3 - p)]
-        far = whole(dot(in_parts(jnp.concatenate(near, axis=1)), oh[p]))
-        for y in range(3):
-            for k in range(NE):
-                at = (NE * y + k) * S
-                pj[NE * (NP * y + p) + k] = far[:, at : at + S] - posx[y, p, pl.ds(0, 8), :]
-
-    disp_x = pj[:, 0, :] + step_x
-    disp_y = pj[:, 1, :] + step_y
-    disp_z = pj[:, 2, :] + edges[1]
+    lanes = far_slot.astype(jnp.int32)
+
+    def far_place(m):
+        found = []
+        for slot in (3, 0, 1, 2):
+            row = jnp.broadcast_to(posx[0, slot, pl.ds(m, 1), :], (EDGE_ROWS, S))
+            found.append(jnp.take_along_axis(row, lanes, axis=1, mode="promise_in_bounds"))
+        low = jnp.where(ext_x == 0.0, found[0], found[1])
+        high = jnp.where(ext_x == 2.0, found[2], found[3])
+        return jnp.where(ext_x < 2.0, low, high)
+
+    disp_x = far_place(0) - edges[4] + step_x
+    disp_y = far_place(1) - edges[5] + step_y
+    disp_z = far_place(2) - edges[6] + edges[1]
     rho = jnp.sqrt(disp_x * disp_x + disp_y * disp_y + disp_z * disp_z + SOFTENING)
     inverse = 1.0 / rho
     u_x, u_y, u_z = disp_x * inverse, disp_y * inverse, disp_z * inverse
@@ -644,10 +646,9 @@
                 pltpu.VMEM((4 * C, C), BF16),
                 pltpu.VMEM((64, EDGE_ROWS, S), F32),
                 pltpu.VMEM((8, EDGE_ROWS, S), F32),
-                pltpu.VMEM((EDGE_ROWS, 8, S), F32),
                 pltpu.VMEM((EDGE_ROWS, S), F32),
                 pltpu.VMEM((EDGE_ROWS, S), F32),
-                pltpu.VMEM((4, EDGE_ROWS, S), F32),
+                pltpu.VMEM((7, EDGE_ROWS, S), F32),
                 pltpu.VMEM((BLOCKS, COUNT, C, S), F32),
                 pltpu.VMEM((NP, C, S), F32),
                 pltpu.VMEM((BLOCKS, COUNT, C, ROWS), F32),
@@ -692,7 +693,7 @@
             scratch_shapes=[
                 pltpu.VMEM((NP, 1, S, BLOCKS * C), BF16),
                 pltpu.VMEM((NP, 3, 1, S), F32),
-                dma((2, 9)),
+                dma((2, 1 + NP)),
             ],
             compiler_params=pltpu.CompilerParams(vmem_limit_bytes=60 * 1024 * 1024),
             cost_estimate=pl.CostEstimate(flops=0, bytes_accessed=12 * 10**5, transcendentals=0),

time: 53.2 us -> 52.8 us (level)
  no operation moved by 1% of the time
where the time goes in v9:
time: 52.8 us; the launch traced here: 52.7 us
  Pallas kernels  52 us (98%)
  between operations  0.64 us (1%)
    pallas_call x1, Pallas kernels, body(): pl.pallas_call(run_all, out_shape=(jax.ShapeDtypeStruct((NP, 1, S, BLOCKS...  50.2 us
    pallas_call x1, Pallas kernels, body(): pl.pallas_call(deliver, out_shape=(jax.ShapeDtypeStruct((NP, 1, S, BLOCKS...  1.83 us

profile of v9, /device:TPU:2, one launch (start us, length us, event | category | flops | bytes accessed | tf_op | source)
XLA Modules:
  0.0 52.7 jit_solution(5041329185140741693)
XLA Ops:
  0.6 50.2 %shard_map.113 = (bf16[2,1,128,1152]{3,2,1,0:T(8,128)(2,1)}, f32[2,3,1,128]{3,2,1,0:T(1,128)}) custom-call(bf16[2,1,128,1152]{3,2,1,0:T(8,128)(2,1)} %refs_0_.1, f32[2,3,1,128]{3,2,1,0:T(1,128)} %bitcast.2, s32[3,2,1,128]{3,2,1,0:T(1,128)} %refs_2_.1, s32[3,2,1,128]{3,2,1,0:T(1,128)} %refs_3_.1, f32[8,896]{1,0:T(8,128)} %refs_4_.1, f32[8,256]{1,0:T(8,128)} %refs_5_.1, ...), custom_call_target="tpu_custom_call" | custom-call | flops 6000000000 | bytes 2000000 | tf_op jit(solution)/shard_map/pallas_call | solution.py:627
  50.8 1.8 %shard_map.114 = (bf16[2,1,128,1152]{3,2,1,0:T(8,128)(2,1)}, f32[2,3,1,128]{3,2,1,0:T(1,128)}) custom-call(bf16[2,1,128,1152]{3,2,1,0:T(8,128)(2,1)} %get-tuple-element.6.mixed, f32[2,3,1,128]{3,2,1,0:T(1,128)} %get-tuple-element.7.forces), custom_call_target="tpu_custom_call" | custom-call | bytes 1200000 | tf_op jit(solution)/shard_map/pallas_call | solution.py:685

commit v10 on v9

--- a/solution.py
+++ b/solution.py
@@ -337,7 +337,7 @@
         return ang[f, pl.ds(NE * q + k, 1), :]
 
     def message_sv(p, r):
-        total = [jnp.zeros((STEP, S), F32) for _ in range(BLOCKS)]
+        total = [jnp.zeros((STEP, S), F32) for _ in range(READ_BLOCKS)]
         for k in range(NE):
             e = columns(k)
             s = gsc[0, p, r, e]
@@ -349,11 +349,18 @@
             r4 = coef[4, p, r, e]
             for m in range(3):
                 total[1 + m] = total[1 + m] + r3s * u[m] + r4 * v[m]
-            r5s = coef[5, p, r, e] * s
+        for b in range(READ_BLOCKS):
+            acc[b, p, r, :] = total[b]
+
+    def message_st(p, r):
+        total = [jnp.zeros((STEP, S), F32) for _ in range(5)]
+        for k in range(NE):
+            e = columns(k)
+            r5s = coef[5, p, r, e] * gsc[0, p, r, e]
             for n in range(5):
-                total[4 + n] = total[4 + n] + r5s * angle(3 + n, p, k)
-        for b in range(BLOCKS):
-            acc[b, p, r, :] = total[b]
+                total[n] = total[n] + r5s * angle(3 + n, p, k)
+        for n in range(5):
+            acc[READ_BLOCKS + n, p, r, :] = total[n]
 
     def message_t(lo, hi):
         def fn(p, r):
@@ -416,11 +423,12 @@
         x_copies[2 * g].wait_recv()
         x_copies[2 * g + 1].wait_recv()
         gather(ext, g, lo, 0, 3)
+        message = message_sv if g == 0 else message_t(lo, hi)
+        each_row(message, NP, COUNT)
+        send_sums(g)
+        each_row(message, 0, NP)
         if g == 0:
-            each_row(message_sv, 0, COUNT)
-        else:
-            each_row(message_t(lo, hi), 0, COUNT)
-        send_sums(g)
+            each_row(message_st, 0, COUNT)
 
     wide[pl.ds(8 * C, C), :] = turned(wq[:, pl.ds(0, C)])
     last = turned(wq[:, pl.ds(C, C)])

time: 52.8 us -> 52.9 us (level)
  no operation moved by 1% of the time
where the time goes in v10:
time: 52.9 us; the launch traced here: 52.8 us
  Pallas kernels  52.1 us (98%)
  between operations  0.64 us (1%)
    pallas_call x1, Pallas kernels, body(): pl.pallas_call(run_all, out_shape=(jax.ShapeDtypeStruct((NP, 1, S, BLOCKS...  50.3 us
    pallas_call x1, Pallas kernels, body(): pl.pallas_call(deliver, out_shape=(jax.ShapeDtypeStruct((NP, 1, S, BLOCKS...  1.83 us

profile of v10, /device:TPU:2, one launch (start us, length us, event | category | flops | bytes accessed | tf_op | source)
XLA Modules:
  0.0 52.8 jit_solution(3918935700299884306)
XLA Ops:
  0.6 50.3 %shard_map.113 = (bf16[2,1,128,1152]{3,2,1,0:T(8,128)(2,1)}, f32[2,3,1,128]{3,2,1,0:T(1,128)}) custom-call(bf16[2,1,128,1152]{3,2,1,0:T(8,128)(2,1)} %refs_0_.1, f32[2,3,1,128]{3,2,1,0:T(1,128)} %bitcast.2, s32[3,2,1,128]{3,2,1,0:T(1,128)} %refs_2_.1, s32[3,2,1,128]{3,2,1,0:T(1,128)} %refs_3_.1, f32[8,896]{1,0:T(8,128)} %refs_4_.1, f32[8,256]{1,0:T(8,128)} %refs_5_.1, ...), custom_call_target="tpu_custom_call" | custom-call | flops 6000000000 | bytes 2000000 | tf_op jit(solution)/shard_map/pallas_call | solution.py:635
  50.9 1.8 %shard_map.114 = (bf16[2,1,128,1152]{3,2,1,0:T(8,128)(2,1)}, f32[2,3,1,128]{3,2,1,0:T(1,128)}) custom-call(bf16[2,1,128,1152]{3,2,1,0:T(8,128)(2,1)} %get-tuple-element.6.mixed, f32[2,3,1,128]{3,2,1,0:T(1,128)} %get-tuple-element.7.forces), custom_call_target="tpu_custom_call" | custom-call | bytes 1200000 | tf_op jit(solution)/shard_map/pallas_call | solution.py:693

commit v11 on v10

--- a/solution.py
+++ b/solution.py
@@ -483,22 +483,8 @@
         )
         for n, (into, src, to, step) in enumerate(spans):
             into.append(remote(src, to, mix_send.at[g, n], mix_recv.at[g, n], step))
-    for copy in (*mix_x, *mix_y):
+    for copy in (*mix_x[:2], *mix_y, *mix_x[2:]):
         copy.start()
-
-    def results(lo, hi, value):
-        for i in range(hi - lo):
-            for p in range(NP):
-                mix_out[p, 0, :, pl.ds((lo + i) * C, C)] = jnp.transpose(value(p, i).astype(BF16))
-
-    mix(4, 9, 3)
-    for g, (lo, hi) in enumerate(GROUPS2):
-        results(lo, hi, lambda p, i: ext2[g][p, i])
-    for g, (lo, hi) in enumerate(GROUPS):
-        if g > 0:
-            results(lo, hi, lambda p, i: ext[g][p, i].astype(F32) + gate[p] * acc[lo + i, p])
-    write = pltpu.make_async_copy(mix_out, mixed, out_sem)
-    write.start()
 
     def near_side(q, r):
         at = jnp.where(q < NP, q, q + 2)
@@ -518,9 +504,6 @@
     for g, (lo, hi) in enumerate(GROUPS2):
         gather(ext2, g, lo, 0, 2)
     each_row(near_side, 0, NP)
-    for copy in mix_y:
-        copy.wait_recv()
-    each_row(near_side, NP, COUNT)
 
     def fold(x):
         return sum(x[8 * i : 8 * i + 8] for i in range(1, STEP // 8)) + x[0:8]
@@ -552,21 +535,25 @@
                 at = pl.ds(NE * q + k, 1)
                 sums[i, at, :] = row if first else sums[i, at, :] + row
 
-    def each_pairs(lo, first):
+    def each_pairs(lo, first, pillars):
         def run(q, carry):
             pairs(q, lo, first)
             return carry
 
-        lax.fori_loop(0, COUNT, run, 0)
-
-    each_pairs(0, True)
+        lax.fori_loop(*pillars, run, 0)
+
+    each_pairs(0, True, (0, NP))
+    for copy in mix_y:
+        copy.wait_recv()
+    each_row(near_side, NP, COUNT)
+    each_pairs(0, True, (NP, COUNT))
     for copy in (*pos_copies, *x_copies, *part_copies):
         copy.wait_send()
     for g, (lo, hi) in enumerate(GROUPS2):
         mix_x[2 * g].wait_recv()
         mix_x[2 * g + 1].wait_recv()
         gather(ext2, g, READ_BLOCKS + lo, 2, 3)
-    each_pairs(READ_BLOCKS, False)
+    each_pairs(READ_BLOCKS, False, (0, COUNT))
 
     t_rho, g_x, g_y, g_z = (sums[i] for i in range(4))
     u_x, u_y, u_z, inverse = ang[0], ang[1], ang[2], inverses[...]
@@ -607,6 +594,20 @@
         out = scatter(p, 0, 2)
         for i in range(NP):
             total[i] = total[i] - out[:, i * S : (i + 1) * S]
+    def results(lo, hi, value):
+        for i in range(hi - lo):
+            for p in range(NP):
+                mix_out[p, 0, :, pl.ds((lo + i) * C, C)] = jnp.transpose(value(p, i).astype(BF16))
+
+    mix(4, 9, 3)
+    for g, (lo, hi) in enumerate(GROUPS2):
+        results(lo, hi, lambda p, i: ext2[g][p, i])
+    for g, (lo, hi) in enumerate(GROUPS):
+        if g > 0:
+            results(lo, hi, lambda p, i: ext[g][p, i].astype(F32) + gate[p] * acc[lo + i, p])
+    write = pltpu.make_async_copy(mix_out, mixed, out_sem)
+    write.start()
+
     for copy in force_copies:
         copy.wait_recv()
     for p in range(NP):

time: 52.9 us -> 52.9 us (level)
  no operation moved by 1% of the time
where the time goes in v11:
time: 52.9 us; the launch traced here: 52.8 us
  Pallas kernels  52.1 us (98%)
  between operations  0.64 us (1%)
    pallas_call x1, Pallas kernels, body(): pl.pallas_call(run_all, out_shape=(jax.ShapeDtypeStruct((NP, 1, S, BLOCKS...  50.3 us
    pallas_call x1, Pallas kernels, body(): pl.pallas_call(deliver, out_shape=(jax.ShapeDtypeStruct((NP, 1, S, BLOCKS...  1.83 us

profile of v11, /device:TPU:2, one launch (start us, length us, event | category | flops | bytes accessed | tf_op | source)
XLA Modules:
  0.0 52.8 jit_solution(7976013830011778841)
XLA Ops:
  0.6 50.3 %shard_map.113 = (bf16[2,1,128,1152]{3,2,1,0:T(8,128)(2,1)}, f32[2,3,1,128]{3,2,1,0:T(1,128)}) custom-call(bf16[2,1,128,1152]{3,2,1,0:T(8,128)(2,1)} %refs_0_.1, f32[2,3,1,128]{3,2,1,0:T(1,128)} %bitcast.2, s32[3,2,1,128]{3,2,1,0:T(1,128)} %refs_2_.1, s32[3,2,1,128]{3,2,1,0:T(1,128)} %refs_3_.1, f32[8,896]{1,0:T(8,128)} %refs_4_.1, f32[8,256]{1,0:T(8,128)} %refs_5_.1, ...), custom_call_target="tpu_custom_call" | custom-call | flops 6000000000 | bytes 2000000 | tf_op jit(solution)/shard_map/pallas_call | solution.py:636
  50.9 1.8 %shard_map.114 = (bf16[2,1,128,1152]{3,2,1,0:T(8,128)(2,1)}, f32[2,3,1,128]{3,2,1,0:T(1,128)}) custom-call(bf16[2,1,128,1152]{3,2,1,0:T(8,128)(2,1)} %get-tuple-element.6.mixed, f32[2,3,1,128]{3,2,1,0:T(1,128)} %get-tuple-element.7.forces), custom_call_target="tpu_custom_call" | custom-call | bytes 1200000 | tf_op jit(solution)/shard_map/pallas_call | solution.py:694

commit v12 on v11

--- a/solution.py
+++ b/solution.py
@@ -324,11 +324,12 @@
                     gsc[to + i, NP * y + p] = out[i * C : (i + 1) * C, y * ROWS : (y + 1) * ROWS]
 
     def each_row(fn, lo, hi):
-        steps = C // STEP
+        steps = C // (2 * STEP)
 
         def run(i, carry):
             q = i // steps
-            fn(q, pl.ds(pl.multiple_of((i - q * steps) * STEP, STEP), STEP))
+            for j in range(2):
+                fn(q, pl.ds(pl.multiple_of((i - q * steps) * (2 * STEP) + j * STEP, STEP), STEP))
             return carry
 
         lax.fori_loop(lo * steps, hi * steps, run, 0)
@@ -511,29 +512,24 @@
     sums[...] = jnp.zeros_like(sums)
 
     def pairs(q, lo, first):
-        def pair(i, carry):
-            r = pl.ds(pl.multiple_of(i * STEP, STEP), STEP)
-            carry = list(carry)
+        totals = [None if first else sums[i % 4, NE * q + i // 4] for i in range(4 * NE)]
+
+        def add(i, term):
+            totals[i] = fold(term) if totals[i] is None else totals[i] + fold(term)
+
+        for start in range(0, C, STEP):
+            r = pl.ds(start, STEP)
             for k in range(NE):
                 e = columns(k)
                 far = [gsc[lo + b, q, r, e] for b in range(READ_BLOCKS)]
                 u = [angle(m, q, k) for m in range(3)]
                 along = u[0] * far[1] + u[1] * far[2] + u[2] * far[3]
-                term = side[q, 0, r, e] * far[0] + side[q, 1, r, e] * along
-                carry[4 * k] = carry[4 * k] + fold(term)
+                add(4 * k, side[q, 0, r, e] * far[0] + side[q, 1, r, e] * along)
                 own_q = side[q, 2, r, e]
                 for m in range(3):
-                    term = side[q, 3 + m, r, e] * along + own_q * far[1 + m]
-                    carry[4 * k + 1 + m] = carry[4 * k + 1 + m] + fold(term)
-            return tuple(carry)
-
-        zero = jnp.zeros((8, S), F32)
-        totals = lax.fori_loop(0, C // STEP, pair, (zero,) * (4 * NE))
-        for k in range(NE):
-            for i in range(4):
-                row = jnp.sum(totals[4 * k + i], axis=0, keepdims=True)
-                at = pl.ds(NE * q + k, 1)
-                sums[i, at, :] = row if first else sums[i, at, :] + row
+                    add(4 * k + 1 + m, side[q, 3 + m, r, e] * along + own_q * far[1 + m])
+        for i in range(4 * NE):
+            sums[i % 4, NE * q + i // 4] = totals[i]
 
     def each_pairs(lo, first, pillars):
         def run(q, carry):
@@ -555,7 +551,7 @@
         gather(ext2, g, READ_BLOCKS + lo, 2, 3)
     each_pairs(READ_BLOCKS, False, (0, COUNT))
 
-    t_rho, g_x, g_y, g_z = (sums[i] for i in range(4))
+    t_rho, g_x, g_y, g_z = (jnp.sum(sums[i], axis=1) for i in range(4))
     u_x, u_y, u_z, inverse = ang[0], ang[1], ang[2], inverses[...]
     radial_part = t_rho - (u_x * g_x + u_y * g_y + u_z * g_z) * inverse
     grad[...] = jnp.zeros_like(grad)
@@ -664,7 +660,7 @@
                 pltpu.VMEM((NP, 1, S, BLOCKS * C), BF16),
                 pltpu.VMEM((NP, 1, S, BLOCKS * C), BF16),
                 pltpu.VMEM((COUNT, 6, C, ROWS), F32),
-                pltpu.VMEM((4, EDGE_ROWS, S), F32),
+                pltpu.VMEM((4, EDGE_ROWS, 8, S), F32),
                 pltpu.VMEM((8, EDGE_ROWS, S), F32),
                 pltpu.VMEM((2, NP, 8, S), F32),
                 pltpu.VMEM((2, NP, 8, S), F32),

time: 52.9 us -> 51.8 us (0.979)
  Pallas kernels: 52.1 us -> 51 us
    pallas_call x1, Pallas kernels: 50.3 us -> 49.2 us  [body(): pl.pallas_call(run_all, out_shape=(jax.ShapeDtypeStruct((NP, 1, S, BLOCKS...]
where the time goes in v12:
time: 51.8 us; the launch traced here: 51.7 us
  Pallas kernels  51 us (98%)
  between operations  0.64 us (1%)
    pallas_call x1, Pallas kernels, body(): pl.pallas_call(run_all, out_shape=(jax.ShapeDtypeStruct((NP, 1, S, BLOCKS...  49.2 us
    pallas_call x1, Pallas kernels, body(): pl.pallas_call(deliver, out_shape=(jax.ShapeDtypeStruct((NP, 1, S, BLOCKS...  1.83 us

profile of v12, /device:TPU:2, one launch (start us, length us, event | category | flops | bytes accessed | tf_op | source)
XLA Modules:
  0.0 51.7 jit_solution(15360034978216103961)
XLA Ops:
  0.6 49.2 %shard_map.113 = (bf16[2,1,128,1152]{3,2,1,0:T(8,128)(2,1)}, f32[2,3,1,128]{3,2,1,0:T(1,128)}) custom-call(bf16[2,1,128,1152]{3,2,1,0:T(8,128)(2,1)} %refs_0_.1, f32[2,3,1,128]{3,2,1,0:T(1,128)} %bitcast.2, s32[3,2,1,128]{3,2,1,0:T(1,128)} %refs_2_.1, s32[3,2,1,128]{3,2,1,0:T(1,128)} %refs_3_.1, f32[8,896]{1,0:T(8,128)} %refs_4_.1, f32[8,256]{1,0:T(8,128)} %refs_5_.1, ...), custom_call_target="tpu_custom_call" | custom-call | flops 6000000000 | bytes 2000000 | tf_op jit(solution)/shard_map/pallas_call | solution.py:632
  49.8 1.8 %shard_map.114 = (bf16[2,1,128,1152]{3,2,1,0:T(8,128)(2,1)}, f32[2,3,1,128]{3,2,1,0:T(1,128)}) custom-call(bf16[2,1,128,1152]{3,2,1,0:T(8,128)(2,1)} %get-tuple-element.6.mixed, f32[2,3,1,128]{3,2,1,0:T(1,128)} %get-tuple-element.7.forces), custom_call_target="tpu_custom_call" | custom-call | bytes 1200000 | tf_op jit(solution)/shard_map/pallas_call | solution.py:690

commit v13 on v12

--- a/solution.py
+++ b/solution.py
@@ -324,15 +324,12 @@
                     gsc[to + i, NP * y + p] = out[i * C : (i + 1) * C, y * ROWS : (y + 1) * ROWS]
 
     def each_row(fn, lo, hi):
-        steps = C // (2 * STEP)
-
-        def run(i, carry):
-            q = i // steps
-            for j in range(2):
-                fn(q, pl.ds(pl.multiple_of((i - q * steps) * (2 * STEP) + j * STEP, STEP), STEP))
+        def run(q, carry):
+            for start in range(0, C, STEP):
+                fn(q, pl.ds(start, STEP))
             return carry
 
-        lax.fori_loop(lo * steps, hi * steps, run, 0)
+        lax.fori_loop(lo, hi, run, 0)
 
     def angle(f, q, k):
         return ang[f, pl.ds(NE * q + k, 1), :]
@@ -391,7 +388,8 @@
                 acc[b, p] = out[:, (b - lo) * S : (b - lo + 1) * S]
             return carry
 
-        lax.fori_loop(0, NP, run, 0)
+        for p in range(NP):
+            run(p, 0)
 
     part_copies = []
     for h in range(len(SUMS)):
@@ -457,7 +455,8 @@
         gate[p] = jax.nn.sigmoid(out[C : 2 * C])
         return carry
 
-    lax.fori_loop(0, NP, scalars, 0)
+    for p in range(NP):
+        scalars(p, 0)
 
     def read_block(b, y, slot):
         g = b // 2

time: 51.8 us -> 51.4 us (level)
  no operation moved by 1% of the time
where the time goes in v13:
time: 51.4 us; the launch traced here: 51.2 us
  Pallas kernels  50.6 us (98%)
  between operations  0.64 us (1%)
    pallas_call x1, Pallas kernels, body(): pl.pallas_call(run_all, out_shape=(jax.ShapeDtypeStruct((NP, 1, S, BLOCKS...  48.8 us
    pallas_call x1, Pallas kernels, body(): pl.pallas_call(deliver, out_shape=(jax.ShapeDtypeStruct((NP, 1, S, BLOCKS...  1.83 us

profile of v13, /device:TPU:2, one launch (start us, length us, event | category | flops | bytes accessed | tf_op | source)
XLA Modules:
  0.0 51.2 jit_solution(11177338883219192470)
XLA Ops:
  0.6 48.8 %shard_map.113 = (bf16[2,1,128,1152]{3,2,1,0:T(8,128)(2,1)}, f32[2,3,1,128]{3,2,1,0:T(1,128)}) custom-call(bf16[2,1,128,1152]{3,2,1,0:T(8,128)(2,1)} %refs_0_.1, f32[2,3,1,128]{3,2,1,0:T(1,128)} %bitcast.2, s32[3,2,1,128]{3,2,1,0:T(1,128)} %refs_2_.1, s32[3,2,1,128]{3,2,1,0:T(1,128)} %refs_3_.1, f32[8,896]{1,0:T(8,128)} %refs_4_.1, f32[8,256]{1,0:T(8,128)} %refs_5_.1, ...), custom_call_target="tpu_custom_call" | custom-call | flops 6000000000 | bytes 2000000 | tf_op jit(solution)/shard_map/pallas_call | solution.py:631
  49.4 1.8 %shard_map.114 = (bf16[2,1,128,1152]{3,2,1,0:T(8,128)(2,1)}, f32[2,3,1,128]{3,2,1,0:T(1,128)}) custom-call(bf16[2,1,128,1152]{3,2,1,0:T(8,128)(2,1)} %get-tuple-element.6.mixed, f32[2,3,1,128]{3,2,1,0:T(1,128)} %get-tuple-element.7.forces), custom_call_target="tpu_custom_call" | custom-call | bytes 1200000 | tf_op jit(solution)/shard_map/pallas_call | solution.py:689

commit v14 on v13

--- a/solution.py
+++ b/solution.py
@@ -324,12 +324,13 @@
                     gsc[to + i, NP * y + p] = out[i * C : (i + 1) * C, y * ROWS : (y + 1) * ROWS]
 
     def each_row(fn, lo, hi):
-        def run(q, carry):
-            for start in range(0, C, STEP):
-                fn(q, pl.ds(start, STEP))
+        def run(y, carry):
+            for p in range(NP):
+                for start in range(0, C, STEP):
+                    fn(NP * y + p, pl.ds(start, STEP))
             return carry
 
-        lax.fori_loop(lo, hi, run, 0)
+        lax.fori_loop(lo // NP, hi // NP, run, 0)
 
     def angle(f, q, k):
         return ang[f, pl.ds(NE * q + k, 1), :]
@@ -531,11 +532,12 @@
             sums[i % 4, NE * q + i // 4] = totals[i]
 
     def each_pairs(lo, first, pillars):
-        def run(q, carry):
-            pairs(q, lo, first)
+        def run(y, carry):
+            for p in range(NP):
+                pairs(NP * y + p, lo, first)
             return carry
 
-        lax.fori_loop(*pillars, run, 0)
+        lax.fori_loop(pillars[0] // NP, pillars[1] // NP, run, 0)
 
     each_pairs(0, True, (0, NP))
     for copy in mix_y:

time: 51.4 us -> 51.3 us (level)
  no operation moved by 1% of the time
where the time goes in v14:
time: 51.3 us; the launch traced here: 51.1 us
  Pallas kernels  50.5 us (98%)
  between operations  0.64 us (1%)
    pallas_call x1, Pallas kernels, body(): pl.pallas_call(run_all, out_shape=(jax.ShapeDtypeStruct((NP, 1, S, BLOCKS...  48.7 us
    pallas_call x1, Pallas kernels, body(): pl.pallas_call(deliver, out_shape=(jax.ShapeDtypeStruct((NP, 1, S, BLOCKS...  1.83 us

profile of v14, /device:TPU:2, one launch (start us, length us, event | category | flops | bytes accessed | tf_op | source)
XLA Modules:
  0.0 51.1 jit_solution(3666329948200650960)
XLA Ops:
  0.6 48.7 %shard_map.113 = (bf16[2,1,128,1152]{3,2,1,0:T(8,128)(2,1)}, f32[2,3,1,128]{3,2,1,0:T(1,128)}) custom-call(bf16[2,1,128,1152]{3,2,1,0:T(8,128)(2,1)} %refs_0_.1, f32[2,3,1,128]{3,2,1,0:T(1,128)} %bitcast.2, s32[3,2,1,128]{3,2,1,0:T(1,128)} %refs_2_.1, s32[3,2,1,128]{3,2,1,0:T(1,128)} %refs_3_.1, f32[8,896]{1,0:T(8,128)} %refs_4_.1, f32[8,256]{1,0:T(8,128)} %refs_5_.1, ...), custom_call_target="tpu_custom_call" | custom-call | flops 6000000000 | bytes 2000000 | tf_op jit(solution)/shard_map/pallas_call | solution.py:633
  49.3 1.8 %shard_map.114 = (bf16[2,1,128,1152]{3,2,1,0:T(8,128)(2,1)}, f32[2,3,1,128]{3,2,1,0:T(1,128)}) custom-call(bf16[2,1,128,1152]{3,2,1,0:T(8,128)(2,1)} %get-tuple-element.6.mixed, f32[2,3,1,128]{3,2,1,0:T(1,128)} %get-tuple-element.7.forces), custom_call_target="tpu_custom_call" | custom-call | bytes 1200000 | tf_op jit(solution)/shard_map/pallas_call | solution.py:691
